TPU v7x, 32 devices: a whole 2x2x4 slice. The times are simulated.
32 devices in a mesh: blk: 16 (over z, y, core), rows: 2 (over x).
Axes of the slice: x: 2, y: 2, z: 4, core: 2. Of those that a mesh axis runs over, the one named last changes fastest.
Arguments:
- coeffs: bfloat16 [64, 12288, 384], P('blk', 'rows'), may hold values from -0.09765625 to 0.09765625
- counts: int32 [64], P('blk'), may hold values from 96 to 384, as said below
- kinetic: float32 [64], replicated, may hold values from -4 to 4
- pair_table: int32 [64, 4], P('blk'), may hold values from 0 to 63
- trial_vecs: bfloat16 [64, 384, 128], P('blk', 'rows'), may hold values from -6 to 6
- owner_map: int32 [2], replicated, may hold values from 0 to 1, each once
Outputs:
- product: bfloat16 [64, 384, 128], P('blk', 'rows')
Inputs may be any that keep to these rules, and one draw needn't show every extreme that they name: `counts`: some angular point keeps all 384 eigenvectors.
All inputs are finite; a program needn't handle non-finite values.
Results may differ from a plain program's by a relative error of at most 0.012.
Values may be sent and summed in bfloat16 or wider, within the bound.
No kernel may reach another device: no remote copies, remote signals or barrier semaphores. Data moves between devices by JAX's collectives and lax.ppermute only.
A program may use at most 128 MiB of HBM per device.

v0:
```python
import jax
import jax.numpy as jnp
from jax import lax
from jax.sharding import PartitionSpec as P


def passed_along(block, axis, distance):
    devices = range(lax.axis_size(axis))
    route = [((i - distance) % len(devices), i) for i in devices]
    return lax.ppermute(block, axis, route)


def apply_vectors(scaled, vectors):
    return jnp.einsum("ijkl,jlv->ikv", scaled, vectors, preferred_element_type=jnp.float32)


def per_device(coeffs, counts, kinetic, pair_table, trial_vecs, owner_map):
    ang_dev = coeffs.shape[0]
    kept = coeffs.shape[2]
    blocks = lax.axis_size("rows")
    column = jnp.arange(kept, dtype=jnp.int32)
    keep_mask = (column[None, :] < counts[:, None]).astype(jnp.bfloat16)
    masked = coeffs * keep_mask[:, None, :]
    prev_sets, prev_rows = passed_along((masked, trial_vecs), "blk", 1)
    prev_whole = lax.all_gather(prev_rows, "rows", axis=1, tiled=True)
    table_index = jnp.arange(kinetic.shape[0], dtype=jnp.int32)
    one_hot = (pair_table[:, :, None] == table_index[None, None, :]).astype(jnp.float32)
    kin_scale = jnp.sum(one_hot * kinetic[None, None, :], axis=2)
    partial_value = jnp.einsum(
        "irk,jrl->ijkl", masked, prev_sets, preferred_element_type=jnp.float32
    )
    grouped = partial_value.reshape(ang_dev, ang_dev, blocks, kept // blocks, kept)
    ordered = jnp.take(grouped, owner_map, axis=2).reshape(ang_dev, ang_dev, kept, kept)
    assembled = lax.psum_scatter(
        ordered.astype(jnp.bfloat16), "rows", scatter_dimension=2, tiled=True
    ).astype(jnp.float32)
    scaled = assembled * kin_scale[:, :, None, None]
    result = apply_vectors(scaled, prev_whole)
    return result.astype(jnp.bfloat16)


def solution(mesh):
    in_specs = (P("blk", "rows", None), P("blk"), P(), P("blk", None), P("blk", "rows", None), P())
    out_specs = P("blk", "rows", None)
    return jax.shard_map(
        per_device, mesh=mesh, in_specs=in_specs, out_specs=out_specs, check_vma=False
    )
```

profile of v0, /device:TPU:0, one launch (start us, length us, event | category | flops | bytes accessed | tf_op | source)
XLA Modules:
  0.0 354.0 jit_solution(396696404693337850)
XLA Ops:
  6.5 0.0 reduce-scatter.2.cloned.1.call-start
  6.5 0.7 fusion.15
  7.3 0.0 copy-start.4
  7.3 16.6 %broadcast_multiply_fusion = bf16[4,6144,384]{2,1,0:T(8,128)(2,1)} fusion(bf16[4,6144,384]{2,1,0:T(8,128)(2,1)} %param.6, bf16[4,384]{1,0:T(4,128)(2,1)S(1)} %fusion.15), kind=kLoop, calls=%fused_computation.8 | loop fusion | flops 9437184 | bytes 37751808 | tf_op jit(solution)/shard_map/mul | solution.py:23
  23.9 0.5 collective-permute-start
  24.3 0.0 copy-done.4
  24.3 0.1 broadcast_in_dim.23
  24.4 0.1 broadcast_in_dim.24
  24.5 208.6 %collective-permute-done = bf16[4,6144,384]{2,1,0:T(8,128)(2,1)} collective-permute-done((bf16[4,6144,384]{2,1,0:T(8,128)(2,1)}, bf16[4,6144,384]{2,1,0:T(8,128)(2,1)}, u32[]{:S(2)}, u32[]{:S(2)}) %collective-permute-start) | collective-permute-done | bytes 18874400 | tf_op jit(solution)/shard_map/ppermute | solution.py:10
  233.1 34.6 %fusion = bf16[4,384,4,384]{1,3,2,0:T(8,128)(2,1)S(1)} fusion(bf16[4,6144,384]{2,1,0:T(8,128)(2,1)} %collective-permute-done, bf16[4,6144,384]{2,1,0:T(8,128)(2,1)} %broadcast_multiply_fusion), kind=kOutput, calls=%fused_computation.2 | convolution fusion | flops 28991029248 | bytes 42467328 | tf_op jit(solution)/shard_map/irk,jrl->ijkl/dot_general | solution.py:29
  267.7 0.3 mini-gather-slice.2
  268.0 1.4 mini-gather-slice.3
  269.4 2.4 gather_fusion
  271.8 0.0 copy-start
  271.8 3.5 gather_fusion.1
  275.3 0.0 copy-done
  275.3 2.0 pad_maximum_fusion
  277.3 0.6 copy.10
  277.9 3.7 %fusion.3 = bf16[4,4,384,384]{3,2,1,0:T(8,128)(2,1)} fusion(bf16[4,4,2,192,384]{4,3,2,1,0:T(8,128)(2,1)S(1)} %copy.10, pred[384]{0:T(512)(128)(4,1)S(1)} %broadcast_in_dim.24), kind=kLoop, calls=%fused_computation.7 | loop fusion | flops 2359296 | bytes 9437568 | tf_op jit(solution)/shard_map/convert_element_type | solution.py:35
  281.6 0.0 copy-start.3
  281.6 0.0 copy-start.1
  281.6 0.0 copy-start.2
  281.6 0.0 reduce-scatter.2.cloned.1.call-update
  281.6 0.9 copy-done.3
  282.5 0.0 collective-permute-start.1
  282.5 0.0 copy-done.1
  282.5 0.0 copy-done.2
  282.5 0.2 select_reduce_fusion
  282.7 7.6 %collective-permute-done.1 = bf16[4,192,128]{2,1,0:T(8,128)(2,1)S(1)} collective-permute-done((bf16[4,192,128]{2,1,0:T(8,128)(2,1)S(1)}, bf16[4,192,128]{2,1,0:T(8,128)(2,1)S(1)}, u32[]{:S(2)}, u32[]{:S(2)}) %collective-permute-start.1) | collective-permute-done | bytes 196640 | tf_op jit(solution)/shard_map/ppermute | solution.py:10
  290.3 10.5 %all_gather.3 = bf16[4,384,128]{2,1,0:T(8,128)(2,1)S(1)} all-gather(bf16[4,192,128]{2,1,0:T(8,128)(2,1)S(1)} %collective-permute-done.1), channel_id=1, replica_groups=mesh['blk'=16,'rows'=2] {'rows'}, dimensions={1}, use_global_device_ids=true | all-gather | bytes 589824 | tf_op jit(solution)/shard_map/all_gather | solution.py:25
  300.8 43.2 %reduce-scatter.2.cloned.1.call-done = bf16[4,4,192,384]{3,2,1,0:T(8,128)(2,1)} async-done(((bf16[4,4,384,384]{3,2,1,0:T(8,128)(2,1)}), bf16[4,4,192,384]{3,2,1,0:T(8,128)(2,1)}) %reduce-scatter.2.cloned.1.call-update) | async-done | bytes 2359312 | tf_op jit(solution)/shard_map/reduce_scatter | solution.py:34
  344.0 3.2 fusion.11
  (3 shorter events, 0.0 us)
Async XLA Ops:
  6.5 337.5 %reduce-scatter.2.cloned.1.call-start = ((), (), s32[]{:S(2)}) async-start(), calls=%async_computation.1 | async-start | bytes 7077888 | tf_op jit(solution)/shard_map/reduce_scatter | solution.py:34
  7.3 17.1 %copy-start.4 = (s32[2]{0:T(128)S(1)}, s32[2]{0:T(128)}, u32[]{:S(2)}) copy-start(s32[2]{0:T(128)} %param.11) | copy-start | bytes 28
  23.9 209.2 %collective-permute-start = (bf16[4,6144,384]{2,1,0:T(8,128)(2,1)}, bf16[4,6144,384]{2,1,0:T(8,128)(2,1)}, u32[]{:S(2)}, u32[]{:S(2)}) collective-permute-start(bf16[4,6144,384]{2,1,0:T(8,128)(2,1)} %broadcast_multiply_fusion), channel_id=1, source_target_pairs={{30,0},{0,2},{2,4},{4,6},{6,8},{8,10},{10,12},{12,14},{14,16},{16,... | collective-permute-start | bytes 56623112 | tf_op jit(solution)/shard_map/ppermute | solution.py:10
  271.8 3.5 copy-start
  281.6 0.9 copy-start.3
  281.6 0.9 copy-start.1
  281.6 0.9 copy-start.2
  282.5 7.8 %collective-permute-start.1 = (bf16[4,192,128]{2,1,0:T(8,128)(2,1)S(1)}, bf16[4,192,128]{2,1,0:T(8,128)(2,1)S(1)}, u32[]{:S(2)}, u32[]{:S(2)}) collective-permute-start(bf16[4,192,128]{2,1,0:T(8,128)(2,1)S(1)} %copy-done.3), channel_id=1, source_target_pairs={{30,0},{0,2},{2,4},{4,6},{6,8},{8,10},{10,12},{12,14},{14,16},{16,... | collective-permute-start | bytes 589832 | tf_op jit(solution)/shard_map/ppermute | solution.py:10
Sparse Core Ops, SparseCore 0:
  281.7 62.2 reduce-scatter.1
where the time goes:
time: 354 us
  waiting for transfers between devices  259 us (73%)
  matrix products  37.7 us (11%)
  other arithmetic  23.2 us (7%)
  between operations  13.4 us (4%)
  blocking collectives  10.5 us (3%)
  local copies, waits for them, and re-layouts  9.24 us (3%)
    ppermute x2, waiting for transfers between devices, passed_along(): return lax.ppermute(block, axis, route)  216 us
    reduce_scatter x1, waiting for transfers between devices, per_device(): lax.psum_scatter(ordered.astype(jnp.bfloat16), 'rows', scatter_dimension=...  43.2 us
    dot_general x1, matrix products, per_device(): jnp.einsum('irk,jrl->ijkl', masked, prev_sets, preferred_element_type=jnp...  34.6 us
    mul x1, other arithmetic, per_device(): masked = coeffs * keep_mask[:, None, :]  16.6 us
    all_gather x1, blocking collectives, per_device(): prev_whole = lax.all_gather(prev_rows, 'rows', axis=1, tiled=True)  10.5 us
    gather x4, local copies, waits for them, and re-layouts, per_device(): jnp.take(grouped, owner_map, axis=2).reshape(ang_dev, ang_dev, kept, kept)  7.57 us
  transfers between devices with their start and end apart: 3, of which 3 were waited for; matrix products, arithmetic and copies ran while one was open for 0% of the time, Pallas kernels for 0%

commit v1 on v0

v1 whole, which is shorter than its diff:
```python
import functools

import jax
import jax.numpy as jnp
from jax import lax
from jax.experimental import pallas as pl
from jax.experimental.pallas import tpu as pltpu
from jax.sharding import PartitionSpec as P

VMEM_LIMIT = 48 * 1024 * 1024


def shifted(block, axis, distance):
    devices = range(lax.axis_size(axis))
    route = [(i, (i + distance) % len(devices)) for i in devices]
    return lax.ppermute(block, axis, route)


def block_rows(length):
    for rows in (768, 512, 384, 256, 192, 128, 96, 64, 48, 32, 16):
        if length % rows == 0:
            return rows
    return length


def produce_kernel(kin_ref, sets_ref, vectors_ref, out_ref):
    points = sets_ref.shape[0]
    products = [
        jnp.dot(sets_ref[j], vectors_ref[j], preferred_element_type=jnp.float32)
        for j in range(points)
    ]
    for a in range(out_ref.shape[0]):
        total = kin_ref[a, 0] * products[0]
        for j in range(1, points):
            total += kin_ref[a, j] * products[j]
        out_ref[a] = total.astype(out_ref.dtype)


def produce(sets, vectors, kin, start, length):
    points, _, kept = sets.shape
    width = vectors.shape[2]
    rows = block_rows(length)
    first = start // rows
    return pl.pallas_call(
        produce_kernel,
        grid=(length // rows,),
        in_specs=[
            pl.BlockSpec(memory_space=pltpu.SMEM),
            pl.BlockSpec((points, rows, kept), lambda i: (0, first + i, 0)),
            pl.BlockSpec((points, kept, width), lambda i: (0, 0, 0)),
        ],
        out_specs=pl.BlockSpec((points, rows, width), lambda i: (0, i, 0)),
        out_shape=jax.ShapeDtypeStruct((points, length, width), jnp.bfloat16),
        compiler_params=pltpu.CompilerParams(vmem_limit_bytes=VMEM_LIMIT),
        cost_estimate=pl.CostEstimate(
            flops=2 * points * length * kept * width,
            bytes_accessed=2 * points * length * (kept + width),
            transcendentals=0,
        ),
    )(kin, sets, vectors)


def consume_kernel(sets_ref, arrived_ref, before_ref, out_ref):
    @pl.when(pl.program_id(0) == 0)
    def _():
        out_ref[...] = before_ref[...]

    for a in range(out_ref.shape[0]):
        out_ref[a] += lax.dot_general(
            arrived_ref[a],
            sets_ref[a],
            (((0,), (0,)), ((), ())),
            preferred_element_type=jnp.float32,
        )


def consume(sets, arrived, before, start):
    points, _, kept = sets.shape
    _, length, width = arrived.shape
    rows = block_rows(length)
    first = start // rows
    return pl.pallas_call(
        consume_kernel,
        grid=(length // rows,),
        in_specs=[
            pl.BlockSpec((points, rows, kept), lambda i: (0, first + i, 0)),
            pl.BlockSpec((points, rows, width), lambda i: (0, i, 0)),
            pl.BlockSpec((points, width, kept), lambda i: (0, 0, 0)),
        ],
        out_specs=pl.BlockSpec((points, width, kept), lambda i: (0, 0, 0)),
        out_shape=jax.ShapeDtypeStruct((points, width, kept), jnp.float32),
        compiler_params=pltpu.CompilerParams(vmem_limit_bytes=VMEM_LIMIT),
        cost_estimate=pl.CostEstimate(
            flops=2 * points * length * kept * width,
            bytes_accessed=2 * points * length * (kept + width),
            transcendentals=0,
        ),
    )(sets, arrived, before)


def per_device(coeffs, counts, kinetic, pair_table, trial_vecs, owner_map):
    points, radial, kept = coeffs.shape
    share, width = trial_vecs.shape[1:]
    blocks = lax.axis_size("rows")
    me = lax.axis_index("rows")

    table_index = jnp.arange(kinetic.shape[0], dtype=jnp.int32)
    one_hot = pair_table[:, :, None] == table_index[None, None, :]
    kin_own = jnp.sum(jnp.where(one_hot, kinetic[None, None, :], 0.0), axis=2)
    kin_next = shifted(kin_own, "blk", -1)

    pieces = [trial_vecs] + [shifted(trial_vecs, "rows", d) for d in range(1, blocks)]
    if blocks == 2:
        low = jnp.where(me == 0, pieces[0], pieces[1])
        high = jnp.where(me == 0, pieces[1], pieces[0])
        vectors = jnp.concatenate([low, high], axis=1)
    else:
        stacked = jnp.stack(pieces, axis=1)
        order = (me - jnp.arange(blocks)) % blocks
        vectors = jnp.take(stacked, order, axis=1).reshape(points, kept, width)
    column = jnp.arange(kept, dtype=jnp.int32)
    keep = column[None, :] < counts[:, None]
    vectors = jnp.where(keep[:, :, None], vectors, jnp.zeros((), vectors.dtype))

    step = radial // 8
    bounds = [(0, step), (step, step), (2 * step, 2 * step), (4 * step, 2 * step), (6 * step, step), (7 * step, step)]
    sent = [shifted(produce(coeffs, vectors, kin_next, s, n), "blk", 1) for s, n in bounds]
    total = jnp.zeros((points, width, kept), jnp.float32)
    for (s, n), z in zip(bounds, sent):
        total = consume(coeffs, z, total, s)

    result = jnp.where(keep[:, :, None], total.transpose(0, 2, 1), 0.0)

    def block_of(index):
        return lax.dynamic_slice_in_dim(result, owner_map[index] * share, share, 1)

    final = block_of(me)
    for d in range(1, blocks):
        out = block_of((me + d) % blocks).astype(jnp.bfloat16)
        final += shifted(out, "rows", d).astype(jnp.float32)
    return final.astype(jnp.bfloat16)


def solution(mesh):
    in_specs = (P("blk", "rows", None), P("blk"), P(), P("blk", None), P("blk", "rows", None), P())
    out_specs = P("blk", "rows", None)
    return jax.shard_map(
        per_device, mesh=mesh, in_specs=in_specs, out_specs=out_specs, check_vma=False
    )
```

time: 354 us -> 98 us (0.28)
  waiting for transfers between devices: 259 us -> 39.9 us
  matrix products: 37.7 us -> 0 us
  Pallas kernels: 0 us -> 37.7 us
  other arithmetic: 23.2 us -> 3.07 us
  between operations: 13.4 us -> 1.45 us
  starting transfers between devices: 0.46 us -> 11.7 us
  blocking collectives: 10.5 us -> 0 us
  local copies, waits for them, and re-layouts: 9.24 us -> 3.78 us
    ppermute x2 -> x9, waiting for transfers between devices: 216 us -> 39.9 us  [shifted(): return lax.ppermute(block, axis, route)]
    reduce_scatter x1 -> x0, waiting for transfers between devices: 43.2 us -> none  [per_device(): lax.psum_scatter(ordered.astype(jnp.bfloat16), 'rows', scatter_dimension=...]
    dot_general x2 -> x0, matrix products: 37.7 us -> none  [the longest x1 34.6 us: per_device(): jnp.einsum('irk,jrl->ijkl', masked, prev_sets, preferred_element_type=jnp...]
    pallas_call x0 -> x12, Pallas kernels: none -> 37.7 us  [the longest x6 21.5 us: produce(): pl.pallas_call(produce_kernel, grid=(length // rows,), in_specs=[pl.Block...]
    mul x1 -> x0, other arithmetic: 16.6 us -> none  [per_device(): masked = coeffs * keep_mask[:, None, :]]
    ppermute x2 -> x9, starting transfers between devices: 0.46 us -> 11.7 us  [shifted(): return lax.ppermute(block, axis, route)]
    all_gather x1 -> x0, blocking collectives: 10.5 us -> none  [per_device(): prev_whole = lax.all_gather(prev_rows, 'rows', axis=1, tiled=True)]
    gather x4 -> x0, local copies, waits for them, and re-layouts: 7.57 us -> none  [per_device(): jnp.take(grouped, owner_map, axis=2).reshape(ang_dev, ang_dev, kept, kept)]
  transfers between devices with their start and end apart: 3 -> 9, of which waited for: 3 -> 4; matrix products, arithmetic and copies ran while one was open for 0% -> 4% of each run, Pallas kernels for 0% -> 31%
where the time goes in v1:
time: 98 us; the launch traced here: 97.6 us
  waiting for transfers between devices  39.9 us (41%)
  Pallas kernels  37.7 us (38%)
  starting transfers between devices  11.7 us (12%)
  local copies, waits for them, and re-layouts  3.78 us (4%)
  other arithmetic  3.07 us (3%)
  between operations  1.45 us (1%)
    ppermute x9, waiting for transfers between devices, shifted(): return lax.ppermute(block, axis, route)  39.9 us
    pallas_call x6, Pallas kernels, produce(): pl.pallas_call(produce_kernel, grid=(length // rows,), in_specs=[pl.Block...  21.5 us
    pallas_call x6, Pallas kernels, consume(): pl.pallas_call(consume_kernel, grid=(length // rows,), in_specs=[pl.Block...  16.2 us
    ppermute x9, starting transfers between devices, shifted(): return lax.ppermute(block, axis, route)  11.7 us
    unnamed x6, local copies, waits for them, and re-layouts  2.11 us
  transfers between devices with their start and end apart: 9, of which 4 were waited for; matrix products, arithmetic and copies ran while one was open for 4% of the time, Pallas kernels for 31%

profile of v1, /device:TPU:0, one launch (start us, length us, event | category | flops | bytes accessed | tf_op | source)
XLA Modules:
  0.0 97.6 jit_solution(2733313097165138875)
XLA Ops:
  0.0 2.9 %collective-permute-start.1 = (bf16[4,192,128]{2,1,0:T(8,128)(2,1)}, bf16[4,192,128]{2,1,0:T(8,128)(2,1)S(1)}, u32[]{:S(2)}, u32[]{:S(2)}) collective-permute-start(bf16[4,192,128]{2,1,0:T(8,128)(2,1)} %param.10), channel_id=1, source_target_pairs={{0,1},{1,0},{2,3},{3,2},{4,5},{5,4},{6,7},{7,6},{8,9},{9,8},{10,11... | collective-permute-start | bytes 589832 | tf_op jit(solution)/shard_map/ppermute | solution.py:16
  2.9 0.9 select_reduce_fusion
  3.8 3.7 %collective-permute-start = (f32[4,4]{1,0:T(4,128)S(1)}, f32[4,4]{1,0:T(4,128)S(1)}, u32[]{:S(2)}, u32[]{:S(2)}) collective-permute-start(f32[4,4]{1,0:T(4,128)S(1)} %select_reduce_fusion), channel_id=1, source_target_pairs={{0,30},{2,0},{4,2},{6,4},{8,6},{10,8},{12,10},{14,12},{16,14},{18,... | collective-permute-start | bytes 200 | tf_op jit(solution)/shard_map/ppermute | solution.py:16
  7.5 0.7 iota_compare_fusion.1
  8.2 0.0 collective-permute-done.1
  8.2 1.0 broadcast_select_fusion.2
  9.2 0.3 maximum_select_fusion.vectors_ref
  9.5 0.0 collective-permute-done.kin_ref
  9.5 4.5 %shard_map.67 = bf16[4,1536,128]{2,1,0:T(8,128)(2,1)} custom-call(f32[4,4]{1,0:T(4,128)S(1)} %collective-permute-done.kin_ref, bf16[4,6144,384]{2,1,0:T(8,128)(2,1)} %sets_ref.23, bf16[4,384,128]{2,1,0:T(8,128)(2,1)S(1)} %maximum_select_fusion.vectors_ref), custom_call_target="tpu_custom_call" | custom-call | flops 603979776 | bytes 6291456 | tf_op jit(solution)/shard_map/pallas_call | solution.py:44
  14.0 0.0 collective-permute-start.5
  14.0 3.7 %shard_map.66 = bf16[4,1536,128]{2,1,0:T(8,128)(2,1)S(1)} custom-call(f32[4,4]{1,0:T(4,128)S(1)} %collective-permute-done.kin_ref, bf16[4,6144,384]{2,1,0:T(8,128)(2,1)} %sets_ref.23, bf16[4,384,128]{2,1,0:T(8,128)(2,1)S(1)} %maximum_select_fusion.vectors_ref), custom_call_target="tpu_custom_call" | custom-call | flops 603979776 | bytes 6291456 | tf_op jit(solution)/shard_map/pallas_call | solution.py:44
  17.8 1.7 %collective-permute-start.4 = (bf16[4,1536,128]{2,1,0:T(8,128)(2,1)S(1)}, bf16[4,1536,128]{2,1,0:T(8,128)(2,1)S(1)}, u32[]{:S(2)}, u32[]{:S(2)}) collective-permute-start(bf16[4,1536,128]{2,1,0:T(8,128)(2,1)S(1)} %shard_map.66), channel_id=1, source_target_pairs={{0,2},{2,4},{4,6},{6,8},{8,10},{10,12},{12,14},{14,16},{16,18},{18... | collective-permute-start | bytes 4718600 | tf_op jit(solution)/shard_map/ppermute | solution.py:16
  19.5 2.6 %shard_map.69 = bf16[4,768,128]{2,1,0:T(8,128)(2,1)S(1)} custom-call(f32[4,4]{1,0:T(4,128)S(1)} %collective-permute-done.kin_ref, bf16[4,6144,384]{2,1,0:T(8,128)(2,1)} %sets_ref.23, bf16[4,384,128]{2,1,0:T(8,128)(2,1)S(1)} %maximum_select_fusion.vectors_ref), custom_call_target="tpu_custom_call" | custom-call | flops 301989888 | bytes 3145728 | tf_op jit(solution)/shard_map/pallas_call | solution.py:44
  22.2 0.1 collective-permute-start.7
  22.2 3.6 %shard_map.68 = bf16[4,768,128]{2,1,0:T(8,128)(2,1)} custom-call(f32[4,4]{1,0:T(4,128)S(1)} %collective-permute-done.kin_ref, bf16[4,6144,384]{2,1,0:T(8,128)(2,1)} %sets_ref.23, bf16[4,384,128]{2,1,0:T(8,128)(2,1)S(1)} %maximum_select_fusion.vectors_ref), custom_call_target="tpu_custom_call" | custom-call | flops 301989888 | bytes 3145728 | tf_op jit(solution)/shard_map/pallas_call | solution.py:44
  25.8 1.6 %collective-permute-start.6 = (bf16[4,768,128]{2,1,0:T(8,128)(2,1)}, bf16[4,768,128]{2,1,0:T(8,128)(2,1)}, u32[]{:S(2)}, u32[]{:S(2)}) collective-permute-start(bf16[4,768,128]{2,1,0:T(8,128)(2,1)} %shard_map.68), channel_id=1, source_target_pairs={{0,2},{2,4},{4,6},{6,8},{8,10},{10,12},{12,14},{14,16},{16,18},{18... | collective-permute-start | bytes 2359304 | tf_op jit(solution)/shard_map/ppermute | solution.py:16
  27.4 3.5 %shard_map.65 = bf16[4,768,128]{2,1,0:T(8,128)(2,1)} custom-call(f32[4,4]{1,0:T(4,128)S(1)} %collective-permute-done.kin_ref, bf16[4,6144,384]{2,1,0:T(8,128)(2,1)} %sets_ref.23, bf16[4,384,128]{2,1,0:T(8,128)(2,1)S(1)} %maximum_select_fusion.vectors_ref), custom_call_target="tpu_custom_call" | custom-call | flops 301989888 | bytes 3145728 | tf_op jit(solution)/shard_map/pallas_call | solution.py:44
  30.9 0.0 copy-start.2
  30.9 0.0 collective-permute-start.3
  30.9 3.5 %shard_map.64 = bf16[4,768,128]{2,1,0:T(8,128)(2,1)} custom-call(f32[4,4]{1,0:T(4,128)S(1)} %collective-permute-done.kin_ref, bf16[4,6144,384]{2,1,0:T(8,128)(2,1)} %sets_ref.23, bf16[4,384,128]{2,1,0:T(8,128)(2,1)S(1)} %maximum_select_fusion.vectors_ref), custom_call_target="tpu_custom_call" | custom-call | flops 301989888 | bytes 3145728 | tf_op jit(solution)/shard_map/pallas_call | solution.py:44
  34.5 27.6 %collective-permute-done.7.arrived_ref = bf16[4,768,128]{2,1,0:T(8,128)(2,1)S(1)} collective-permute-done((bf16[4,768,128]{2,1,0:T(8,128)(2,1)S(1)}, bf16[4,768,128]{2,1,0:T(8,128)(2,1)S(1)}, u32[]{:S(2)}, u32[]{:S(2)}) %collective-permute-start.7) | collective-permute-done | bytes 786464 | tf_op jit(solution)/shard_map/ppermute | solution.py:16
  62.1 0.0 copy-start
  62.1 1.0 %copy-done = bf16[4,768,128]{2,1,0:T(8,128)(2,1)} copy-done((bf16[4,768,128]{2,1,0:T(8,128)(2,1)}, bf16[4,768,128]{2,1,0:T(8,128)(2,1)S(1)}, u32[]{:S(2)}) %copy-start) | copy-done | bytes 786456
  63.0 0.0 collective-permute-start.2
  63.0 0.0 copy-done.2
  63.0 0.7 fusion.2
  64.3 0.1 broadcast_in_dim.49.before_ref
  64.4 0.0 copy-start.1
  64.4 1.1 %copy-done.1 = bf16[4,768,128]{2,1,0:T(8,128)(2,1)S(1)} copy-done((bf16[4,768,128]{2,1,0:T(8,128)(2,1)S(1)}, bf16[4,768,128]{2,1,0:T(8,128)(2,1)}, u32[]{:S(2)}) %copy-start.1) | copy-done | bytes 786456
  65.5 2.3 %shard_map.70.before_ref = f32[4,128,384]{2,1,0:T(8,128)S(1)} custom-call(bf16[4,6144,384]{2,1,0:T(8,128)(2,1)} %sets_ref.23, bf16[4,768,128]{2,1,0:T(8,128)(2,1)S(1)} %copy-done.1, f32[4,128,384]{2,1,0:T(8,128)S(1)} %broadcast_in_dim.49.before_ref), custom_call_target="tpu_custom_call" | custom-call | flops 301989888 | bytes 3145728 | tf_op jit(solution)/shard_map/pallas_call | solution.py:82
  67.8 2.8 %collective-permute-done.6.arrived_ref = bf16[4,768,128]{2,1,0:T(8,128)(2,1)} collective-permute-done((bf16[4,768,128]{2,1,0:T(8,128)(2,1)}, bf16[4,768,128]{2,1,0:T(8,128)(2,1)}, u32[]{:S(2)}, u32[]{:S(2)}) %collective-permute-start.6) | collective-permute-done | bytes 786464 | tf_op jit(solution)/shard_map/ppermute | solution.py:16
  70.6 2.5 %shard_map.71.before_ref = f32[4,128,384]{2,1,0:T(8,128)S(1)} custom-call(bf16[4,6144,384]{2,1,0:T(8,128)(2,1)} %sets_ref.23, bf16[4,768,128]{2,1,0:T(8,128)(2,1)} %collective-permute-done.6.arrived_ref, f32[4,128,384]{2,1,0:T(8,128)S(1)} %shard_map.70.before_ref), custom_call_target="tpu_custom_call" | custom-call | flops 301989888 | bytes 3145728 | tf_op jit(solution)/shard_map/pallas_call | solution.py:82
  73.1 0.0 collective-permute-done.5.arrived_ref
  73.1 3.4 %shard_map.72.before_ref = f32[4,128,384]{2,1,0:T(8,128)S(1)} custom-call(bf16[4,6144,384]{2,1,0:T(8,128)(2,1)} %sets_ref.23, bf16[4,1536,128]{2,1,0:T(8,128)(2,1)} %collective-permute-done.5.arrived_ref, f32[4,128,384]{2,1,0:T(8,128)S(1)} %shard_map.71.before_ref), custom_call_target="tpu_custom_call" | custom-call | flops 603979776 | bytes 6291456 | tf_op jit(solution)/shard_map/pallas_call | solution.py:82
  76.5 0.0 collective-permute-done.4.arrived_ref
  76.5 3.1 %shard_map.73.before_ref = f32[4,128,384]{2,1,0:T(8,128)S(1)} custom-call(bf16[4,6144,384]{2,1,0:T(8,128)(2,1)} %sets_ref.23, bf16[4,1536,128]{2,1,0:T(8,128)(2,1)S(1)} %collective-permute-done.4.arrived_ref, f32[4,128,384]{2,1,0:T(8,128)S(1)} %shard_map.72.before_ref), custom_call_target="tpu_custom_call" | custom-call | flops 603979776 | bytes 6291456 | tf_op jit(solution)/shard_map/pallas_call | solution.py:82
  79.6 0.0 collective-permute-done.3.arrived_ref
  79.6 2.5 %shard_map.74.before_ref = f32[4,128,384]{2,1,0:T(8,128)S(1)} custom-call(bf16[4,6144,384]{2,1,0:T(8,128)(2,1)} %sets_ref.23, bf16[4,768,128]{2,1,0:T(8,128)(2,1)} %collective-permute-done.3.arrived_ref, f32[4,128,384]{2,1,0:T(8,128)S(1)} %shard_map.73.before_ref), custom_call_target="tpu_custom_call" | custom-call | flops 301989888 | bytes 3145728 | tf_op jit(solution)/shard_map/pallas_call | solution.py:82
  82.1 5.4 %collective-permute-done.2.arrived_ref = bf16[4,768,128]{2,1,0:T(8,128)(2,1)} collective-permute-done((bf16[4,768,128]{2,1,0:T(8,128)(2,1)}, bf16[4,768,128]{2,1,0:T(8,128)(2,1)}, u32[]{:S(2)}, u32[]{:S(2)}) %collective-permute-start.2) | collective-permute-done | bytes 786464 | tf_op jit(solution)/shard_map/ppermute | solution.py:16
  87.4 2.5 %shard_map.75 = f32[4,128,384]{2,1,0:T(8,128)S(1)} custom-call(bf16[4,6144,384]{2,1,0:T(8,128)(2,1)} %sets_ref.23, bf16[4,768,128]{2,1,0:T(8,128)(2,1)} %collective-permute-done.2.arrived_ref, f32[4,128,384]{2,1,0:T(8,128)S(1)} %shard_map.74.before_ref), custom_call_target="tpu_custom_call" | custom-call | flops 301989888 | bytes 3145728 | tf_op jit(solution)/shard_map/pallas_call | solution.py:82
  89.9 0.1 broadcast_select_fusion
  90.0 0.1 fusion.1
  90.1 1.6 %collective-permute-start.8 = (bf16[4,192,128]{1,2,0:T(8,128)(2,1)S(1)}, bf16[4,192,128]{1,2,0:T(8,128)(2,1)S(1)}, u32[]{:S(2)}, u32[]{:S(2)}) collective-permute-start(bf16[4,192,128]{1,2,0:T(8,128)(2,1)S(1)} %fusion.1), channel_id=1, source_target_pairs={{0,1},{1,0},{2,3},{3,2},{4,5},{5,4},{6,7},{7,6},{8,9},{9,8},{10,11... | collective-permute-start | bytes 589832 | tf_op jit(solution)/shard_map/ppermute | solution.py:16
  92.4 4.2 %collective-permute-done.8 = bf16[4,192,128]{1,2,0:T(8,128)(2,1)S(1)} collective-permute-done((bf16[4,192,128]{1,2,0:T(8,128)(2,1)S(1)}, bf16[4,192,128]{1,2,0:T(8,128)(2,1)S(1)}, u32[]{:S(2)}, u32[]{:S(2)}) %collective-permute-start.8) | collective-permute-done | bytes 196640 | tf_op jit(solution)/shard_map/ppermute | solution.py:16
  96.6 0.2 fusion
  96.8 0.8 copy.8
Async XLA Ops:
  0.0 8.2 %collective-permute-start.1 = (bf16[4,192,128]{2,1,0:T(8,128)(2,1)}, bf16[4,192,128]{2,1,0:T(8,128)(2,1)S(1)}, u32[]{:S(2)}, u32[]{:S(2)}) collective-permute-start(bf16[4,192,128]{2,1,0:T(8,128)(2,1)} %param.10), channel_id=1, source_target_pairs={{0,1},{1,0},{2,3},{3,2},{4,5},{5,4},{6,7},{7,6},{8,9},{9,8},{10,11... | collective-permute-start | bytes 589832 | tf_op jit(solution)/shard_map/ppermute | solution.py:16
  3.8 5.7 %collective-permute-start = (f32[4,4]{1,0:T(4,128)S(1)}, f32[4,4]{1,0:T(4,128)S(1)}, u32[]{:S(2)}, u32[]{:S(2)}) collective-permute-start(f32[4,4]{1,0:T(4,128)S(1)} %select_reduce_fusion), channel_id=1, source_target_pairs={{0,30},{2,0},{4,2},{6,4},{8,6},{10,8},{12,10},{14,12},{16,14},{18,... | collective-permute-start | bytes 200 | tf_op jit(solution)/shard_map/ppermute | solution.py:16
  14.0 59.0 %collective-permute-start.5 = (bf16[4,1536,128]{2,1,0:T(8,128)(2,1)}, bf16[4,1536,128]{2,1,0:T(8,128)(2,1)}, u32[]{:S(2)}, u32[]{:S(2)}) collective-permute-start(bf16[4,1536,128]{2,1,0:T(8,128)(2,1)} %shard_map.67), channel_id=1, source_target_pairs={{0,2},{2,4},{4,6},{6,8},{8,10},{10,12},{12,14},{14,16},{16,18},{18... | collective-permute-start | bytes 4718600 | tf_op jit(solution)/shard_map/ppermute | solution.py:16
  17.8 58.7 %collective-permute-start.4 = (bf16[4,1536,128]{2,1,0:T(8,128)(2,1)S(1)}, bf16[4,1536,128]{2,1,0:T(8,128)(2,1)S(1)}, u32[]{:S(2)}, u32[]{:S(2)}) collective-permute-start(bf16[4,1536,128]{2,1,0:T(8,128)(2,1)S(1)} %shard_map.66), channel_id=1, source_target_pairs={{0,2},{2,4},{4,6},{6,8},{8,10},{10,12},{12,14},{14,16},{16,18},{18... | collective-permute-start | bytes 4718600 | tf_op jit(solution)/shard_map/ppermute | solution.py:16
  22.2 39.9 %collective-permute-start.7 = (bf16[4,768,128]{2,1,0:T(8,128)(2,1)S(1)}, bf16[4,768,128]{2,1,0:T(8,128)(2,1)S(1)}, u32[]{:S(2)}, u32[]{:S(2)}) collective-permute-start(bf16[4,768,128]{2,1,0:T(8,128)(2,1)S(1)} %shard_map.69), channel_id=1, source_target_pairs={{0,2},{2,4},{4,6},{6,8},{8,10},{10,12},{12,14},{14,16},{16,18},{18... | collective-permute-start | bytes 2359304 | tf_op jit(solution)/shard_map/ppermute | solution.py:16
  25.8 44.8 %collective-permute-start.6 = (bf16[4,768,128]{2,1,0:T(8,128)(2,1)}, bf16[4,768,128]{2,1,0:T(8,128)(2,1)}, u32[]{:S(2)}, u32[]{:S(2)}) collective-permute-start(bf16[4,768,128]{2,1,0:T(8,128)(2,1)} %shard_map.68), channel_id=1, source_target_pairs={{0,2},{2,4},{4,6},{6,8},{8,10},{10,12},{12,14},{14,16},{16,18},{18... | collective-permute-start | bytes 2359304 | tf_op jit(solution)/shard_map/ppermute | solution.py:16
  30.9 32.1 %copy-start.2 = (s32[2]{0:T(128)S(1)}, s32[2]{0:T(128)}, u32[]{:S(2)}) copy-start(s32[2]{0:T(128)} %param.11) | copy-start | bytes 28
  30.9 48.7 %collective-permute-start.3 = (bf16[4,768,128]{2,1,0:T(8,128)(2,1)}, bf16[4,768,128]{2,1,0:T(8,128)(2,1)}, u32[]{:S(2)}, u32[]{:S(2)}) collective-permute-start(bf16[4,768,128]{2,1,0:T(8,128)(2,1)} %shard_map.65), channel_id=1, source_target_pairs={{0,2},{2,4},{4,6},{6,8},{8,10},{10,12},{12,14},{14,16},{16,18},{18... | collective-permute-start | bytes 2359304 | tf_op jit(solution)/shard_map/ppermute | solution.py:16
  62.1 1.0 %copy-start = (bf16[4,768,128]{2,1,0:T(8,128)(2,1)}, bf16[4,768,128]{2,1,0:T(8,128)(2,1)S(1)}, u32[]{:S(2)}) copy-start(bf16[4,768,128]{2,1,0:T(8,128)(2,1)S(1)} %collective-permute-done.7.arrived_ref) | copy-start | bytes 2359300
  63.0 24.4 %collective-permute-start.2 = (bf16[4,768,128]{2,1,0:T(8,128)(2,1)}, bf16[4,768,128]{2,1,0:T(8,128)(2,1)}, u32[]{:S(2)}, u32[]{:S(2)}) collective-permute-start(bf16[4,768,128]{2,1,0:T(8,128)(2,1)} %shard_map.64), channel_id=1, source_target_pairs={{0,2},{2,4},{4,6},{6,8},{8,10},{10,12},{12,14},{14,16},{16,18},{18... | collective-permute-start | bytes 2359304 | tf_op jit(solution)/shard_map/ppermute | solution.py:16
  64.4 1.1 %copy-start.1 = (bf16[4,768,128]{2,1,0:T(8,128)(2,1)S(1)}, bf16[4,768,128]{2,1,0:T(8,128)(2,1)}, u32[]{:S(2)}) copy-start(bf16[4,768,128]{2,1,0:T(8,128)(2,1)} %copy-done) | copy-start | bytes 2359300
  90.1 6.4 %collective-permute-start.8 = (bf16[4,192,128]{1,2,0:T(8,128)(2,1)S(1)}, bf16[4,192,128]{1,2,0:T(8,128)(2,1)S(1)}, u32[]{:S(2)}, u32[]{:S(2)}) collective-permute-start(bf16[4,192,128]{1,2,0:T(8,128)(2,1)S(1)} %fusion.1), channel_id=1, source_target_pairs={{0,1},{1,0},{2,3},{3,2},{4,5},{5,4},{6,7},{7,6},{8,9},{9,8},{10,11... | collective-permute-start | bytes 589832 | tf_op jit(solution)/shard_map/ppermute | solution.py:16

commit v2 on v0

v2 whole, which is shorter than its diff:
```python
import functools

import jax
import jax.numpy as jnp
from jax import lax
from jax.experimental import pallas as pl
from jax.experimental.pallas import tpu as pltpu
from jax.sharding import PartitionSpec as P

VMEM_LIMIT = 50 * 1024 * 1024
SMEM = pl.BlockSpec(memory_space=pltpu.SMEM)
VMEM = pl.BlockSpec(memory_space=pltpu.VMEM)
ORDER = pl.BlockSpec(memory_space=pl.ANY)
CHEAP = pl.CostEstimate(flops=1, bytes_accessed=1, transcendentals=0)


def shifted(block, axis, distance):
    devices = range(lax.axis_size(axis))
    route = [(i, (i + distance) % len(devices)) for i in devices]
    return lax.ppermute(block, axis, route)


def after(value, *others):
    return lax.optimization_barrier((value, *others))[0]


def params():
    return pltpu.CompilerParams(vmem_limit_bytes=VMEM_LIMIT)


def contract_rows(left, right):
    return lax.dot_general(
        left, right, (((0,), (0,)), ((), ())), preferred_element_type=jnp.float32
    )


def fill(vectors, pieces, count, me):
    share = pieces[0].shape[0]
    blocks = len(pieces)
    for d, piece in enumerate(pieces):
        start = pl.multiple_of(lax.rem(me + (blocks - d), blocks) * share, 16)
        row = start + lax.broadcasted_iota(jnp.int32, piece.shape, 0)
        kept = jnp.where(row < count, piece.astype(jnp.float32), 0.0)
        vectors[pl.ds(start, share), :] = kept.astype(vectors.dtype)


def apply_kernel(first, _, counts_ref, me_ref, sets_ref, own_ref, *rest):
    *others, out_ref, vectors = rest
    i = pl.program_id(0)
    fill(vectors, [r[0] for r in (own_ref, *others)], counts_ref[first + i], me_ref[0])
    out_ref[0] = jnp.dot(
        sets_ref[0], vectors[...], preferred_element_type=jnp.float32
    ).astype(out_ref.dtype)


def apply_first(sets, own, others, counts, me, start, rows):
    kept = sets.shape[2]
    share, width = own.shape[1:]
    block = rows // 2
    skip = start // block

    def kernel(counts_ref, me_ref, sets_ref, own_ref, *rest):
        *pieces, out_ref, vectors = rest

        @pl.when(pl.program_id(0) == 0)
        def _():
            fill(vectors, [r[0] for r in (own_ref, *pieces)], counts_ref[0], me_ref[0])

        out_ref[0] = jnp.dot(
            sets_ref[0], vectors[...], preferred_element_type=jnp.float32
        ).astype(out_ref.dtype)

    return pl.pallas_call(
        kernel,
        grid=(2,),
        in_specs=[SMEM, SMEM, pl.BlockSpec((1, block, kept), lambda i: (0, skip + i, 0))]
        + [pl.BlockSpec((1, share, width), lambda i: (0, 0, 0))] * (1 + len(others)),
        out_specs=pl.BlockSpec((1, block, width), lambda i: (0, i, 0)),
        out_shape=jax.ShapeDtypeStruct((1, rows, width), jnp.bfloat16),
        scratch_shapes=[pltpu.VMEM((kept, width), jnp.bfloat16)],
        compiler_params=params(),
        cost_estimate=CHEAP,
        name="apply_first",
    )(counts, me, sets, own, *others)


def apply_rest(sets, own, others, earlier, counts, me, start, rows):
    points, _, kept = sets.shape
    share, width = own.shape[1:]
    own_spec = pl.BlockSpec((1, share, width), lambda i: (i + 1, 0, 0))
    skip = start // rows
    return pl.pallas_call(
        functools.partial(apply_kernel, 1),
        grid=(points - 1,),
        in_specs=[ORDER, SMEM, SMEM, pl.BlockSpec((1, rows, kept), lambda i: (i + 1, skip, 0))]
        + [own_spec] * (1 + len(others)),
        out_specs=pl.BlockSpec((1, rows, width), lambda i: (i, 0, 0)),
        out_shape=jax.ShapeDtypeStruct((points - 1, rows, width), jnp.bfloat16),
        scratch_shapes=[pltpu.VMEM((kept, width), jnp.bfloat16)],
        compiler_params=params(),
        cost_estimate=CHEAP,
        name="apply_rest",
    )(earlier, counts, me, sets, own, *others)


def combine(sets, own, others, counts, me, kin, length, block, tail):
    points, _, kept = sets.shape
    share, width = own.shape[1:]
    steps = length // block
    body = steps - tail // block
    peers = len(others)

    def kernel(counts_ref, me_ref, kin_ref, sets_ref, own_ref, *refs):
        other_refs, outs, vectors = refs[:peers], refs[peers:-1], refs[-1]
        i = pl.program_id(0)

        @pl.when(i == 0)
        def _():
            for j in range(points):
                pieces = [r[j] for r in (own_ref, *other_refs)]
                fill(vectors.at[j], pieces, counts_ref[j], me_ref[0])

        products = [
            jnp.dot(sets_ref[j], vectors[j], preferred_element_type=jnp.float32)
            for j in range(points)
        ]

        def mixed(a):
            total = kin_ref[a, 0] * products[0]
            for j in range(1, points):
                total += kin_ref[a, j] * products[j]
            return total.astype(jnp.bfloat16)

        for a in range(points - 1):
            outs[a][...] = mixed(a)
        last = mixed(points - 1)

        @pl.when(i < body)
        def _():
            outs[points - 1][...] = last

        @pl.when(i >= body)
        def _():
            outs[points][...] = last

    whole = pl.BlockSpec((block, width), lambda i: (i, 0))
    return pl.pallas_call(
        kernel,
        grid=(steps,),
        in_specs=[SMEM, SMEM, SMEM, pl.BlockSpec((points, block, kept), lambda i: (0, i, 0))]
        + [VMEM] * (1 + peers),
        out_specs=[whole] * (points - 1)
        + [
            pl.BlockSpec((block, width), lambda i: (jnp.minimum(i, body - 1), 0)),
            pl.BlockSpec((block, width), lambda i: (jnp.maximum(i - body, 0), 0)),
        ],
        out_shape=[jax.ShapeDtypeStruct((length, width), jnp.bfloat16)] * (points - 1)
        + [
            jax.ShapeDtypeStruct((length - tail, width), jnp.bfloat16),
            jax.ShapeDtypeStruct((tail, width), jnp.bfloat16),
        ],
        scratch_shapes=[pltpu.VMEM((points, kept, width), jnp.bfloat16)],
        compiler_params=params(),
        cost_estimate=CHEAP,
        name="combine",
    )(counts, me, kin, sets, own, *others)


def collect(sets, first, rest, kin, start, rows):
    points, _, kept = sets.shape
    width = first.shape[2]
    skip = start // rows

    def kernel(kin_ref, sets_ref, first_ref, rest_ref, out_ref):
        a = pl.program_id(0)
        arrived = [first_ref[0]] + [rest_ref[j] for j in range(points - 1)]
        products = contract_rows(sets_ref[0], jnp.concatenate(arrived, axis=1))
        total = kin_ref[a, 0] * products[:, :width]
        for j in range(1, points):
            total += kin_ref[a, j] * products[:, j * width : (j + 1) * width]
        out_ref[0] = total

    return pl.pallas_call(
        kernel,
        grid=(points,),
        in_specs=[SMEM, pl.BlockSpec((1, rows, kept), lambda a: (a, skip, 0)), VMEM, VMEM],
        out_specs=pl.BlockSpec((1, kept, width), lambda a: (a, 0, 0)),
        out_shape=jax.ShapeDtypeStruct((points, kept, width), jnp.float32),
        compiler_params=params(),
        cost_estimate=CHEAP,
        name="collect",
    )(kin, sets, first, rest)


def split_blocks(total, point, counts_ref, owner_ref, me, held, own_ref, send_ref):
    blocks = owner_ref.shape[0]
    share = own_ref.shape[0]
    row = lax.broadcasted_iota(jnp.int32, total.shape, 0)
    held[...] = jnp.where(row < counts_ref[point], total, 0.0)
    for d in range(blocks):
        start = pl.multiple_of(owner_ref[lax.rem(me + d, blocks)] * share, 16)
        part = held[pl.ds(start, share), :]
        if d == 0:
            own_ref[...] = part
        else:
            send_ref[d - 1] = part.astype(send_ref.dtype)


def gather_rows(sets, arrived, before, earlier, point, block):
    kept = sets.shape[2]
    length, width = arrived.shape

    def kernel(_, sets_ref, arrived_ref, before_ref, out_ref):
        @pl.when(pl.program_id(0) == 0)
        def _():
            out_ref[...] = before_ref[0]

        out_ref[...] += contract_rows(sets_ref[0], arrived_ref[...])

    return pl.pallas_call(
        kernel,
        grid=(length // block,),
        in_specs=[
            ORDER,
            pl.BlockSpec((1, block, kept), lambda i: (point, i, 0)),
            pl.BlockSpec((block, width), lambda i: (i, 0)),
            pl.BlockSpec((1, kept, width), lambda i: (point, 0, 0)),
        ],
        out_specs=pl.BlockSpec((kept, width), lambda i: (0, 0)),
        out_shape=jax.ShapeDtypeStruct((kept, width), jnp.float32),
        compiler_params=params(),
        cost_estimate=CHEAP,
        name="gather_rows",
    )(earlier, sets, arrived, before)


def finish_rows(sets, arrived, before, earlier, counts, me, owner_map, point, block, share):
    kept = sets.shape[2]
    length, width = arrived.shape
    steps = length // block
    blocks = owner_map.shape[0]

    def kernel(_, counts_ref, me_ref, owner_ref, sets_ref, arrived_ref, before_ref, own_ref, send_ref, total, held):
        i = pl.program_id(0)

        @pl.when(i == 0)
        def _():
            total[...] = before_ref[0]

        total[...] += contract_rows(sets_ref[0], arrived_ref[...])

        @pl.when(i == steps - 1)
        def _():
            split_blocks(total[...], point, counts_ref, owner_ref, me_ref[0], held, own_ref, send_ref)

    return pl.pallas_call(
        kernel,
        grid=(steps,),
        in_specs=[
            ORDER,
            SMEM,
            SMEM,
            SMEM,
            pl.BlockSpec((1, block, kept), lambda i: (point, i, 0)),
            pl.BlockSpec((block, width), lambda i: (i, 0)),
            pl.BlockSpec((1, kept, width), lambda i: (point, 0, 0)),
        ],
        out_specs=[
            pl.BlockSpec((share, width), lambda i: (0, 0)),
            pl.BlockSpec((blocks - 1, share, width), lambda i: (0, 0, 0)),
        ],
        out_shape=[
            jax.ShapeDtypeStruct((share, width), jnp.float32),
            jax.ShapeDtypeStruct((blocks - 1, share, width), jnp.bfloat16),
        ],
        scratch_shapes=[pltpu.VMEM((kept, width), jnp.float32)] * 2,
        compiler_params=params(),
        cost_estimate=CHEAP,
        name="finish_rows",
    )(earlier, counts, me, owner_map, sets, arrived, before)


def finish_last(sets, arrived, before, earlier, counts, me, owner_map, point, share):
    kept = sets.shape[1]
    width = arrived.shape[1]
    blocks = owner_map.shape[0]

    def kernel(_, counts_ref, me_ref, owner_ref, sets_ref, arrived_ref, before_ref, own_ref, send_ref, held):
        total = before_ref[...] + contract_rows(sets_ref[...], arrived_ref[...])
        split_blocks(total, point, counts_ref, owner_ref, me_ref[0], held, own_ref, send_ref)

    return pl.pallas_call(
        kernel,
        in_specs=[ORDER] + [SMEM] * 3 + [VMEM] * 3,
        out_specs=[VMEM, VMEM],
        out_shape=[
            jax.ShapeDtypeStruct((share, width), jnp.float32),
            jax.ShapeDtypeStruct((blocks - 1, share, width), jnp.bfloat16),
        ],
        scratch_shapes=[pltpu.VMEM((kept, width), jnp.float32)],
        compiler_params=params(),
        cost_estimate=CHEAP,
        name="finish_last",
    )(earlier, counts, me, owner_map, sets, arrived, before)


def place_last(ready, own, others):
    points, share, width = ready.shape

    def kernel(_, own_ref, *rest):
        *other_refs, out_ref = rest
        total = own_ref[...]
        for r in other_refs:
            total += r[...].astype(jnp.float32)
        out_ref[0] = total.astype(out_ref.dtype)

    return pl.pallas_call(
        kernel,
        grid=(1,),
        in_specs=[ORDER] + [VMEM] * (1 + len(others)),
        out_specs=pl.BlockSpec((1, share, width), lambda i: (points - 1, 0, 0)),
        out_shape=jax.ShapeDtypeStruct(ready.shape, ready.dtype),
        input_output_aliases={0: 0},
        compiler_params=params(),
        cost_estimate=CHEAP,
        name="place_last",
    )(ready, own, *others)


def exchange(own, send):
    for d in range(1, send.shape[0] + 1):
        own += shifted(send[d - 1], "rows", d).astype(jnp.float32)
    return own


def per_device(coeffs, counts, kinetic, pair_table, trial_vecs, owner_map):
    points, radial, kept = coeffs.shape
    share, width = trial_vecs.shape[1:]
    blocks = owner_map.shape[0]
    me = lax.axis_index("rows").astype(jnp.int32).reshape(1)
    unit = radial // 12
    plain, tail = 4 * unit, unit
    mixed_rows = radial - plain
    peers = range(1, blocks)

    first_own = trial_vecs[:1]
    first_vectors = [shifted(first_own, "rows", d) for d in peers]
    vectors = [shifted(trial_vecs, "rows", d) for d in peers]

    first = apply_first(coeffs, first_own, first_vectors, counts, me, mixed_rows, plain)
    first_sent = shifted(first, "blk", 1)

    table_index = jnp.arange(kinetic.shape[0], dtype=jnp.int32)
    one_hot = pair_table[:, :, None] == table_index[None, None, :]
    kin_own = jnp.sum(jnp.where(one_hot, kinetic[None, None, :], 0.0), axis=2)
    rest = apply_rest(coeffs, trial_vecs, vectors, first, counts, me, mixed_rows, plain)
    rest_sent = shifted(rest, "blk", 1)
    kin_next = shifted(after(kin_own, rest, first_sent), "blk", -1)
    mixed = combine(
        coeffs, trial_vecs, vectors, counts, me, kin_next, mixed_rows, unit, tail
    )
    mixed_sent = []
    previous = rest
    for z in mixed:
        z = after(z, previous)
        previous = z
        mixed_sent.append(shifted(z, "blk", 1))

    base = collect(coeffs, first_sent, rest_sent, kin_own, mixed_rows, plain)
    done = []
    earlier = first_sent
    for a in range(points - 1):
        own, send = finish_rows(
            coeffs, mixed_sent[a], base, earlier, counts, me, owner_map, a, mixed_rows // 2, share
        )
        earlier = own
        done.append(exchange(own, send))
    last = points - 1
    total = gather_rows(coeffs, mixed_sent[last], base, earlier, last, mixed_rows - tail)
    ready = jnp.stack(done + done[:1]).astype(jnp.bfloat16)
    own, send = finish_last(
        coeffs[last, mixed_rows - tail : mixed_rows], mixed_sent[points], total, ready, counts, me, owner_map, last, share
    )
    return place_last(ready, own, [shifted(send[d - 1], "rows", d) for d in peers])


def solution(mesh):
    in_specs = (P("blk", "rows", None), P("blk"), P(), P("blk", None), P("blk", "rows", None), P())
    out_specs = P("blk", "rows", None)
    return jax.shard_map(
        per_device, mesh=mesh, in_specs=in_specs, out_specs=out_specs, check_vma=False
    )
```

time: 354 us -> 93 us (0.26)
  waiting for transfers between devices: 259 us -> 41.1 us
  matrix products: 37.7 us -> 0 us
  Pallas kernels: 0 us -> 34.8 us
  other arithmetic: 23.2 us -> 0.23 us
  starting transfers between devices: 0.46 us -> 13.7 us
  between operations: 13.4 us -> 0.18 us
  blocking collectives: 10.5 us -> 0 us
  local copies, waits for them, and re-layouts: 9.24 us -> 2.55 us
    ppermute x2 -> x14, waiting for transfers between devices: 216 us -> 41.1 us  [shifted(): return lax.ppermute(block, axis, route)]
    reduce_scatter x1 -> x0, waiting for transfers between devices: 43.2 us -> none  [per_device(): lax.psum_scatter(ordered.astype(jnp.bfloat16), 'rows', scatter_dimension=...]
    dot_general x2 -> x0, matrix products: 37.7 us -> none  [the longest x1 34.6 us: per_device(): jnp.einsum('irk,jrl->ijkl', masked, prev_sets, preferred_element_type=jnp...]
    pallas_call x0 -> x10, Pallas kernels: none -> 34.8 us  [the longest x1 10.2 us: combine(): pl.pallas_call(kernel, grid=(steps,), in_specs=[SMEM, SMEM, SMEM, pl.Bloc...]
    mul x1 -> x0, other arithmetic: 16.6 us -> none  [per_device(): masked = coeffs * keep_mask[:, None, :]]
    ppermute x2 -> x14, starting transfers between devices: 0.46 us -> 13.7 us  [shifted(): return lax.ppermute(block, axis, route)]
    all_gather x1 -> x0, blocking collectives: 10.5 us -> none  [per_device(): prev_whole = lax.all_gather(prev_rows, 'rows', axis=1, tiled=True)]
    gather x4 -> x0, local copies, waits for them, and re-layouts: 7.57 us -> none  [per_device(): jnp.take(grouped, owner_map, axis=2).reshape(ang_dev, ang_dev, kept, kept)]
  transfers between devices with their start and end apart: 3 -> 14, of which waited for: 3 -> 9; matrix products, arithmetic and copies ran while one was open for 0% -> 2% of each run, Pallas kernels for 0% -> 36%
where the time goes in v2:
time: 93 us; the launch traced here: 92.6 us
  waiting for transfers between devices  41.1 us (44%)
  Pallas kernels  34.8 us (37%)
  starting transfers between devices  13.7 us (15%)
  local copies, waits for them, and re-layouts  2.55 us (3%)
    ppermute x14, waiting for transfers between devices, shifted(): return lax.ppermute(block, axis, route)  41.1 us
    ppermute x14, starting transfers between devices, shifted(): return lax.ppermute(block, axis, route)  13.7 us
    pallas_call x1, Pallas kernels, combine(): pl.pallas_call(kernel, grid=(steps,), in_specs=[SMEM, SMEM, SMEM, pl.Bloc...  10.2 us
    pallas_call x3, Pallas kernels, finish_rows(): pl.pallas_call(kernel, grid=(steps,), in_specs=[ORDER, SMEM, SMEM, SMEM,...  8.26 us
    pallas_call x1, Pallas kernels, collect(): pl.pallas_call(kernel, grid=(points,), in_specs=[SMEM, pl.BlockSpec((1, r...  5.99 us
    pallas_call x1, Pallas kernels, apply_rest(): pl.pallas_call(functools.partial(apply_kernel, 1), grid=(points - 1,), in...  4.09 us
    pallas_call x1, Pallas kernels, gather_rows(): pl.pallas_call(kernel, grid=(length // block,), in_specs=[ORDER, pl.Block...  2.7 us
    pallas_call x1, Pallas kernels, apply_first(): pl.pallas_call(kernel, grid=(2,), in_specs=[SMEM, SMEM, pl.BlockSpec((1,...  1.99 us
  transfers between devices with their start and end apart: 14, of which 9 were waited for; matrix products, arithmetic and copies ran while one was open for 2% of the time, Pallas kernels for 36%

profile of v2, /device:TPU:0, one launch (start us, length us, event | category | flops | bytes accessed | tf_op | source)
XLA Modules:
  0.0 92.6 jit_solution(15463101667373497615)
XLA Ops:
  0.0 2.9 %collective-permute-start.2 = (bf16[4,192,128]{2,1,0:T(8,128)(2,1)}, bf16[4,192,128]{2,1,0:T(8,128)(2,1)S(1)}, u32[]{:S(2)}, u32[]{:S(2)}) collective-permute-start(bf16[4,192,128]{2,1,0:T(8,128)(2,1)} %own_ref.3), channel_id=1, source_target_pairs={{0,1},{1,0},{2,3},{3,2},{4,5},{5,4},{6,7},{7,6},{8,9},{9,8},{10,11... | collective-permute-start | bytes 589832 | tf_op jit(solution)/shard_map/ppermute | solution.py:20
  2.9 0.8 slice.6.own_ref
  3.8 0.1 collective-permute-start
  3.9 5.3 %collective-permute-done.rest_0_ = bf16[1,192,128]{2,1,0:T(8,128)(2,1)S(1)} collective-permute-done((bf16[1,192,128]{2,1,0:T(8,128)(2,1)S(1)}, bf16[1,192,128]{2,1,0:T(8,128)(2,1)S(1)}, u32[]{:S(2)}, u32[]{:S(2)}) %collective-permute-start) | collective-permute-done | bytes 49184 | tf_op jit(solution)/shard_map/ppermute | solution.py:20
  9.2 0.7 copy-done.2
  9.8 2.0 %apply_first.1._ = bf16[1,2048,128]{2,1,0:T(8,128)(2,1)S(1)} custom-call(s32[4]{0:T(128)S(1)} %copy-done.2, s32[1]{0:T(128)} %bitcast.me_ref, bf16[4,6144,384]{2,1,0:T(8,128)(2,1)} %sets_ref.15, bf16[1,192,128]{2,1,0:T(8,128)(2,1)S(1)} %slice.6.own_ref, bf16[1,192,128]{2,1,0:T(8,128)(2,1)S(1)} %collective-permute-done.rest_0_), custom_call_target="tpu_custom_call" | custom-call | flops 1 | bytes 1 | tf_op jit(solution)/shard_map/apply_first/pallas_call | solution.py:73
  11.8 0.1 collective-permute-start.1
  11.9 0.0 collective-permute-done.2.rest_0_.refs_0_
  11.9 0.0 copy-done.1
  11.9 4.1 %apply_rest.1 = bf16[3,2048,128]{2,1,0:T(8,128)(2,1)S(1)} custom-call(bf16[1,2048,128]{2,1,0:T(8,128)(2,1)S(1)} %apply_first.1._, s32[4]{0:T(128)S(1)} %copy-done.2, s32[1]{0:T(128)} %bitcast.me_ref, bf16[4,6144,384]{2,1,0:T(8,128)(2,1)} %sets_ref.15, bf16[4,192,128]{2,1,0:T(8,128)(2,1)S(1)} %copy-done.1, ...), custom_call_target="tpu_custom_call" | custom-call | flops 1 | bytes 1 | tf_op jit(solution)/shard_map/apply_rest/pallas_call | solution.py:92
  16.0 1.8 %collective-permute-start.5 = (bf16[3,2048,128]{2,1,0:T(8,128)(2,1)S(1)}, bf16[3,2048,128]{2,1,0:T(8,128)(2,1)S(1)}, u32[]{:S(2)}, u32[]{:S(2)}) collective-permute-start(bf16[3,2048,128]{2,1,0:T(8,128)(2,1)S(1)} %apply_rest.1), channel_id=1, source_target_pairs={{0,2},{2,4},{4,6},{6,8},{8,10},{10,12},{12,14},{14,16},{16,18},{18... | collective-permute-start | bytes 4718600 | tf_op jit(solution)/shard_map/ppermute | solution.py:20
  17.8 0.0 copy-done.5
  17.8 0.0 copy-done.6
  17.8 0.2 select_reduce_fusion.kin_ref
  18.0 5.2 %collective-permute-done.1.first_ref._ = bf16[1,2048,128]{2,1,0:T(8,128)(2,1)S(1)} collective-permute-done((bf16[1,2048,128]{2,1,0:T(8,128)(2,1)S(1)}, bf16[1,2048,128]{2,1,0:T(8,128)(2,1)S(1)}, u32[]{:S(2)}, u32[]{:S(2)}) %collective-permute-start.1) | collective-permute-done | bytes 524320 | tf_op jit(solution)/shard_map/ppermute | solution.py:20
  23.2 0.0 collective-permute-start.3
  23.2 1.3 %collective-permute-done.3.kin_ref = f32[4,4]{1,0:T(4,128)S(1)} collective-permute-done((f32[4,4]{1,0:T(4,128)S(1)}, f32[4,4]{1,0:T(4,128)S(1)}, u32[]{:S(2)}, u32[]{:S(2)}) %collective-permute-start.3) | collective-permute-done | bytes 96 | tf_op jit(solution)/shard_map/ppermute | solution.py:20
  24.5 10.2 %combine.1 = (bf16[4096,128]{1,0:T(8,128)(2,1)S(1)}, bf16[4096,128]{1,0:T(8,128)(2,1)S(1)}, bf16[4096,128]{1,0:T(8,128)(2,1)}, bf16[3584,128]{1,0:T(8,128)(2,1)S(1)}, bf16[512,128]{1,0:T(8,128)(2,1)S(1)}) custom-call(s32[4]{0:T(128)S(1)} %copy-done.2, s32[1]{0:T(128)} %bitcast.me_ref, f32[4,4]{1,0:T(4,128)S(1)} %collective-permute-done.3.kin_ref, ...), custom_call_target="tpu_custom_call" | custom-call | flops 1 | bytes 1 | tf_op jit(solution)/shard_map/combine/pallas_call | solution.py:147
  34.7 0.0 collective-permute-start.4
  34.8 0.0 collective-permute-start.7
  34.8 1.7 %collective-permute-start.9 = (bf16[4096,128]{1,0:T(8,128)(2,1)}, bf16[4096,128]{1,0:T(8,128)(2,1)S(1)}, u32[]{:S(2)}, u32[]{:S(2)}) collective-permute-start(bf16[4096,128]{1,0:T(8,128)(2,1)} %get-tuple-element.34), channel_id=1, source_target_pairs={{0,2},{2,4},{4,6},{6,8},{8,10},{10,12},{12,14},{14,16},{16,18},{18... | collective-permute-start | bytes 3145736 | tf_op jit(solution)/shard_map/ppermute | solution.py:20
  36.5 0.0 collective-permute-start.12
  36.5 3.6 %collective-permute-done.5.rest_ref = bf16[3,2048,128]{2,1,0:T(8,128)(2,1)S(1)} collective-permute-done((bf16[3,2048,128]{2,1,0:T(8,128)(2,1)S(1)}, bf16[3,2048,128]{2,1,0:T(8,128)(2,1)S(1)}, u32[]{:S(2)}, u32[]{:S(2)}) %collective-permute-start.5) | collective-permute-done | bytes 1572896 | tf_op jit(solution)/shard_map/ppermute | solution.py:20
  40.1 6.0 %collect.1.before_ref = f32[4,384,128]{2,1,0:T(8,128)S(1)} custom-call(f32[4,4]{1,0:T(4,128)S(1)} %select_reduce_fusion.kin_ref, bf16[4,6144,384]{2,1,0:T(8,128)(2,1)} %sets_ref.15, bf16[1,2048,128]{2,1,0:T(8,128)(2,1)S(1)} %collective-permute-done.1.first_ref._, bf16[3,2048,128]{2,1,0:T(8,128)(2,1)S(1)} %collective-permute-done.5.rest_ref), custom_call_target="tpu_custom_call" | custom-call | flops 1 | bytes 1 | tf_op jit(solution)/shard_map/collect/pallas_call | solution.py:183
  46.1 5.7 %collective-permute-done.4.arrived_ref = bf16[4096,128]{1,0:T(8,128)(2,1)S(1)} collective-permute-done((bf16[4096,128]{1,0:T(8,128)(2,1)S(1)}, bf16[4096,128]{1,0:T(8,128)(2,1)S(1)}, u32[]{:S(2)}, u32[]{:S(2)}) %collective-permute-start.4) | collective-permute-done | bytes 1048608 | tf_op jit(solution)/shard_map/ppermute | solution.py:20
  51.7 0.0 copy-done.3
  51.7 0.0 copy-done.4
  51.7 2.8 %finish_rows.3 = (f32[192,128]{1,0:T(8,128)S(1)}, bf16[1,192,128]{2,1,0:T(8,128)(2,1)S(1)}) custom-call(bf16[1,2048,128]{2,1,0:T(8,128)(2,1)S(1)} %collective-permute-done.1.first_ref._, s32[4]{0:T(128)S(1)} %copy-done.3, s32[1]{0:T(128)} %bitcast.me_ref, s32[2]{0:T(128)S(1)} %copy-done.4, bf16[4,6144,384]{2,1,0:T(8,128)(2,1)} %sets_ref.15, ...), custom_call_target="tpu_custom_call" | custom-call | flops 1 | bytes 1 | tf_op jit(solution)/shard_map/finish_rows/pallas_call | solution.py:256
  54.5 1.7 %collective-permute-start.6 = (bf16[192,128]{1,0:T(8,128)(2,1)S(1)}, bf16[192,128]{1,0:T(8,128)(2,1)S(1)}, u32[]{:S(2)}, u32[]{:S(2)}) collective-permute-start(bf16[192,128]{1,0:T(8,128)(2,1)S(1)} %bitcast.13), channel_id=1, source_target_pairs={{0,1},{1,0},{2,3},{3,2},{4,5},{5,4},{6,7},{7,6},{8,9},{9,8},{10,11... | collective-permute-start | bytes 147464 | tf_op jit(solution)/shard_map/ppermute | solution.py:20
  56.2 1.0 %slice_bitcast_fusion.sets_ref = bf16[512,384]{1,0:T(8,128)(2,1)S(1)} fusion(bf16[4,6144,384]{2,1,0:T(8,128)(2,1)} %sets_ref.15), kind=kLoop, calls=%fused_computation | loop fusion | bytes 786432 | tf_op jit(solution)/shard_map/squeeze | solution.py:382
  57.3 0.1 collective-permute-start.11
  57.3 5.6 %collective-permute-done.7.arrived_ref = bf16[4096,128]{1,0:T(8,128)(2,1)S(1)} collective-permute-done((bf16[4096,128]{1,0:T(8,128)(2,1)S(1)}, bf16[4096,128]{1,0:T(8,128)(2,1)S(1)}, u32[]{:S(2)}, u32[]{:S(2)}) %collective-permute-start.7) | collective-permute-done | bytes 1048608 | tf_op jit(solution)/shard_map/ppermute | solution.py:20
  63.0 2.8 %finish_rows.4 = (f32[192,128]{1,0:T(8,128)S(1)}, bf16[1,192,128]{2,1,0:T(8,128)(2,1)S(1)}) custom-call(f32[192,128]{1,0:T(8,128)S(1)} %get-tuple-element.27._, s32[4]{0:T(128)S(1)} %copy-done.3, s32[1]{0:T(128)} %bitcast.me_ref, s32[2]{0:T(128)S(1)} %copy-done.4, bf16[4,6144,384]{2,1,0:T(8,128)(2,1)} %sets_ref.15, ...), custom_call_target="tpu_custom_call" | custom-call | flops 1 | bytes 1 | tf_op jit(solution)/shard_map/finish_rows/pallas_call | solution.py:256
  65.7 1.7 %collective-permute-start.8 = (bf16[192,128]{1,0:T(8,128)(2,1)S(1)}, bf16[192,128]{1,0:T(8,128)(2,1)S(1)}, u32[]{:S(2)}, u32[]{:S(2)}) collective-permute-start(bf16[192,128]{1,0:T(8,128)(2,1)S(1)} %bitcast.14), channel_id=1, source_target_pairs={{0,1},{1,0},{2,3},{3,2},{4,5},{5,4},{6,7},{7,6},{8,9},{9,8},{10,11... | collective-permute-start | bytes 147464 | tf_op jit(solution)/shard_map/ppermute | solution.py:20
  67.5 6.7 %collective-permute-done.9.arrived_ref = bf16[4096,128]{1,0:T(8,128)(2,1)S(1)} collective-permute-done((bf16[4096,128]{1,0:T(8,128)(2,1)}, bf16[4096,128]{1,0:T(8,128)(2,1)S(1)}, u32[]{:S(2)}, u32[]{:S(2)}) %collective-permute-start.9) | collective-permute-done | bytes 1048608 | tf_op jit(solution)/shard_map/ppermute | solution.py:20
  74.2 2.8 %finish_rows.5 = (f32[192,128]{1,0:T(8,128)S(1)}, bf16[1,192,128]{2,1,0:T(8,128)(2,1)S(1)}) custom-call(f32[192,128]{1,0:T(8,128)S(1)} %get-tuple-element.31._, s32[4]{0:T(128)S(1)} %copy-done.3, s32[1]{0:T(128)} %bitcast.me_ref, s32[2]{0:T(128)S(1)} %copy-done.4, bf16[4,6144,384]{2,1,0:T(8,128)(2,1)} %sets_ref.15, ...), custom_call_target="tpu_custom_call" | custom-call | flops 1 | bytes 1 | tf_op jit(solution)/shard_map/finish_rows/pallas_call | solution.py:256
  77.0 1.7 %collective-permute-start.10 = (bf16[192,128]{1,0:T(8,128)(2,1)S(1)}, bf16[192,128]{1,0:T(8,128)(2,1)S(1)}, u32[]{:S(2)}, u32[]{:S(2)}) collective-permute-start(bf16[192,128]{1,0:T(8,128)(2,1)S(1)} %bitcast.15), channel_id=1, source_target_pairs={{0,1},{1,0},{2,3},{3,2},{4,5},{5,4},{6,7},{7,6},{8,9},{9,8},{10,11... | collective-permute-start | bytes 147464 | tf_op jit(solution)/shard_map/ppermute | solution.py:20
  78.7 5.3 %collective-permute-done.12.arrived_ref = bf16[3584,128]{1,0:T(8,128)(2,1)S(1)} collective-permute-done((bf16[3584,128]{1,0:T(8,128)(2,1)S(1)}, bf16[3584,128]{1,0:T(8,128)(2,1)S(1)}, u32[]{:S(2)}, u32[]{:S(2)}) %collective-permute-start.12) | collective-permute-done | bytes 917536 | tf_op jit(solution)/shard_map/ppermute | solution.py:20
  84.0 2.7 %gather_rows.1.before_ref = f32[384,128]{1,0:T(8,128)S(1)} custom-call(f32[192,128]{1,0:T(8,128)S(1)} %get-tuple-element.35._, bf16[4,6144,384]{2,1,0:T(8,128)(2,1)} %sets_ref.15, bf16[3584,128]{1,0:T(8,128)(2,1)S(1)} %collective-permute-done.12.arrived_ref, f32[4,384,128]{2,1,0:T(8,128)S(1)} %collect.1.before_ref), custom_call_target="tpu_custom_call" | custom-call | flops 1 | bytes 1 | tf_op jit(solution)/shard_map/gather_rows/pallas_call | solution.py:220
  86.7 0.0 collective-permute-done.6
  86.8 0.0 collective-permute-done.8
  86.8 0.0 collective-permute-done.10
  86.9 0.0 copy-start
  86.9 0.0 collective-permute-done.11.arrived_ref
  86.9 0.9 finish_last.1
  87.8 1.7 %collective-permute-start.13 = (bf16[192,128]{1,0:T(8,128)(2,1)S(1)}, bf16[192,128]{1,0:T(8,128)(2,1)S(1)}, u32[]{:S(2)}, u32[]{:S(2)}) collective-permute-start(bf16[192,128]{1,0:T(8,128)(2,1)S(1)} %bitcast.16), channel_id=1, source_target_pairs={{0,1},{1,0},{2,3},{3,2},{4,5},{5,4},{6,7},{7,6},{8,9},{9,8},{10,11... | collective-permute-start | bytes 147464 | tf_op jit(solution)/shard_map/ppermute | solution.py:20
  89.5 2.4 %collective-permute-done.13.rest_0_ = bf16[192,128]{1,0:T(8,128)(2,1)S(1)} collective-permute-done((bf16[192,128]{1,0:T(8,128)(2,1)S(1)}, bf16[192,128]{1,0:T(8,128)(2,1)S(1)}, u32[]{:S(2)}, u32[]{:S(2)}) %collective-permute-start.13) | collective-permute-done | bytes 49184 | tf_op jit(solution)/shard_map/ppermute | solution.py:20
  91.9 0.6 place_last.1
  (11 shorter events, 0.1 us)
Async XLA Ops:
  0.0 11.9 %copy-start.1 = (bf16[4,192,128]{2,1,0:T(8,128)(2,1)S(1)}, bf16[4,192,128]{2,1,0:T(8,128)(2,1)}, u32[]{:S(2)}) copy-start(bf16[4,192,128]{2,1,0:T(8,128)(2,1)} %own_ref.3) | copy-start | bytes 589828
  0.0 11.9 %collective-permute-start.2 = (bf16[4,192,128]{2,1,0:T(8,128)(2,1)}, bf16[4,192,128]{2,1,0:T(8,128)(2,1)S(1)}, u32[]{:S(2)}, u32[]{:S(2)}) collective-permute-start(bf16[4,192,128]{2,1,0:T(8,128)(2,1)} %own_ref.3), channel_id=1, source_target_pairs={{0,1},{1,0},{2,3},{3,2},{4,5},{5,4},{6,7},{7,6},{8,9},{9,8},{10,11... | collective-permute-start | bytes 589832 | tf_op jit(solution)/shard_map/ppermute | solution.py:20
  3.8 5.4 %collective-permute-start = (bf16[1,192,128]{2,1,0:T(8,128)(2,1)S(1)}, bf16[1,192,128]{2,1,0:T(8,128)(2,1)S(1)}, u32[]{:S(2)}, u32[]{:S(2)}) collective-permute-start(bf16[1,192,128]{2,1,0:T(8,128)(2,1)S(1)} %slice.6.own_ref), channel_id=1, source_target_pairs={{0,1},{1,0},{2,3},{3,2},{4,5},{5,4},{6,7},{7,6},{8,9},{9,8},{10,11... | collective-permute-start | bytes 147464 | tf_op jit(solution)/shard_map/ppermute | solution.py:20
  9.2 0.7 copy-start.2
  9.8 8.0 %copy-start.5 = (s32[4,4]{1,0:T(4,128)S(1)}, s32[4,4]{1,0:T(4,128)}, u32[]{:S(2)}) copy-start(s32[4,4]{1,0:T(4,128)} %param.9) | copy-start | bytes 196
  9.8 8.0 %copy-start.6 = (f32[64]{0:T(128)S(1)}, f32[64]{0:T(128)}, u32[]{:S(2)}) copy-start(f32[64]{0:T(128)} %param.8) | copy-start | bytes 772
  11.8 11.4 %collective-permute-start.1 = (bf16[1,2048,128]{2,1,0:T(8,128)(2,1)S(1)}, bf16[1,2048,128]{2,1,0:T(8,128)(2,1)S(1)}, u32[]{:S(2)}, u32[]{:S(2)}) collective-permute-start(bf16[1,2048,128]{2,1,0:T(8,128)(2,1)S(1)} %apply_first.1._), channel_id=1, source_target_pairs={{0,2},{2,4},{4,6},{6,8},{8,10},{10,12},{12,14},{14,16},{16,18},{18... | collective-permute-start | bytes 1572872 | tf_op jit(solution)/shard_map/ppermute | solution.py:20
  16.0 24.1 %collective-permute-start.5 = (bf16[3,2048,128]{2,1,0:T(8,128)(2,1)S(1)}, bf16[3,2048,128]{2,1,0:T(8,128)(2,1)S(1)}, u32[]{:S(2)}, u32[]{:S(2)}) collective-permute-start(bf16[3,2048,128]{2,1,0:T(8,128)(2,1)S(1)} %apply_rest.1), channel_id=1, source_target_pairs={{0,2},{2,4},{4,6},{6,8},{8,10},{10,12},{12,14},{14,16},{16,18},{18... | collective-permute-start | bytes 4718600 | tf_op jit(solution)/shard_map/ppermute | solution.py:20
  18.0 33.7 %copy-start.3 = (s32[4]{0:T(128)S(1)}, s32[4]{0:T(128)}, u32[]{:S(2)}) copy-start(s32[4]{0:T(128)} %counts_ref.13) | copy-start | bytes 52
  18.0 33.7 %copy-start.4 = (s32[2]{0:T(128)S(1)}, s32[2]{0:T(128)}, u32[]{:S(2)}) copy-start(s32[2]{0:T(128)} %owner_ref.7) | copy-start | bytes 28
  23.2 1.3 %collective-permute-start.3 = (f32[4,4]{1,0:T(4,128)S(1)}, f32[4,4]{1,0:T(4,128)S(1)}, u32[]{:S(2)}, u32[]{:S(2)}) collective-permute-start(f32[4,4]{1,0:T(4,128)S(1)} %select_reduce_fusion.kin_ref), channel_id=1, source_target_pairs={{0,30},{2,0},{4,2},{6,4},{8,6},{10,8},{12,10},{14,12},{16,14},{18,... | collective-permute-start | bytes 200 | tf_op jit(solution)/shard_map/ppermute | solution.py:20
  34.7 17.0 %collective-permute-start.4 = (bf16[4096,128]{1,0:T(8,128)(2,1)S(1)}, bf16[4096,128]{1,0:T(8,128)(2,1)S(1)}, u32[]{:S(2)}, u32[]{:S(2)}) collective-permute-start(bf16[4096,128]{1,0:T(8,128)(2,1)S(1)} %get-tuple-element.26), channel_id=1, source_target_pairs={{0,2},{2,4},{4,6},{6,8},{8,10},{10,12},{12,14},{14,16},{16,18},{18... | collective-permute-start | bytes 3145736 | tf_op jit(solution)/shard_map/ppermute | solution.py:20
  34.8 28.2 %collective-permute-start.7 = (bf16[4096,128]{1,0:T(8,128)(2,1)S(1)}, bf16[4096,128]{1,0:T(8,128)(2,1)S(1)}, u32[]{:S(2)}, u32[]{:S(2)}) collective-permute-start(bf16[4096,128]{1,0:T(8,128)(2,1)S(1)} %get-tuple-element.30), channel_id=1, source_target_pairs={{0,2},{2,4},{4,6},{6,8},{8,10},{10,12},{12,14},{14,16},{16,18},{18... | collective-permute-start | bytes 3145736 | tf_op jit(solution)/shard_map/ppermute | solution.py:20
  34.8 39.4 %collective-permute-start.9 = (bf16[4096,128]{1,0:T(8,128)(2,1)}, bf16[4096,128]{1,0:T(8,128)(2,1)S(1)}, u32[]{:S(2)}, u32[]{:S(2)}) collective-permute-start(bf16[4096,128]{1,0:T(8,128)(2,1)} %get-tuple-element.34), channel_id=1, source_target_pairs={{0,2},{2,4},{4,6},{6,8},{8,10},{10,12},{12,14},{14,16},{16,18},{18... | collective-permute-start | bytes 3145736 | tf_op jit(solution)/shard_map/ppermute | solution.py:20
  36.5 47.6 %collective-permute-start.12 = (bf16[3584,128]{1,0:T(8,128)(2,1)S(1)}, bf16[3584,128]{1,0:T(8,128)(2,1)S(1)}, u32[]{:S(2)}, u32[]{:S(2)}) collective-permute-start(bf16[3584,128]{1,0:T(8,128)(2,1)S(1)} %get-tuple-element.39), channel_id=1, source_target_pairs={{0,2},{2,4},{4,6},{6,8},{8,10},{10,12},{12,14},{14,16},{16,18},{18... | collective-permute-start | bytes 2752520 | tf_op jit(solution)/shard_map/ppermute | solution.py:20
  54.5 32.2 %collective-permute-start.6 = (bf16[192,128]{1,0:T(8,128)(2,1)S(1)}, bf16[192,128]{1,0:T(8,128)(2,1)S(1)}, u32[]{:S(2)}, u32[]{:S(2)}) collective-permute-start(bf16[192,128]{1,0:T(8,128)(2,1)S(1)} %bitcast.13), channel_id=1, source_target_pairs={{0,1},{1,0},{2,3},{3,2},{4,5},{5,4},{6,7},{7,6},{8,9},{9,8},{10,11... | collective-permute-start | bytes 147464 | tf_op jit(solution)/shard_map/ppermute | solution.py:20
  57.3 29.6 %collective-permute-start.11 = (bf16[512,128]{1,0:T(8,128)(2,1)S(1)}, bf16[512,128]{1,0:T(8,128)(2,1)S(1)}, u32[]{:S(2)}, u32[]{:S(2)}) collective-permute-start(bf16[512,128]{1,0:T(8,128)(2,1)S(1)} %get-tuple-element.40), channel_id=1, source_target_pairs={{0,2},{2,4},{4,6},{6,8},{8,10},{10,12},{12,14},{14,16},{16,18},{18... | collective-permute-start | bytes 393224 | tf_op jit(solution)/shard_map/ppermute | solution.py:20
  65.7 21.0 %collective-permute-start.8 = (bf16[192,128]{1,0:T(8,128)(2,1)S(1)}, bf16[192,128]{1,0:T(8,128)(2,1)S(1)}, u32[]{:S(2)}, u32[]{:S(2)}) collective-permute-start(bf16[192,128]{1,0:T(8,128)(2,1)S(1)} %bitcast.14), channel_id=1, source_target_pairs={{0,1},{1,0},{2,3},{3,2},{4,5},{5,4},{6,7},{7,6},{8,9},{9,8},{10,11... | collective-permute-start | bytes 147464 | tf_op jit(solution)/shard_map/ppermute | solution.py:20
  77.0 9.8 %collective-permute-start.10 = (bf16[192,128]{1,0:T(8,128)(2,1)S(1)}, bf16[192,128]{1,0:T(8,128)(2,1)S(1)}, u32[]{:S(2)}, u32[]{:S(2)}) collective-permute-start(bf16[192,128]{1,0:T(8,128)(2,1)S(1)} %bitcast.15), channel_id=1, source_target_pairs={{0,1},{1,0},{2,3},{3,2},{4,5},{5,4},{6,7},{7,6},{8,9},{9,8},{10,11... | collective-permute-start | bytes 147464 | tf_op jit(solution)/shard_map/ppermute | solution.py:20
  86.9 5.1 %copy-start = (bf16[4,192,128]{2,1,0:T(8,128)(2,1)}, bf16[4,192,128]{2,1,0:T(8,128)(2,1)S(1)}, u32[]{:S(2)}) copy-start(bf16[4,192,128]{2,1,0:T(8,128)(2,1)S(1)} %pad_maximum_fusion._) | copy-start | bytes 589828
  87.8 4.2 %collective-permute-start.13 = (bf16[192,128]{1,0:T(8,128)(2,1)S(1)}, bf16[192,128]{1,0:T(8,128)(2,1)S(1)}, u32[]{:S(2)}, u32[]{:S(2)}) collective-permute-start(bf16[192,128]{1,0:T(8,128)(2,1)S(1)} %bitcast.16), channel_id=1, source_target_pairs={{0,1},{1,0},{2,3},{3,2},{4,5},{5,4},{6,7},{7,6},{8,9},{9,8},{10,11... | collective-permute-start | bytes 147464 | tf_op jit(solution)/shard_map/ppermute | solution.py:20

commit v3 on v2

--- a/solution.py
+++ b/solution.py
@@ -44,27 +44,51 @@
         vectors[pl.ds(start, share), :] = kept.astype(vectors.dtype)
 
 
-def apply_kernel(first, _, counts_ref, me_ref, sets_ref, own_ref, *rest):
-    *others, out_ref, vectors = rest
-    i = pl.program_id(0)
-    fill(vectors, [r[0] for r in (own_ref, *others)], counts_ref[first + i], me_ref[0])
-    out_ref[0] = jnp.dot(
-        sets_ref[0], vectors[...], preferred_element_type=jnp.float32
-    ).astype(out_ref.dtype)
-
-
-def apply_first(sets, own, others, counts, me, start, rows):
+def parcels(points):
+    return 1, points - 1
+
+
+def place(point, sizes):
+    for index, size in enumerate(sizes):
+        if point < size:
+            return index, point
+        point -= size
+    raise ValueError(point)
+
+
+def parted(vectors):
+    points, share, width = vectors.shape
+    sizes = parcels(points)
+
+    def kernel(vectors_ref, *outs):
+        start = 0
+        for out, size in zip(outs, sizes):
+            out[...] = vectors_ref[start : start + size]
+            start += size
+
+    return pl.pallas_call(
+        kernel,
+        in_specs=[VMEM],
+        out_specs=[VMEM] * len(sizes),
+        out_shape=[jax.ShapeDtypeStruct((size, share, width), vectors.dtype) for size in sizes],
+        compiler_params=params(),
+        cost_estimate=CHEAP,
+        name="parted",
+    )(vectors)
+
+
+def apply_first(sets, pieces, facts, start, rows):
     kept = sets.shape[2]
-    share, width = own.shape[1:]
+    width = pieces[0].shape[2]
     block = rows // 2
     skip = start // block
 
-    def kernel(counts_ref, me_ref, sets_ref, own_ref, *rest):
-        *pieces, out_ref, vectors = rest
+    def kernel(facts_ref, sets_ref, *rest):
+        *piece_refs, out_ref, vectors = rest
 
         @pl.when(pl.program_id(0) == 0)
         def _():
-            fill(vectors, [r[0] for r in (own_ref, *pieces)], counts_ref[0], me_ref[0])
+            fill(vectors, [r[0] for r in piece_refs], facts_ref[1], facts_ref[0])
 
         out_ref[0] = jnp.dot(
             sets_ref[0], vectors[...], preferred_element_type=jnp.float32
@@ -73,52 +97,72 @@
     return pl.pallas_call(
         kernel,
         grid=(2,),
-        in_specs=[SMEM, SMEM, pl.BlockSpec((1, block, kept), lambda i: (0, skip + i, 0))]
-        + [pl.BlockSpec((1, share, width), lambda i: (0, 0, 0))] * (1 + len(others)),
+        in_specs=[SMEM, pl.BlockSpec((1, block, kept), lambda i: (0, skip + i, 0))]
+        + [VMEM] * len(pieces),
         out_specs=pl.BlockSpec((1, block, width), lambda i: (0, i, 0)),
         out_shape=jax.ShapeDtypeStruct((1, rows, width), jnp.bfloat16),
         scratch_shapes=[pltpu.VMEM((kept, width), jnp.bfloat16)],
         compiler_params=params(),
-        cost_estimate=CHEAP,
+        cost_estimate=pl.CostEstimate(flops=10**9, bytes_accessed=10**6, transcendentals=0),
         name="apply_first",
-    )(counts, me, sets, own, *others)
-
-
-def apply_rest(sets, own, others, earlier, counts, me, start, rows):
+    )(facts, sets, *pieces)
+
+
+def apply_rest(sets, pieces, earlier, facts, start, rows):
     points, _, kept = sets.shape
-    share, width = own.shape[1:]
-    own_spec = pl.BlockSpec((1, share, width), lambda i: (i + 1, 0, 0))
+    width = pieces[0][0].shape[2]
+    blocks = len(pieces[0])
     skip = start // rows
-    return pl.pallas_call(
-        functools.partial(apply_kernel, 1),
+    sizes = parcels(points)
+
+    def kernel(_, facts_ref, sets_ref, *rest):
+        *piece_refs, out_ref, vectors = rest
+        for j in range(1, points):
+
+            @pl.when(pl.program_id(0) == j - 1)
+            def _():
+                index, row = place(j, sizes)
+                mine = piece_refs[index * blocks :][:blocks]
+                fill(vectors, [r[row] for r in mine], facts_ref[1 + j], facts_ref[0])
+
+        out_ref[0] = jnp.dot(
+            sets_ref[0], vectors[...], preferred_element_type=jnp.float32
+        ).astype(out_ref.dtype)
+
+    return pl.pallas_call(
+        kernel,
         grid=(points - 1,),
-        in_specs=[ORDER, SMEM, SMEM, pl.BlockSpec((1, rows, kept), lambda i: (i + 1, skip, 0))]
-        + [own_spec] * (1 + len(others)),
+        in_specs=[ORDER, SMEM, pl.BlockSpec((1, rows, kept), lambda i: (i + 1, skip, 0))]
+        + [VMEM] * (len(sizes) * blocks),
         out_specs=pl.BlockSpec((1, rows, width), lambda i: (i, 0, 0)),
         out_shape=jax.ShapeDtypeStruct((points - 1, rows, width), jnp.bfloat16),
         scratch_shapes=[pltpu.VMEM((kept, width), jnp.bfloat16)],
         compiler_params=params(),
         cost_estimate=CHEAP,
         name="apply_rest",
-    )(earlier, counts, me, sets, own, *others)
-
-
-def combine(sets, own, others, counts, me, kin, length, block, tail):
+    )(earlier, facts, sets, *sum(pieces, []))
+
+
+def combine(sets, pieces, facts, kin, length, block, tail):
     points, _, kept = sets.shape
-    share, width = own.shape[1:]
+    width = pieces[0][0].shape[2]
+    sizes = parcels(points)
     steps = length // block
     body = steps - tail // block
-    peers = len(others)
-
-    def kernel(counts_ref, me_ref, kin_ref, sets_ref, own_ref, *refs):
-        other_refs, outs, vectors = refs[:peers], refs[peers:-1], refs[-1]
+    blocks = len(pieces[0])
+
+    def kernel(facts_ref, kin_ref, sets_ref, *refs):
+        used = len(sizes) * blocks
+        piece_refs = refs[:used]
+        outs, vectors = refs[used:-1], refs[-1]
         i = pl.program_id(0)
 
         @pl.when(i == 0)
         def _():
             for j in range(points):
-                pieces = [r[j] for r in (own_ref, *other_refs)]
-                fill(vectors.at[j], pieces, counts_ref[j], me_ref[0])
+                index, row = place(j, sizes)
+                mine = piece_refs[index * blocks :][:blocks]
+                fill(vectors.at[j], [r[row] for r in mine], facts_ref[1 + j], facts_ref[0])
 
         products = [
             jnp.dot(sets_ref[j], vectors[j], preferred_element_type=jnp.float32)
@@ -147,8 +191,8 @@
     return pl.pallas_call(
         kernel,
         grid=(steps,),
-        in_specs=[SMEM, SMEM, SMEM, pl.BlockSpec((points, block, kept), lambda i: (0, i, 0))]
-        + [VMEM] * (1 + peers),
+        in_specs=[SMEM, SMEM, pl.BlockSpec((points, block, kept), lambda i: (0, i, 0))]
+        + [VMEM] * (len(sizes) * blocks),
         out_specs=[whole] * (points - 1)
         + [
             pl.BlockSpec((block, width), lambda i: (jnp.minimum(i, body - 1), 0)),
@@ -163,7 +207,7 @@
         compiler_params=params(),
         cost_estimate=CHEAP,
         name="combine",
-    )(counts, me, kin, sets, own, *others)
+    )(facts, kin, sets, *sum(pieces, []))
 
 
 def collect(sets, first, rest, kin, start, rows):
@@ -192,13 +236,13 @@
     )(kin, sets, first, rest)
 
 
-def split_blocks(total, point, counts_ref, owner_ref, me, held, own_ref, send_ref):
-    blocks = owner_ref.shape[0]
+def split_blocks(total, point, points, facts_ref, held, own_ref, send_ref):
+    blocks = facts_ref.shape[0] - 1 - points
     share = own_ref.shape[0]
     row = lax.broadcasted_iota(jnp.int32, total.shape, 0)
-    held[...] = jnp.where(row < counts_ref[point], total, 0.0)
+    held[...] = jnp.where(row < facts_ref[1 + point], total, 0.0)
     for d in range(blocks):
-        start = pl.multiple_of(owner_ref[lax.rem(me + d, blocks)] * share, 16)
+        start = pl.multiple_of(facts_ref[1 + points + lax.rem(facts_ref[0] + d, blocks)] * share, 16)
         part = held[pl.ds(start, share), :]
         if d == 0:
             own_ref[...] = part
@@ -234,13 +278,13 @@
     )(earlier, sets, arrived, before)
 
 
-def finish_rows(sets, arrived, before, earlier, counts, me, owner_map, point, block, share):
-    kept = sets.shape[2]
+def finish_rows(sets, arrived, before, earlier, facts, point, block, share):
+    points, _, kept = sets.shape
     length, width = arrived.shape
     steps = length // block
-    blocks = owner_map.shape[0]
-
-    def kernel(_, counts_ref, me_ref, owner_ref, sets_ref, arrived_ref, before_ref, own_ref, send_ref, total, held):
+    blocks = facts.shape[0] - 1 - points
+
+    def kernel(_, facts_ref, sets_ref, arrived_ref, before_ref, own_ref, send_ref, total, held):
         i = pl.program_id(0)
 
         @pl.when(i == 0)
@@ -251,7 +295,7 @@
 
         @pl.when(i == steps - 1)
         def _():
-            split_blocks(total[...], point, counts_ref, owner_ref, me_ref[0], held, own_ref, send_ref)
+            split_blocks(total[...], point, points, facts_ref, held, own_ref, send_ref)
 
     return pl.pallas_call(
         kernel,
@@ -259,8 +303,6 @@
         in_specs=[
             ORDER,
             SMEM,
-            SMEM,
-            SMEM,
             pl.BlockSpec((1, block, kept), lambda i: (point, i, 0)),
             pl.BlockSpec((block, width), lambda i: (i, 0)),
             pl.BlockSpec((1, kept, width), lambda i: (point, 0, 0)),
@@ -277,21 +319,21 @@
         compiler_params=params(),
         cost_estimate=CHEAP,
         name="finish_rows",
-    )(earlier, counts, me, owner_map, sets, arrived, before)
-
-
-def finish_last(sets, arrived, before, earlier, counts, me, owner_map, point, share):
+    )(earlier, facts, sets, arrived, before)
+
+
+def finish_last(sets, arrived, before, earlier, facts, point, points, share):
     kept = sets.shape[1]
     width = arrived.shape[1]
-    blocks = owner_map.shape[0]
-
-    def kernel(_, counts_ref, me_ref, owner_ref, sets_ref, arrived_ref, before_ref, own_ref, send_ref, held):
+    blocks = facts.shape[0] - 1 - points
+
+    def kernel(_, facts_ref, sets_ref, arrived_ref, before_ref, own_ref, send_ref, held):
         total = before_ref[...] + contract_rows(sets_ref[...], arrived_ref[...])
-        split_blocks(total, point, counts_ref, owner_ref, me_ref[0], held, own_ref, send_ref)
-
-    return pl.pallas_call(
-        kernel,
-        in_specs=[ORDER] + [SMEM] * 3 + [VMEM] * 3,
+        split_blocks(total, point, points, facts_ref, held, own_ref, send_ref)
+
+    return pl.pallas_call(
+        kernel,
+        in_specs=[ORDER, SMEM] + [VMEM] * 3,
         out_specs=[VMEM, VMEM],
         out_shape=[
             jax.ShapeDtypeStruct((share, width), jnp.float32),
@@ -301,7 +343,7 @@
         compiler_params=params(),
         cost_estimate=CHEAP,
         name="finish_last",
-    )(earlier, counts, me, owner_map, sets, arrived, before)
+    )(earlier, facts, sets, arrived, before)
 
 
 def place_last(ready, own, others):
@@ -338,27 +380,23 @@
     share, width = trial_vecs.shape[1:]
     blocks = owner_map.shape[0]
     me = lax.axis_index("rows").astype(jnp.int32).reshape(1)
+    facts = jnp.concatenate([me, counts, owner_map])
     unit = radial // 12
-    plain, tail = 4 * unit, unit
+    plain, tail = 4 * unit, 2 * unit
     mixed_rows = radial - plain
     peers = range(1, blocks)
 
-    first_own = trial_vecs[:1]
-    first_vectors = [shifted(first_own, "rows", d) for d in peers]
-    vectors = [shifted(trial_vecs, "rows", d) for d in peers]
-
-    first = apply_first(coeffs, first_own, first_vectors, counts, me, mixed_rows, plain)
+    pieces = [[v] + [shifted(v, "rows", d) for d in peers] for v in parted(trial_vecs)]
+    first = apply_first(coeffs, pieces[0], facts, mixed_rows, plain)
     first_sent = shifted(first, "blk", 1)
 
     table_index = jnp.arange(kinetic.shape[0], dtype=jnp.int32)
     one_hot = pair_table[:, :, None] == table_index[None, None, :]
     kin_own = jnp.sum(jnp.where(one_hot, kinetic[None, None, :], 0.0), axis=2)
-    rest = apply_rest(coeffs, trial_vecs, vectors, first, counts, me, mixed_rows, plain)
+    rest = apply_rest(coeffs, pieces, first, facts, mixed_rows, plain)
     rest_sent = shifted(rest, "blk", 1)
     kin_next = shifted(after(kin_own, rest, first_sent), "blk", -1)
-    mixed = combine(
-        coeffs, trial_vecs, vectors, counts, me, kin_next, mixed_rows, unit, tail
-    )
+    mixed = combine(coeffs, pieces, facts, kin_next, mixed_rows, tail, tail)
     mixed_sent = []
     previous = rest
     for z in mixed:
@@ -371,7 +409,7 @@
     earlier = first_sent
     for a in range(points - 1):
         own, send = finish_rows(
-            coeffs, mixed_sent[a], base, earlier, counts, me, owner_map, a, mixed_rows // 2, share
+            coeffs, mixed_sent[a], base, earlier, facts, a, mixed_rows // 2, share
         )
         earlier = own
         done.append(exchange(own, send))
@@ -379,7 +417,7 @@
     total = gather_rows(coeffs, mixed_sent[last], base, earlier, last, mixed_rows - tail)
     ready = jnp.stack(done + done[:1]).astype(jnp.bfloat16)
     own, send = finish_last(
-        coeffs[last, mixed_rows - tail : mixed_rows], mixed_sent[points], total, ready, counts, me, owner_map, last, share
+        coeffs[last, mixed_rows - tail : mixed_rows], mixed_sent[points], total, ready, facts, last, points, share
     )
     return place_last(ready, own, [shifted(send[d - 1], "rows", d) for d in peers])
 

time: 93 us -> 87.8 us (0.944)
  waiting for transfers between devices: 41.1 us -> 33.7 us
  starting transfers between devices: 13.7 us -> 17.3 us
  Pallas kernels: 34.8 us -> 33.1 us
    ppermute x14, waiting for transfers between devices: 41.1 us -> 33.7 us  [shifted(): return lax.ppermute(block, axis, route)]
    ppermute x14, starting transfers between devices: 13.7 us -> 17.3 us  [shifted(): return lax.ppermute(block, axis, route)]
    pallas_call x7 -> x8, Pallas kernels: 25.4 us -> 24 us  [the longest x1 8.66 us: combine(): pl.pallas_call(kernel, grid=(steps,), in_specs=[SMEM, SMEM, pl.BlockSpec(...]
  transfers between devices with their start and end apart: 14 -> 14, of which waited for: 9 -> 11; matrix products, arithmetic and copies ran while one was open for 2% -> 2% of each run, Pallas kernels for 36% -> 36%
where the time goes in v3:
time: 87.8 us; the launch traced here: 87.5 us
  waiting for transfers between devices  33.7 us (38%)
  Pallas kernels  33.1 us (38%)
  starting transfers between devices  17.3 us (20%)
  local copies, waits for them, and re-layouts  2.15 us (2%)
  other arithmetic  0.97 us (1%)
    ppermute x14, waiting for transfers between devices, shifted(): return lax.ppermute(block, axis, route)  33.7 us
    ppermute x14, starting transfers between devices, shifted(): return lax.ppermute(block, axis, route)  17.3 us
    pallas_call x1, Pallas kernels, combine(): pl.pallas_call(kernel, grid=(steps,), in_specs=[SMEM, SMEM, pl.BlockSpec(...  8.66 us
    pallas_call x3, Pallas kernels, finish_rows(): pl.pallas_call(kernel, grid=(steps,), in_specs=[ORDER, SMEM, pl.BlockSpec...  8.26 us
    pallas_call x1, Pallas kernels, collect(): pl.pallas_call(kernel, grid=(points,), in_specs=[SMEM, pl.BlockSpec((1, r...  6.04 us
    pallas_call x1, Pallas kernels, apply_rest(): pl.pallas_call(kernel, grid=(points - 1,), in_specs=[ORDER, SMEM, pl.Bloc...  4.1 us
    pallas_call x1, Pallas kernels, gather_rows(): pl.pallas_call(kernel, grid=(length // block,), in_specs=[ORDER, pl.Block...  2.48 us
    pallas_call x1, Pallas kernels, apply_first(): pl.pallas_call(kernel, grid=(2,), in_specs=[SMEM, pl.BlockSpec((1, block,...  1.97 us
  transfers between devices with their start and end apart: 14, of which 11 were waited for; matrix products, arithmetic and copies ran while one was open for 2% of the time, Pallas kernels for 36%

profile of v3, /device:TPU:0, one launch (start us, length us, event | category | flops | bytes accessed | tf_op | source)
XLA Modules:
  0.0 87.5 jit_solution(17680283603258692166)
XLA Ops:
  0.0 0.0 copy-start.1
  0.0 0.9 %copy-done.1 = bf16[4,192,128]{2,1,0:T(8,128)(2,1)S(1)} copy-done((bf16[4,192,128]{2,1,0:T(8,128)(2,1)S(1)}, bf16[4,192,128]{2,1,0:T(8,128)(2,1)}, u32[]{:S(2)}) %copy-start.1) | copy-done | bytes 196632
  0.9 3.0 %collective-permute-start = (bf16[1,192,128]{2,1,0:T(8,128)(2,1)S(1)}, bf16[1,192,128]{2,1,0:T(8,128)(2,1)S(1)}, u32[]{:S(2)}, u32[]{:S(2)}) collective-permute-start(bf16[1,192,128]{2,1,0:T(8,128)(2,1)S(1)} %get-tuple-element.26.rest_0_.refs_0_), channel_id=1, source_target_pairs={{0,1},{1,0},{2,3},{3,2},{4,5},{5,4},{6,7},{7,6},{8,9},{9,8},{10,11... | collective-permute-start | bytes 147464 | tf_op jit(solution)/shard_map/ppermute | solution.py:20
  3.9 0.1 collective-permute-start.2
  4.0 0.7 pad_add_fusion.facts_ref
  4.8 0.0 copy-start.2
  4.8 1.3 %collective-permute-done.rest_1_.refs_1_ = bf16[1,192,128]{2,1,0:T(8,128)(2,1)S(1)} collective-permute-done((bf16[1,192,128]{2,1,0:T(8,128)(2,1)S(1)}, bf16[1,192,128]{2,1,0:T(8,128)(2,1)S(1)}, u32[]{:S(2)}, u32[]{:S(2)}) %collective-permute-start) | collective-permute-done | bytes 49184 | tf_op jit(solution)/shard_map/ppermute | solution.py:20
  6.1 2.0 %apply_first.1._ = bf16[1,2048,128]{2,1,0:T(8,128)(2,1)S(1)} custom-call(s32[7]{0:T(128)S(1)} %pad_add_fusion.facts_ref, bf16[4,6144,384]{2,1,0:T(8,128)(2,1)} %sets_ref.15, bf16[1,192,128]{2,1,0:T(8,128)(2,1)S(1)} %get-tuple-element.26.rest_0_.refs_0_, bf16[1,192,128]{2,1,0:T(8,128)(2,1)S(1)} %collective-permute-done.rest_1_.refs_1_), custom_call_target="tpu_custom_call" | custom-call | flops 1000000000 | bytes 1000000 | tf_op jit(solution)/shard_map/apply_first/pallas_call | solution.py:97
  8.1 0.1 collective-permute-start.1
  8.1 1.1 %collective-permute-done.2.rest_3_.refs_3_ = bf16[3,192,128]{2,1,0:T(8,128)(2,1)S(1)} collective-permute-done((bf16[3,192,128]{2,1,0:T(8,128)(2,1)S(1)}, bf16[3,192,128]{2,1,0:T(8,128)(2,1)S(1)}, u32[]{:S(2)}, u32[]{:S(2)}) %collective-permute-start.2) | collective-permute-done | bytes 147488 | tf_op jit(solution)/shard_map/ppermute | solution.py:20
  9.3 4.1 %apply_rest.1 = bf16[3,2048,128]{2,1,0:T(8,128)(2,1)S(1)} custom-call(bf16[1,2048,128]{2,1,0:T(8,128)(2,1)S(1)} %apply_first.1._, s32[7]{0:T(128)S(1)} %pad_add_fusion.facts_ref, bf16[4,6144,384]{2,1,0:T(8,128)(2,1)} %sets_ref.15, bf16[1,192,128]{2,1,0:T(8,128)(2,1)S(1)} %get-tuple-element.26.rest_0_.refs_0_, ...), custom_call_target="tpu_custom_call" | custom-call | flops 1 | bytes 1 | tf_op jit(solution)/shard_map/apply_rest/pallas_call | solution.py:132
  13.4 1.5 %collective-permute-start.5 = (bf16[3,2048,128]{2,1,0:T(8,128)(2,1)S(1)}, bf16[3,2048,128]{2,1,0:T(8,128)(2,1)S(1)}, u32[]{:S(2)}, u32[]{:S(2)}) collective-permute-start(bf16[3,2048,128]{2,1,0:T(8,128)(2,1)S(1)} %apply_rest.1), channel_id=1, source_target_pairs={{0,2},{2,4},{4,6},{6,8},{8,10},{10,12},{12,14},{14,16},{16,18},{18... | collective-permute-start | bytes 4718600 | tf_op jit(solution)/shard_map/ppermute | solution.py:20
  14.8 0.0 copy-done.2
  14.8 0.0 copy-done.3
  14.8 0.2 select_reduce_fusion.kin_ref
  15.0 4.4 %collective-permute-done.1.first_ref._ = bf16[1,2048,128]{2,1,0:T(8,128)(2,1)S(1)} collective-permute-done((bf16[1,2048,128]{2,1,0:T(8,128)(2,1)S(1)}, bf16[1,2048,128]{2,1,0:T(8,128)(2,1)S(1)}, u32[]{:S(2)}, u32[]{:S(2)}) %collective-permute-start.1) | collective-permute-done | bytes 524320 | tf_op jit(solution)/shard_map/ppermute | solution.py:20
  19.4 0.0 collective-permute-start.3
  19.4 1.3 %collective-permute-done.3.kin_ref = f32[4,4]{1,0:T(4,128)S(1)} collective-permute-done((f32[4,4]{1,0:T(4,128)S(1)}, f32[4,4]{1,0:T(4,128)S(1)}, u32[]{:S(2)}, u32[]{:S(2)}) %collective-permute-start.3) | collective-permute-done | bytes 96 | tf_op jit(solution)/shard_map/ppermute | solution.py:20
  20.7 8.7 %combine.1 = (bf16[4096,128]{1,0:T(8,128)(2,1)S(1)}, bf16[4096,128]{1,0:T(8,128)(2,1)S(1)}, bf16[4096,128]{1,0:T(8,128)(2,1)}, bf16[3072,128]{1,0:T(8,128)(2,1)S(1)}, bf16[1024,128]{1,0:T(8,128)(2,1)S(1)}) custom-call(s32[7]{0:T(128)S(1)} %pad_add_fusion.facts_ref, f32[4,4]{1,0:T(4,128)S(1)} %collective-permute-done.3.kin_ref, ...), custom_call_target="tpu_custom_call" | custom-call | flops 1 | bytes 1 | tf_op jit(solution)/shard_map/combine/pallas_call | solution.py:191
  29.4 0.3 collective-permute-start.4
  29.7 0.0 collective-permute-start.7
  29.7 2.1 %collective-permute-start.9 = (bf16[4096,128]{1,0:T(8,128)(2,1)}, bf16[4096,128]{1,0:T(8,128)(2,1)S(1)}, u32[]{:S(2)}, u32[]{:S(2)}) collective-permute-start(bf16[4096,128]{1,0:T(8,128)(2,1)} %get-tuple-element.38), channel_id=1, source_target_pairs={{0,2},{2,4},{4,6},{6,8},{8,10},{10,12},{12,14},{14,16},{16,18},{18... | collective-permute-start | bytes 3145736 | tf_op jit(solution)/shard_map/ppermute | solution.py:20
  31.8 0.0 collective-permute-start.12
  31.9 4.4 %collective-permute-done.5.rest_ref = bf16[3,2048,128]{2,1,0:T(8,128)(2,1)S(1)} collective-permute-done((bf16[3,2048,128]{2,1,0:T(8,128)(2,1)S(1)}, bf16[3,2048,128]{2,1,0:T(8,128)(2,1)S(1)}, u32[]{:S(2)}, u32[]{:S(2)}) %collective-permute-start.5) | collective-permute-done | bytes 1572896 | tf_op jit(solution)/shard_map/ppermute | solution.py:20
  36.3 6.0 %collect.1.before_ref = f32[4,384,128]{2,1,0:T(8,128)S(1)} custom-call(f32[4,4]{1,0:T(4,128)S(1)} %select_reduce_fusion.kin_ref, bf16[4,6144,384]{2,1,0:T(8,128)(2,1)} %sets_ref.15, bf16[1,2048,128]{2,1,0:T(8,128)(2,1)S(1)} %collective-permute-done.1.first_ref._, bf16[3,2048,128]{2,1,0:T(8,128)(2,1)S(1)} %collective-permute-done.5.rest_ref), custom_call_target="tpu_custom_call" | custom-call | flops 1 | bytes 1 | tf_op jit(solution)/shard_map/collect/pallas_call | solution.py:227
  42.3 5.2 %collective-permute-done.4.arrived_ref = bf16[4096,128]{1,0:T(8,128)(2,1)S(1)} collective-permute-done((bf16[4096,128]{1,0:T(8,128)(2,1)S(1)}, bf16[4096,128]{1,0:T(8,128)(2,1)S(1)}, u32[]{:S(2)}, u32[]{:S(2)}) %collective-permute-start.4) | collective-permute-done | bytes 1048608 | tf_op jit(solution)/shard_map/ppermute | solution.py:20
  47.5 2.8 %finish_rows.3 = (f32[192,128]{1,0:T(8,128)S(1)}, bf16[1,192,128]{2,1,0:T(8,128)(2,1)S(1)}) custom-call(bf16[1,2048,128]{2,1,0:T(8,128)(2,1)S(1)} %collective-permute-done.1.first_ref._, s32[7]{0:T(128)S(1)} %pad_add_fusion.facts_ref, bf16[4,6144,384]{2,1,0:T(8,128)(2,1)} %sets_ref.15, bf16[4096,128]{1,0:T(8,128)(2,1)S(1)} %collective-permute-done.4.arrived_ref, ...), custom_call_target="tpu_custom_call" | custom-call | flops 1 | bytes 1 | tf_op jit(solution)/shard_map/finish_rows/pallas_call | solution.py:300
  50.3 2.5 %collective-permute-start.6 = (bf16[192,128]{1,0:T(8,128)(2,1)S(1)}, bf16[192,128]{1,0:T(8,128)(2,1)S(1)}, u32[]{:S(2)}, u32[]{:S(2)}) collective-permute-start(bf16[192,128]{1,0:T(8,128)(2,1)S(1)} %bitcast.13), channel_id=1, source_target_pairs={{0,1},{1,0},{2,3},{3,2},{4,5},{5,4},{6,7},{7,6},{8,9},{9,8},{10,11... | collective-permute-start | bytes 147464 | tf_op jit(solution)/shard_map/ppermute | solution.py:20
  52.8 1.2 %slice_bitcast_fusion.sets_ref = bf16[1024,384]{1,0:T(8,128)(2,1)S(1)} fusion(bf16[4,6144,384]{2,1,0:T(8,128)(2,1)} %sets_ref.15), kind=kLoop, calls=%fused_computation | loop fusion | bytes 1572864 | tf_op jit(solution)/shard_map/squeeze | solution.py:420
  54.1 0.1 collective-permute-start.11
  54.1 4.6 %collective-permute-done.7.arrived_ref = bf16[4096,128]{1,0:T(8,128)(2,1)S(1)} collective-permute-done((bf16[4096,128]{1,0:T(8,128)(2,1)S(1)}, bf16[4096,128]{1,0:T(8,128)(2,1)S(1)}, u32[]{:S(2)}, u32[]{:S(2)}) %collective-permute-start.7) | collective-permute-done | bytes 1048608 | tf_op jit(solution)/shard_map/ppermute | solution.py:20
  58.8 2.8 %finish_rows.4 = (f32[192,128]{1,0:T(8,128)S(1)}, bf16[1,192,128]{2,1,0:T(8,128)(2,1)S(1)}) custom-call(f32[192,128]{1,0:T(8,128)S(1)} %get-tuple-element.31._, s32[7]{0:T(128)S(1)} %pad_add_fusion.facts_ref, bf16[4,6144,384]{2,1,0:T(8,128)(2,1)} %sets_ref.15, bf16[4096,128]{1,0:T(8,128)(2,1)S(1)} %collective-permute-done.7.arrived_ref, ...), custom_call_target="tpu_custom_call" | custom-call | flops 1 | bytes 1 | tf_op jit(solution)/shard_map/finish_rows/pallas_call | solution.py:300
  61.5 2.5 %collective-permute-start.8 = (bf16[192,128]{1,0:T(8,128)(2,1)S(1)}, bf16[192,128]{1,0:T(8,128)(2,1)S(1)}, u32[]{:S(2)}, u32[]{:S(2)}) collective-permute-start(bf16[192,128]{1,0:T(8,128)(2,1)S(1)} %bitcast.14), channel_id=1, source_target_pairs={{0,1},{1,0},{2,3},{3,2},{4,5},{5,4},{6,7},{7,6},{8,9},{9,8},{10,11... | collective-permute-start | bytes 147464 | tf_op jit(solution)/shard_map/ppermute | solution.py:20
  64.1 5.9 %collective-permute-done.9.arrived_ref = bf16[4096,128]{1,0:T(8,128)(2,1)S(1)} collective-permute-done((bf16[4096,128]{1,0:T(8,128)(2,1)}, bf16[4096,128]{1,0:T(8,128)(2,1)S(1)}, u32[]{:S(2)}, u32[]{:S(2)}) %collective-permute-start.9) | collective-permute-done | bytes 1048608 | tf_op jit(solution)/shard_map/ppermute | solution.py:20
  70.0 2.8 %finish_rows.5 = (f32[192,128]{1,0:T(8,128)S(1)}, bf16[1,192,128]{2,1,0:T(8,128)(2,1)S(1)}) custom-call(f32[192,128]{1,0:T(8,128)S(1)} %get-tuple-element.35._, s32[7]{0:T(128)S(1)} %pad_add_fusion.facts_ref, bf16[4,6144,384]{2,1,0:T(8,128)(2,1)} %sets_ref.15, bf16[4096,128]{1,0:T(8,128)(2,1)S(1)} %collective-permute-done.9.arrived_ref, ...), custom_call_target="tpu_custom_call" | custom-call | flops 1 | bytes 1 | tf_op jit(solution)/shard_map/finish_rows/pallas_call | solution.py:300
  72.8 2.5 %collective-permute-start.10 = (bf16[192,128]{1,0:T(8,128)(2,1)S(1)}, bf16[192,128]{1,0:T(8,128)(2,1)S(1)}, u32[]{:S(2)}, u32[]{:S(2)}) collective-permute-start(bf16[192,128]{1,0:T(8,128)(2,1)S(1)} %bitcast.15), channel_id=1, source_target_pairs={{0,1},{1,0},{2,3},{3,2},{4,5},{5,4},{6,7},{7,6},{8,9},{9,8},{10,11... | collective-permute-start | bytes 147464 | tf_op jit(solution)/shard_map/ppermute | solution.py:20
  75.3 3.1 %collective-permute-done.12.arrived_ref = bf16[3072,128]{1,0:T(8,128)(2,1)S(1)} collective-permute-done((bf16[3072,128]{1,0:T(8,128)(2,1)S(1)}, bf16[3072,128]{1,0:T(8,128)(2,1)S(1)}, u32[]{:S(2)}, u32[]{:S(2)}) %collective-permute-start.12) | collective-permute-done | bytes 786464 | tf_op jit(solution)/shard_map/ppermute | solution.py:20
  78.4 2.5 %gather_rows.1.before_ref = f32[384,128]{1,0:T(8,128)S(1)} custom-call(f32[192,128]{1,0:T(8,128)S(1)} %get-tuple-element.39._, bf16[4,6144,384]{2,1,0:T(8,128)(2,1)} %sets_ref.15, bf16[3072,128]{1,0:T(8,128)(2,1)S(1)} %collective-permute-done.12.arrived_ref, f32[4,384,128]{2,1,0:T(8,128)S(1)} %collect.1.before_ref), custom_call_target="tpu_custom_call" | custom-call | flops 1 | bytes 1 | tf_op jit(solution)/shard_map/gather_rows/pallas_call | solution.py:264
  80.9 0.0 collective-permute-done.6
  81.0 0.0 collective-permute-done.8
  81.0 0.0 collective-permute-done.10
  81.1 0.0 copy-start
  81.1 0.2 collective-permute-done.11.arrived_ref
  81.2 1.0 %finish_last.1 = (f32[192,128]{1,0:T(8,128)S(1)}, bf16[1,192,128]{2,1,0:T(8,128)(2,1)S(1)}) custom-call(bf16[4,192,128]{2,1,0:T(8,128)(2,1)S(1)} %pad_maximum_fusion._, s32[7]{0:T(128)S(1)} %pad_add_fusion.facts_ref, bf16[1024,384]{1,0:T(8,128)(2,1)S(1)} %slice_bitcast_fusion.sets_ref, bf16[1024,128]{1,0:T(8,128)(2,1)S(1)} %collective-permute-done.11.arrived_ref, ...), custom_call_target="tpu_custom_call" | custom-call | flops 1 | bytes 1 | tf_op jit(solution)/shard_map/finish_last/pallas_call | solution.py:334
  82.2 2.5 %collective-permute-start.13 = (bf16[192,128]{1,0:T(8,128)(2,1)S(1)}, bf16[192,128]{1,0:T(8,128)(2,1)S(1)}, u32[]{:S(2)}, u32[]{:S(2)}) collective-permute-start(bf16[192,128]{1,0:T(8,128)(2,1)S(1)} %bitcast.16), channel_id=1, source_target_pairs={{0,1},{1,0},{2,3},{3,2},{4,5},{5,4},{6,7},{7,6},{8,9},{9,8},{10,11... | collective-permute-start | bytes 147464 | tf_op jit(solution)/shard_map/ppermute | solution.py:20
  84.8 2.1 %collective-permute-done.13.rest_0_ = bf16[192,128]{1,0:T(8,128)(2,1)S(1)} collective-permute-done((bf16[192,128]{1,0:T(8,128)(2,1)S(1)}, bf16[192,128]{1,0:T(8,128)(2,1)S(1)}, u32[]{:S(2)}, u32[]{:S(2)}) %collective-permute-start.13) | collective-permute-done | bytes 49184 | tf_op jit(solution)/shard_map/ppermute | solution.py:20
  86.8 0.0 copy-done
  86.8 0.6 place_last.1
  (6 shorter events, 0.1 us)
Async XLA Ops:
  0.0 0.9 %copy-start.1 = (bf16[4,192,128]{2,1,0:T(8,128)(2,1)S(1)}, bf16[4,192,128]{2,1,0:T(8,128)(2,1)}, u32[]{:S(2)}) copy-start(bf16[4,192,128]{2,1,0:T(8,128)(2,1)} %vectors_ref.1) | copy-start | bytes 589828
  0.9 5.2 %collective-permute-start = (bf16[1,192,128]{2,1,0:T(8,128)(2,1)S(1)}, bf16[1,192,128]{2,1,0:T(8,128)(2,1)S(1)}, u32[]{:S(2)}, u32[]{:S(2)}) collective-permute-start(bf16[1,192,128]{2,1,0:T(8,128)(2,1)S(1)} %get-tuple-element.26.rest_0_.refs_0_), channel_id=1, source_target_pairs={{0,1},{1,0},{2,3},{3,2},{4,5},{5,4},{6,7},{7,6},{8,9},{9,8},{10,11... | collective-permute-start | bytes 147464 | tf_op jit(solution)/shard_map/ppermute | solution.py:20
  3.9 5.3 %collective-permute-start.2 = (bf16[3,192,128]{2,1,0:T(8,128)(2,1)S(1)}, bf16[3,192,128]{2,1,0:T(8,128)(2,1)S(1)}, u32[]{:S(2)}, u32[]{:S(2)}) collective-permute-start(bf16[3,192,128]{2,1,0:T(8,128)(2,1)S(1)} %get-tuple-element.27.rest_2_.refs_2_), channel_id=1, source_target_pairs={{0,1},{1,0},{2,3},{3,2},{4,5},{5,4},{6,7},{7,6},{8,9},{9,8},{10,11... | collective-permute-start | bytes 442376 | tf_op jit(solution)/shard_map/ppermute | solution.py:20
  4.8 10.1 %copy-start.2 = (s32[4,4]{1,0:T(4,128)S(1)}, s32[4,4]{1,0:T(4,128)}, u32[]{:S(2)}) copy-start(s32[4,4]{1,0:T(4,128)} %param.9) | copy-start | bytes 196
  4.8 10.1 %copy-start.3 = (f32[64]{0:T(128)S(1)}, f32[64]{0:T(128)}, u32[]{:S(2)}) copy-start(f32[64]{0:T(128)} %param.8) | copy-start | bytes 772
  8.1 11.4 %collective-permute-start.1 = (bf16[1,2048,128]{2,1,0:T(8,128)(2,1)S(1)}, bf16[1,2048,128]{2,1,0:T(8,128)(2,1)S(1)}, u32[]{:S(2)}, u32[]{:S(2)}) collective-permute-start(bf16[1,2048,128]{2,1,0:T(8,128)(2,1)S(1)} %apply_first.1._), channel_id=1, source_target_pairs={{0,2},{2,4},{4,6},{6,8},{8,10},{10,12},{12,14},{14,16},{16,18},{18... | collective-permute-start | bytes 1572872 | tf_op jit(solution)/shard_map/ppermute | solution.py:20
  13.4 22.9 %collective-permute-start.5 = (bf16[3,2048,128]{2,1,0:T(8,128)(2,1)S(1)}, bf16[3,2048,128]{2,1,0:T(8,128)(2,1)S(1)}, u32[]{:S(2)}, u32[]{:S(2)}) collective-permute-start(bf16[3,2048,128]{2,1,0:T(8,128)(2,1)S(1)} %apply_rest.1), channel_id=1, source_target_pairs={{0,2},{2,4},{4,6},{6,8},{8,10},{10,12},{12,14},{14,16},{16,18},{18... | collective-permute-start | bytes 4718600 | tf_op jit(solution)/shard_map/ppermute | solution.py:20
  19.4 1.3 %collective-permute-start.3 = (f32[4,4]{1,0:T(4,128)S(1)}, f32[4,4]{1,0:T(4,128)S(1)}, u32[]{:S(2)}, u32[]{:S(2)}) collective-permute-start(f32[4,4]{1,0:T(4,128)S(1)} %select_reduce_fusion.kin_ref), channel_id=1, source_target_pairs={{0,30},{2,0},{4,2},{6,4},{8,6},{10,8},{12,10},{14,12},{16,14},{18,... | collective-permute-start | bytes 200 | tf_op jit(solution)/shard_map/ppermute | solution.py:20
  29.4 18.1 %collective-permute-start.4 = (bf16[4096,128]{1,0:T(8,128)(2,1)S(1)}, bf16[4096,128]{1,0:T(8,128)(2,1)S(1)}, u32[]{:S(2)}, u32[]{:S(2)}) collective-permute-start(bf16[4096,128]{1,0:T(8,128)(2,1)S(1)} %get-tuple-element.30), channel_id=1, source_target_pairs={{0,2},{2,4},{4,6},{6,8},{8,10},{10,12},{12,14},{14,16},{16,18},{18... | collective-permute-start | bytes 3145736 | tf_op jit(solution)/shard_map/ppermute | solution.py:20
  29.7 29.1 %collective-permute-start.7 = (bf16[4096,128]{1,0:T(8,128)(2,1)S(1)}, bf16[4096,128]{1,0:T(8,128)(2,1)S(1)}, u32[]{:S(2)}, u32[]{:S(2)}) collective-permute-start(bf16[4096,128]{1,0:T(8,128)(2,1)S(1)} %get-tuple-element.34), channel_id=1, source_target_pairs={{0,2},{2,4},{4,6},{6,8},{8,10},{10,12},{12,14},{14,16},{16,18},{18... | collective-permute-start | bytes 3145736 | tf_op jit(solution)/shard_map/ppermute | solution.py:20
  29.7 40.3 %collective-permute-start.9 = (bf16[4096,128]{1,0:T(8,128)(2,1)}, bf16[4096,128]{1,0:T(8,128)(2,1)S(1)}, u32[]{:S(2)}, u32[]{:S(2)}) collective-permute-start(bf16[4096,128]{1,0:T(8,128)(2,1)} %get-tuple-element.38), channel_id=1, source_target_pairs={{0,2},{2,4},{4,6},{6,8},{8,10},{10,12},{12,14},{14,16},{16,18},{18... | collective-permute-start | bytes 3145736 | tf_op jit(solution)/shard_map/ppermute | solution.py:20
  31.8 46.6 %collective-permute-start.12 = (bf16[3072,128]{1,0:T(8,128)(2,1)S(1)}, bf16[3072,128]{1,0:T(8,128)(2,1)S(1)}, u32[]{:S(2)}, u32[]{:S(2)}) collective-permute-start(bf16[3072,128]{1,0:T(8,128)(2,1)S(1)} %get-tuple-element.43), channel_id=1, source_target_pairs={{0,2},{2,4},{4,6},{6,8},{8,10},{10,12},{12,14},{14,16},{16,18},{18... | collective-permute-start | bytes 2359304 | tf_op jit(solution)/shard_map/ppermute | solution.py:20
  50.3 30.6 %collective-permute-start.6 = (bf16[192,128]{1,0:T(8,128)(2,1)S(1)}, bf16[192,128]{1,0:T(8,128)(2,1)S(1)}, u32[]{:S(2)}, u32[]{:S(2)}) collective-permute-start(bf16[192,128]{1,0:T(8,128)(2,1)S(1)} %bitcast.13), channel_id=1, source_target_pairs={{0,1},{1,0},{2,3},{3,2},{4,5},{5,4},{6,7},{7,6},{8,9},{9,8},{10,11... | collective-permute-start | bytes 147464 | tf_op jit(solution)/shard_map/ppermute | solution.py:20
  54.1 27.2 %collective-permute-start.11 = (bf16[1024,128]{1,0:T(8,128)(2,1)S(1)}, bf16[1024,128]{1,0:T(8,128)(2,1)S(1)}, u32[]{:S(2)}, u32[]{:S(2)}) collective-permute-start(bf16[1024,128]{1,0:T(8,128)(2,1)S(1)} %get-tuple-element.44), channel_id=1, source_target_pairs={{0,2},{2,4},{4,6},{6,8},{8,10},{10,12},{12,14},{14,16},{16,18},{18... | collective-permute-start | bytes 786440 | tf_op jit(solution)/shard_map/ppermute | solution.py:20
  61.5 19.4 %collective-permute-start.8 = (bf16[192,128]{1,0:T(8,128)(2,1)S(1)}, bf16[192,128]{1,0:T(8,128)(2,1)S(1)}, u32[]{:S(2)}, u32[]{:S(2)}) collective-permute-start(bf16[192,128]{1,0:T(8,128)(2,1)S(1)} %bitcast.14), channel_id=1, source_target_pairs={{0,1},{1,0},{2,3},{3,2},{4,5},{5,4},{6,7},{7,6},{8,9},{9,8},{10,11... | collective-permute-start | bytes 147464 | tf_op jit(solution)/shard_map/ppermute | solution.py:20
  72.8 8.2 %collective-permute-start.10 = (bf16[192,128]{1,0:T(8,128)(2,1)S(1)}, bf16[192,128]{1,0:T(8,128)(2,1)S(1)}, u32[]{:S(2)}, u32[]{:S(2)}) collective-permute-start(bf16[192,128]{1,0:T(8,128)(2,1)S(1)} %bitcast.15), channel_id=1, source_target_pairs={{0,1},{1,0},{2,3},{3,2},{4,5},{5,4},{6,7},{7,6},{8,9},{9,8},{10,11... | collective-permute-start | bytes 147464 | tf_op jit(solution)/shard_map/ppermute | solution.py:20
  81.1 5.8 %copy-start = (bf16[4,192,128]{2,1,0:T(8,128)(2,1)}, bf16[4,192,128]{2,1,0:T(8,128)(2,1)S(1)}, u32[]{:S(2)}) copy-start(bf16[4,192,128]{2,1,0:T(8,128)(2,1)S(1)} %pad_maximum_fusion._) | copy-start | bytes 589828
  82.2 4.6 %collective-permute-start.13 = (bf16[192,128]{1,0:T(8,128)(2,1)S(1)}, bf16[192,128]{1,0:T(8,128)(2,1)S(1)}, u32[]{:S(2)}, u32[]{:S(2)}) collective-permute-start(bf16[192,128]{1,0:T(8,128)(2,1)S(1)} %bitcast.16), channel_id=1, source_target_pairs={{0,1},{1,0},{2,3},{3,2},{4,5},{5,4},{6,7},{7,6},{8,9},{9,8},{10,11... | collective-permute-start | bytes 147464 | tf_op jit(solution)/shard_map/ppermute | solution.py:20

commit v4 on v3

--- a/solution.py
+++ b/solution.py
@@ -56,50 +56,62 @@
     raise ValueError(point)
 
 
-def parted(vectors):
-    points, share, width = vectors.shape
-    sizes = parcels(points)
-
-    def kernel(vectors_ref, *outs):
-        start = 0
-        for out, size in zip(outs, sizes):
-            out[...] = vectors_ref[start : start + size]
-            start += size
-
-    return pl.pallas_call(
-        kernel,
-        in_specs=[VMEM],
-        out_specs=[VMEM] * len(sizes),
-        out_shape=[jax.ShapeDtypeStruct((size, share, width), vectors.dtype) for size in sizes],
-        compiler_params=params(),
-        cost_estimate=CHEAP,
-        name="parted",
-    )(vectors)
-
-
-def apply_first(sets, pieces, facts, start, rows):
+def part_of(vectors, first, size, *earlier):
+    share, width = vectors.shape[1:]
+
+    def kernel(vectors_ref, *rest):
+        out_ref, sem = rest[-2:]
+        copy = pltpu.make_async_copy(vectors_ref.at[pl.ds(first, size)], out_ref, sem)
+        copy.start()
+        copy.wait()
+
+    return pl.pallas_call(
+        kernel,
+        in_specs=[ORDER] * (1 + len(earlier)),
+        out_specs=VMEM,
+        out_shape=jax.ShapeDtypeStruct((size, share, width), vectors.dtype),
+        scratch_shapes=[pltpu.SemaphoreType.DMA],
+        compiler_params=params(),
+        cost_estimate=CHEAP,
+        name="part_of",
+    )(vectors, *earlier)
+
+
+def fetch(sets, earlier, point, start, rows):
     kept = sets.shape[2]
+
+    def kernel(sets_ref, _, block_ref, sem):
+        copy = pltpu.make_async_copy(sets_ref.at[point, pl.ds(start, rows), :], block_ref, sem)
+        copy.start()
+        copy.wait()
+
+    return pl.pallas_call(
+        kernel,
+        in_specs=[ORDER, ORDER],
+        out_specs=VMEM,
+        out_shape=jax.ShapeDtypeStruct((rows, kept), sets.dtype),
+        scratch_shapes=[pltpu.SemaphoreType.DMA],
+        compiler_params=params(),
+        cost_estimate=CHEAP,
+        name="fetch",
+    )(sets, earlier)
+
+
+def apply_first(sets, pieces, facts):
+    rows, kept = sets.shape
     width = pieces[0].shape[2]
-    block = rows // 2
-    skip = start // block
 
     def kernel(facts_ref, sets_ref, *rest):
         *piece_refs, out_ref, vectors = rest
-
-        @pl.when(pl.program_id(0) == 0)
-        def _():
-            fill(vectors, [r[0] for r in piece_refs], facts_ref[1], facts_ref[0])
-
+        fill(vectors, [r[0] for r in piece_refs], facts_ref[1], facts_ref[0])
         out_ref[0] = jnp.dot(
-            sets_ref[0], vectors[...], preferred_element_type=jnp.float32
+            sets_ref[...], vectors[...], preferred_element_type=jnp.float32
         ).astype(out_ref.dtype)
 
     return pl.pallas_call(
         kernel,
-        grid=(2,),
-        in_specs=[SMEM, pl.BlockSpec((1, block, kept), lambda i: (0, skip + i, 0))]
-        + [VMEM] * len(pieces),
-        out_specs=pl.BlockSpec((1, block, width), lambda i: (0, i, 0)),
+        in_specs=[SMEM] + [VMEM] * (1 + len(pieces)),
+        out_specs=VMEM,
         out_shape=jax.ShapeDtypeStruct((1, rows, width), jnp.bfloat16),
         scratch_shapes=[pltpu.VMEM((kept, width), jnp.bfloat16)],
         compiler_params=params(),
@@ -108,39 +120,48 @@
     )(facts, sets, *pieces)
 
 
-def apply_rest(sets, pieces, earlier, facts, start, rows):
+def apply_rest(sets, second, pieces, facts, start):
     points, _, kept = sets.shape
+    rows = second.shape[0]
     width = pieces[0][0].shape[2]
     blocks = len(pieces[0])
-    skip = start // rows
     sizes = parcels(points)
 
-    def kernel(_, facts_ref, sets_ref, *rest):
-        *piece_refs, out_ref, vectors = rest
+    def kernel(facts_ref, sets_ref, second_ref, *rest):
+        *piece_refs, out_ref, vectors, held, sems = rest
+        copies = [
+            pltpu.make_async_copy(
+                sets_ref.at[j, pl.ds(start, rows), :], held.at[j - 2], sems.at[j - 2]
+            )
+            for j in range(2, points)
+        ]
+        for copy in copies:
+            copy.start()
         for j in range(1, points):
-
-            @pl.when(pl.program_id(0) == j - 1)
-            def _():
-                index, row = place(j, sizes)
-                mine = piece_refs[index * blocks :][:blocks]
-                fill(vectors, [r[row] for r in mine], facts_ref[1 + j], facts_ref[0])
-
-        out_ref[0] = jnp.dot(
-            sets_ref[0], vectors[...], preferred_element_type=jnp.float32
-        ).astype(out_ref.dtype)
-
-    return pl.pallas_call(
-        kernel,
-        grid=(points - 1,),
-        in_specs=[ORDER, SMEM, pl.BlockSpec((1, rows, kept), lambda i: (i + 1, skip, 0))]
-        + [VMEM] * (len(sizes) * blocks),
-        out_specs=pl.BlockSpec((1, rows, width), lambda i: (i, 0, 0)),
+            index, row = place(j, sizes)
+            mine = piece_refs[index * blocks :][:blocks]
+            fill(vectors, [r[row] for r in mine], facts_ref[1 + j], facts_ref[0])
+            if j > 1:
+                copies[j - 2].wait()
+            block = second_ref[...] if j == 1 else held[j - 2]
+            out_ref[j - 1] = jnp.dot(
+                block, vectors[...], preferred_element_type=jnp.float32
+            ).astype(out_ref.dtype)
+
+    return pl.pallas_call(
+        kernel,
+        in_specs=[SMEM, ORDER, VMEM] + [VMEM] * (len(sizes) * blocks),
+        out_specs=VMEM,
         out_shape=jax.ShapeDtypeStruct((points - 1, rows, width), jnp.bfloat16),
-        scratch_shapes=[pltpu.VMEM((kept, width), jnp.bfloat16)],
+        scratch_shapes=[
+            pltpu.VMEM((kept, width), jnp.bfloat16),
+            pltpu.VMEM((points - 2, rows, kept), sets.dtype),
+            pltpu.SemaphoreType.DMA((points - 2,)),
+        ],
         compiler_params=params(),
         cost_estimate=CHEAP,
         name="apply_rest",
-    )(earlier, facts, sets, *sum(pieces, []))
+    )(facts, sets, second, *sum(pieces, []))
 
 
 def combine(sets, pieces, facts, kin, length, block, tail):
@@ -386,14 +407,18 @@
     mixed_rows = radial - plain
     peers = range(1, blocks)
 
-    pieces = [[v] + [shifted(v, "rows", d) for d in peers] for v in parted(trial_vecs)]
-    first = apply_first(coeffs, pieces[0], facts, mixed_rows, plain)
+    early = part_of(trial_vecs, 0, 1)
+    late = part_of(trial_vecs, 1, points - 1, early)
+    first_sets = fetch(coeffs, late, 0, mixed_rows, plain)
+    pieces = [[v] + [shifted(v, "rows", d) for d in peers] for v in (early, late)]
+    first = apply_first(first_sets, pieces[0], facts)
     first_sent = shifted(first, "blk", 1)
 
     table_index = jnp.arange(kinetic.shape[0], dtype=jnp.int32)
     one_hot = pair_table[:, :, None] == table_index[None, None, :]
     kin_own = jnp.sum(jnp.where(one_hot, kinetic[None, None, :], 0.0), axis=2)
-    rest = apply_rest(coeffs, pieces, first, facts, mixed_rows, plain)
+    second = fetch(coeffs, first, 1, mixed_rows, plain)
+    rest = apply_rest(coeffs, second, pieces, facts, mixed_rows)
     rest_sent = shifted(rest, "blk", 1)
     kin_next = shifted(after(kin_own, rest, first_sent), "blk", -1)
     mixed = combine(coeffs, pieces, facts, kin_next, mixed_rows, tail, tail)

time: 87.8 us -> 87 us (level)
  Pallas kernels: 33.1 us -> 34.6 us
  starting transfers between devices: 17.3 us -> 15.9 us
  waiting for transfers between devices: 33.7 us -> 32.8 us
    pallas_call x3 -> x6, Pallas kernels: 6.08 us -> 7.57 us  [the longest x1 3.39 us: apply_rest(): pl.pallas_call(kernel, in_specs=[SMEM, ORDER, VMEM] + [VMEM] * (len(sizes...]
    ppermute x14, starting transfers between devices: 17.3 us -> 15.9 us  [shifted(): return lax.ppermute(block, axis, route)]
    ppermute x14, waiting for transfers between devices: 33.7 us -> 32.8 us  [shifted(): return lax.ppermute(block, axis, route)]
  transfers between devices with their start and end apart: 14 -> 14, of which waited for: 11 -> 10; matrix products, arithmetic and copies ran while one was open for 2% -> 3% of each run, Pallas kernels for 36% -> 38%
where the time goes in v4:
time: 87 us; the launch traced here: 86.7 us
  Pallas kernels  34.6 us (40%)
  waiting for transfers between devices  32.8 us (38%)
  starting transfers between devices  15.9 us (18%)
  local copies, waits for them, and re-layouts  2.16 us (2%)
  other arithmetic  0.97 us (1%)
    ppermute x14, waiting for transfers between devices, shifted(): return lax.ppermute(block, axis, route)  32.8 us
    ppermute x14, starting transfers between devices, shifted(): return lax.ppermute(block, axis, route)  15.9 us
    pallas_call x1, Pallas kernels, combine(): pl.pallas_call(kernel, grid=(steps,), in_specs=[SMEM, SMEM, pl.BlockSpec(...  8.67 us
    pallas_call x3, Pallas kernels, finish_rows(): pl.pallas_call(kernel, grid=(steps,), in_specs=[ORDER, SMEM, pl.BlockSpec...  8.26 us
    pallas_call x1, Pallas kernels, collect(): pl.pallas_call(kernel, grid=(points,), in_specs=[SMEM, pl.BlockSpec((1, r...  6.03 us
    pallas_call x1, Pallas kernels, apply_rest(): pl.pallas_call(kernel, in_specs=[SMEM, ORDER, VMEM] + [VMEM] * (len(sizes...  3.39 us
    pallas_call x2, Pallas kernels, fetch(): pl.pallas_call(kernel, in_specs=[ORDER, ORDER], out_specs=VMEM, out_shape...  2.84 us
    pallas_call x1, Pallas kernels, gather_rows(): pl.pallas_call(kernel, grid=(length // block,), in_specs=[ORDER, pl.Block...  2.48 us
  transfers between devices with their start and end apart: 14, of which 10 were waited for; matrix products, arithmetic and copies ran while one was open for 3% of the time, Pallas kernels for 38%

profile of v4, /device:TPU:0, one launch (start us, length us, event | category | flops | bytes accessed | tf_op | source)
XLA Modules:
  0.0 86.7 jit_solution(11847132459661384437)
XLA Ops:
  0.0 0.9 %copy-done.1 = bf16[4,192,128]{2,1,0:T(8,128)(2,1)S(1)} copy-done((bf16[4,192,128]{2,1,0:T(8,128)(2,1)S(1)}, bf16[4,192,128]{2,1,0:T(8,128)(2,1)}, u32[]{:S(2)}) %copy-start.1) | copy-done | bytes 196632
  1.0 3.0 %collective-permute-start = (bf16[1,192,128]{2,1,0:T(8,128)(2,1)S(1)}, bf16[1,192,128]{2,1,0:T(8,128)(2,1)S(1)}, u32[]{:S(2)}, u32[]{:S(2)}) collective-permute-start(bf16[1,192,128]{2,1,0:T(8,128)(2,1)S(1)} %part_of.2.rest_0_.refs_0_), channel_id=1, source_target_pairs={{0,1},{1,0},{2,3},{3,2},{4,5},{5,4},{6,7},{7,6},{8,9},{9,8},{10,11... | collective-permute-start | bytes 147464 | tf_op jit(solution)/shard_map/ppermute | solution.py:20
  4.0 0.2 part_of.3._.rest_2_.refs_2_
  4.2 0.1 collective-permute-start.2
  4.3 0.7 pad_add_fusion.facts_ref
  5.0 1.4 %fetch.2.sets_ref = bf16[2048,384]{1,0:T(8,128)(2,1)S(1)} custom-call(bf16[4,6144,384]{2,1,0:T(8,128)(2,1)} %sets_ref.17, bf16[3,192,128]{2,1,0:T(8,128)(2,1)S(1)} %part_of.3._.rest_2_.refs_2_), custom_call_target="tpu_custom_call" | custom-call | flops 1 | bytes 1 | tf_op jit(solution)/shard_map/fetch/pallas_call | solution.py:88
  6.4 0.0 collective-permute-done.rest_1_.refs_1_
  6.5 1.1 %apply_first.1._ = bf16[1,2048,128]{2,1,0:T(8,128)(2,1)S(1)} custom-call(s32[7]{0:T(128)S(1)} %pad_add_fusion.facts_ref, bf16[2048,384]{1,0:T(8,128)(2,1)S(1)} %fetch.2.sets_ref, bf16[1,192,128]{2,1,0:T(8,128)(2,1)S(1)} %part_of.2.rest_0_.refs_0_, bf16[1,192,128]{2,1,0:T(8,128)(2,1)S(1)} %collective-permute-done.rest_1_.refs_1_), custom_call_target="tpu_custom_call" | custom-call | flops 1000000000 | bytes 1000000 | tf_op jit(solution)/shard_map/apply_first/pallas_call | solution.py:111
  7.6 0.1 collective-permute-start.1
  7.7 1.4 %fetch.3.second_ref = bf16[2048,384]{1,0:T(8,128)(2,1)S(1)} custom-call(bf16[4,6144,384]{2,1,0:T(8,128)(2,1)} %sets_ref.17, bf16[1,2048,128]{2,1,0:T(8,128)(2,1)S(1)} %apply_first.1._), custom_call_target="tpu_custom_call" | custom-call | flops 1 | bytes 1 | tf_op jit(solution)/shard_map/fetch/pallas_call | solution.py:88
  9.1 0.0 copy-start.2
  9.1 0.0 copy-start.3
  9.1 0.4 collective-permute-done.2.rest_3_.refs_3_
  9.5 3.4 %apply_rest.1 = bf16[3,2048,128]{2,1,0:T(8,128)(2,1)S(1)} custom-call(s32[7]{0:T(128)S(1)} %pad_add_fusion.facts_ref, bf16[4,6144,384]{2,1,0:T(8,128)(2,1)} %sets_ref.17, bf16[2048,384]{1,0:T(8,128)(2,1)S(1)} %fetch.3.second_ref, bf16[1,192,128]{2,1,0:T(8,128)(2,1)S(1)} %part_of.2.rest_0_.refs_0_, ...), custom_call_target="tpu_custom_call" | custom-call | flops 1 | bytes 1 | tf_op jit(solution)/shard_map/apply_rest/pallas_call | solution.py:151
  12.9 1.8 %collective-permute-start.5 = (bf16[3,2048,128]{2,1,0:T(8,128)(2,1)S(1)}, bf16[3,2048,128]{2,1,0:T(8,128)(2,1)S(1)}, u32[]{:S(2)}, u32[]{:S(2)}) collective-permute-start(bf16[3,2048,128]{2,1,0:T(8,128)(2,1)S(1)} %apply_rest.1), channel_id=1, source_target_pairs={{0,2},{2,4},{4,6},{6,8},{8,10},{10,12},{12,14},{14,16},{16,18},{18... | collective-permute-start | bytes 4718600 | tf_op jit(solution)/shard_map/ppermute | solution.py:20
  14.7 0.2 select_reduce_fusion.kin_ref
  14.9 4.1 %collective-permute-done.1.first_ref._ = bf16[1,2048,128]{2,1,0:T(8,128)(2,1)S(1)} collective-permute-done((bf16[1,2048,128]{2,1,0:T(8,128)(2,1)S(1)}, bf16[1,2048,128]{2,1,0:T(8,128)(2,1)S(1)}, u32[]{:S(2)}, u32[]{:S(2)}) %collective-permute-start.1) | collective-permute-done | bytes 524320 | tf_op jit(solution)/shard_map/ppermute | solution.py:20
  19.0 0.0 collective-permute-start.3
  19.0 1.3 %collective-permute-done.3.kin_ref = f32[4,4]{1,0:T(4,128)S(1)} collective-permute-done((f32[4,4]{1,0:T(4,128)S(1)}, f32[4,4]{1,0:T(4,128)S(1)}, u32[]{:S(2)}, u32[]{:S(2)}) %collective-permute-start.3) | collective-permute-done | bytes 96 | tf_op jit(solution)/shard_map/ppermute | solution.py:20
  20.3 8.7 %combine.1 = (bf16[4096,128]{1,0:T(8,128)(2,1)S(1)}, bf16[4096,128]{1,0:T(8,128)(2,1)S(1)}, bf16[4096,128]{1,0:T(8,128)(2,1)}, bf16[3072,128]{1,0:T(8,128)(2,1)S(1)}, bf16[1024,128]{1,0:T(8,128)(2,1)S(1)}) custom-call(s32[7]{0:T(128)S(1)} %pad_add_fusion.facts_ref, f32[4,4]{1,0:T(4,128)S(1)} %collective-permute-done.3.kin_ref, ...), custom_call_target="tpu_custom_call" | custom-call | flops 1 | bytes 1 | tf_op jit(solution)/shard_map/combine/pallas_call | solution.py:212
  28.9 0.0 collective-permute-start.4
  29.0 0.0 collective-permute-start.7
  29.0 2.0 %collective-permute-start.9 = (bf16[4096,128]{1,0:T(8,128)(2,1)}, bf16[4096,128]{1,0:T(8,128)(2,1)S(1)}, u32[]{:S(2)}, u32[]{:S(2)}) collective-permute-start(bf16[4096,128]{1,0:T(8,128)(2,1)} %get-tuple-element.34), channel_id=1, source_target_pairs={{0,2},{2,4},{4,6},{6,8},{8,10},{10,12},{12,14},{14,16},{16,18},{18... | collective-permute-start | bytes 3145736 | tf_op jit(solution)/shard_map/ppermute | solution.py:20
  31.0 0.0 collective-permute-start.12
  31.0 4.8 %collective-permute-done.5.rest_ref = bf16[3,2048,128]{2,1,0:T(8,128)(2,1)S(1)} collective-permute-done((bf16[3,2048,128]{2,1,0:T(8,128)(2,1)S(1)}, bf16[3,2048,128]{2,1,0:T(8,128)(2,1)S(1)}, u32[]{:S(2)}, u32[]{:S(2)}) %collective-permute-start.5) | collective-permute-done | bytes 1572896 | tf_op jit(solution)/shard_map/ppermute | solution.py:20
  35.8 6.0 %collect.1.before_ref = f32[4,384,128]{2,1,0:T(8,128)S(1)} custom-call(f32[4,4]{1,0:T(4,128)S(1)} %select_reduce_fusion.kin_ref, bf16[4,6144,384]{2,1,0:T(8,128)(2,1)} %sets_ref.17, bf16[1,2048,128]{2,1,0:T(8,128)(2,1)S(1)} %collective-permute-done.1.first_ref._, bf16[3,2048,128]{2,1,0:T(8,128)(2,1)S(1)} %collective-permute-done.5.rest_ref), custom_call_target="tpu_custom_call" | custom-call | flops 1 | bytes 1 | tf_op jit(solution)/shard_map/collect/pallas_call | solution.py:248
  41.9 5.2 %collective-permute-done.4.arrived_ref = bf16[4096,128]{1,0:T(8,128)(2,1)S(1)} collective-permute-done((bf16[4096,128]{1,0:T(8,128)(2,1)S(1)}, bf16[4096,128]{1,0:T(8,128)(2,1)S(1)}, u32[]{:S(2)}, u32[]{:S(2)}) %collective-permute-start.4) | collective-permute-done | bytes 1048608 | tf_op jit(solution)/shard_map/ppermute | solution.py:20
  47.1 2.8 %finish_rows.3 = (f32[192,128]{1,0:T(8,128)S(1)}, bf16[1,192,128]{2,1,0:T(8,128)(2,1)S(1)}) custom-call(bf16[1,2048,128]{2,1,0:T(8,128)(2,1)S(1)} %collective-permute-done.1.first_ref._, s32[7]{0:T(128)S(1)} %pad_add_fusion.facts_ref, bf16[4,6144,384]{2,1,0:T(8,128)(2,1)} %sets_ref.17, bf16[4096,128]{1,0:T(8,128)(2,1)S(1)} %collective-permute-done.4.arrived_ref, ...), custom_call_target="tpu_custom_call" | custom-call | flops 1 | bytes 1 | tf_op jit(solution)/shard_map/finish_rows/pallas_call | solution.py:321
  49.8 2.2 %collective-permute-start.6 = (bf16[192,128]{1,0:T(8,128)(2,1)S(1)}, bf16[192,128]{1,0:T(8,128)(2,1)S(1)}, u32[]{:S(2)}, u32[]{:S(2)}) collective-permute-start(bf16[192,128]{1,0:T(8,128)(2,1)S(1)} %bitcast.13), channel_id=1, source_target_pairs={{0,1},{1,0},{2,3},{3,2},{4,5},{5,4},{6,7},{7,6},{8,9},{9,8},{10,11... | collective-permute-start | bytes 147464 | tf_op jit(solution)/shard_map/ppermute | solution.py:20
  52.1 1.2 %slice_bitcast_fusion.sets_ref = bf16[1024,384]{1,0:T(8,128)(2,1)S(1)} fusion(bf16[4,6144,384]{2,1,0:T(8,128)(2,1)} %sets_ref.17), kind=kLoop, calls=%fused_computation | loop fusion | bytes 1572864 | tf_op jit(solution)/shard_map/squeeze | solution.py:445
  53.3 0.1 collective-permute-start.11
  53.3 5.0 %collective-permute-done.7.arrived_ref = bf16[4096,128]{1,0:T(8,128)(2,1)S(1)} collective-permute-done((bf16[4096,128]{1,0:T(8,128)(2,1)S(1)}, bf16[4096,128]{1,0:T(8,128)(2,1)S(1)}, u32[]{:S(2)}, u32[]{:S(2)}) %collective-permute-start.7) | collective-permute-done | bytes 1048608 | tf_op jit(solution)/shard_map/ppermute | solution.py:20
  58.3 2.8 %finish_rows.4 = (f32[192,128]{1,0:T(8,128)S(1)}, bf16[1,192,128]{2,1,0:T(8,128)(2,1)S(1)}) custom-call(f32[192,128]{1,0:T(8,128)S(1)} %get-tuple-element.27._, s32[7]{0:T(128)S(1)} %pad_add_fusion.facts_ref, bf16[4,6144,384]{2,1,0:T(8,128)(2,1)} %sets_ref.17, bf16[4096,128]{1,0:T(8,128)(2,1)S(1)} %collective-permute-done.7.arrived_ref, ...), custom_call_target="tpu_custom_call" | custom-call | flops 1 | bytes 1 | tf_op jit(solution)/shard_map/finish_rows/pallas_call | solution.py:321
  61.1 2.2 %collective-permute-start.8 = (bf16[192,128]{1,0:T(8,128)(2,1)S(1)}, bf16[192,128]{1,0:T(8,128)(2,1)S(1)}, u32[]{:S(2)}, u32[]{:S(2)}) collective-permute-start(bf16[192,128]{1,0:T(8,128)(2,1)S(1)} %bitcast.14), channel_id=1, source_target_pairs={{0,1},{1,0},{2,3},{3,2},{4,5},{5,4},{6,7},{7,6},{8,9},{9,8},{10,11... | collective-permute-start | bytes 147464 | tf_op jit(solution)/shard_map/ppermute | solution.py:20
  63.3 6.3 %collective-permute-done.9.arrived_ref = bf16[4096,128]{1,0:T(8,128)(2,1)S(1)} collective-permute-done((bf16[4096,128]{1,0:T(8,128)(2,1)}, bf16[4096,128]{1,0:T(8,128)(2,1)S(1)}, u32[]{:S(2)}, u32[]{:S(2)}) %collective-permute-start.9) | collective-permute-done | bytes 1048608 | tf_op jit(solution)/shard_map/ppermute | solution.py:20
  69.5 2.8 %finish_rows.5 = (f32[192,128]{1,0:T(8,128)S(1)}, bf16[1,192,128]{2,1,0:T(8,128)(2,1)S(1)}) custom-call(f32[192,128]{1,0:T(8,128)S(1)} %get-tuple-element.31._, s32[7]{0:T(128)S(1)} %pad_add_fusion.facts_ref, bf16[4,6144,384]{2,1,0:T(8,128)(2,1)} %sets_ref.17, bf16[4096,128]{1,0:T(8,128)(2,1)S(1)} %collective-permute-done.9.arrived_ref, ...), custom_call_target="tpu_custom_call" | custom-call | flops 1 | bytes 1 | tf_op jit(solution)/shard_map/finish_rows/pallas_call | solution.py:321
  72.3 2.2 %collective-permute-start.10 = (bf16[192,128]{1,0:T(8,128)(2,1)S(1)}, bf16[192,128]{1,0:T(8,128)(2,1)S(1)}, u32[]{:S(2)}, u32[]{:S(2)}) collective-permute-start(bf16[192,128]{1,0:T(8,128)(2,1)S(1)} %bitcast.15), channel_id=1, source_target_pairs={{0,1},{1,0},{2,3},{3,2},{4,5},{5,4},{6,7},{7,6},{8,9},{9,8},{10,11... | collective-permute-start | bytes 147464 | tf_op jit(solution)/shard_map/ppermute | solution.py:20
  74.5 3.4 %collective-permute-done.12.arrived_ref = bf16[3072,128]{1,0:T(8,128)(2,1)S(1)} collective-permute-done((bf16[3072,128]{1,0:T(8,128)(2,1)S(1)}, bf16[3072,128]{1,0:T(8,128)(2,1)S(1)}, u32[]{:S(2)}, u32[]{:S(2)}) %collective-permute-start.12) | collective-permute-done | bytes 786464 | tf_op jit(solution)/shard_map/ppermute | solution.py:20
  78.0 2.5 %gather_rows.1.before_ref = f32[384,128]{1,0:T(8,128)S(1)} custom-call(f32[192,128]{1,0:T(8,128)S(1)} %get-tuple-element.35._, bf16[4,6144,384]{2,1,0:T(8,128)(2,1)} %sets_ref.17, bf16[3072,128]{1,0:T(8,128)(2,1)S(1)} %collective-permute-done.12.arrived_ref, f32[4,384,128]{2,1,0:T(8,128)S(1)} %collect.1.before_ref), custom_call_target="tpu_custom_call" | custom-call | flops 1 | bytes 1 | tf_op jit(solution)/shard_map/gather_rows/pallas_call | solution.py:285
  80.5 0.0 collective-permute-done.6
  80.5 0.0 collective-permute-done.8
  80.5 0.0 collective-permute-done.10
  80.6 0.0 copy-start
  80.6 0.2 collective-permute-done.11.arrived_ref
  80.8 1.0 %finish_last.1 = (f32[192,128]{1,0:T(8,128)S(1)}, bf16[1,192,128]{2,1,0:T(8,128)(2,1)S(1)}) custom-call(bf16[4,192,128]{2,1,0:T(8,128)(2,1)S(1)} %pad_maximum_fusion._, s32[7]{0:T(128)S(1)} %pad_add_fusion.facts_ref, bf16[1024,384]{1,0:T(8,128)(2,1)S(1)} %slice_bitcast_fusion.sets_ref, bf16[1024,128]{1,0:T(8,128)(2,1)S(1)} %collective-permute-done.11.arrived_ref, ...), custom_call_target="tpu_custom_call" | custom-call | flops 1 | bytes 1 | tf_op jit(solution)/shard_map/finish_last/pallas_call | solution.py:355
  81.7 2.2 %collective-permute-start.13 = (bf16[192,128]{1,0:T(8,128)(2,1)S(1)}, bf16[192,128]{1,0:T(8,128)(2,1)S(1)}, u32[]{:S(2)}, u32[]{:S(2)}) collective-permute-start(bf16[192,128]{1,0:T(8,128)(2,1)S(1)} %bitcast.16), channel_id=1, source_target_pairs={{0,1},{1,0},{2,3},{3,2},{4,5},{5,4},{6,7},{7,6},{8,9},{9,8},{10,11... | collective-permute-start | bytes 147464 | tf_op jit(solution)/shard_map/ppermute | solution.py:20
  84.0 2.1 %collective-permute-done.13.rest_0_ = bf16[192,128]{1,0:T(8,128)(2,1)S(1)} collective-permute-done((bf16[192,128]{1,0:T(8,128)(2,1)S(1)}, bf16[192,128]{1,0:T(8,128)(2,1)S(1)}, u32[]{:S(2)}, u32[]{:S(2)}) %collective-permute-start.13) | collective-permute-done | bytes 49184 | tf_op jit(solution)/shard_map/ppermute | solution.py:20
  86.0 0.6 place_last.1
  (9 shorter events, 0.1 us)
Async XLA Ops:
  0.0 0.9 %copy-start.1 = (bf16[4,192,128]{2,1,0:T(8,128)(2,1)S(1)}, bf16[4,192,128]{2,1,0:T(8,128)(2,1)}, u32[]{:S(2)}) copy-start(bf16[4,192,128]{2,1,0:T(8,128)(2,1)} %vectors_ref.3) | copy-start | bytes 589828
  1.0 5.5 %collective-permute-start = (bf16[1,192,128]{2,1,0:T(8,128)(2,1)S(1)}, bf16[1,192,128]{2,1,0:T(8,128)(2,1)S(1)}, u32[]{:S(2)}, u32[]{:S(2)}) collective-permute-start(bf16[1,192,128]{2,1,0:T(8,128)(2,1)S(1)} %part_of.2.rest_0_.refs_0_), channel_id=1, source_target_pairs={{0,1},{1,0},{2,3},{3,2},{4,5},{5,4},{6,7},{7,6},{8,9},{9,8},{10,11... | collective-permute-start | bytes 147464 | tf_op jit(solution)/shard_map/ppermute | solution.py:20
  4.2 5.4 %collective-permute-start.2 = (bf16[3,192,128]{2,1,0:T(8,128)(2,1)S(1)}, bf16[3,192,128]{2,1,0:T(8,128)(2,1)S(1)}, u32[]{:S(2)}, u32[]{:S(2)}) collective-permute-start(bf16[3,192,128]{2,1,0:T(8,128)(2,1)S(1)} %part_of.3._.rest_2_.refs_2_), channel_id=1, source_target_pairs={{0,1},{1,0},{2,3},{3,2},{4,5},{5,4},{6,7},{7,6},{8,9},{9,8},{10,11... | collective-permute-start | bytes 442376 | tf_op jit(solution)/shard_map/ppermute | solution.py:20
  7.6 11.4 %collective-permute-start.1 = (bf16[1,2048,128]{2,1,0:T(8,128)(2,1)S(1)}, bf16[1,2048,128]{2,1,0:T(8,128)(2,1)S(1)}, u32[]{:S(2)}, u32[]{:S(2)}) collective-permute-start(bf16[1,2048,128]{2,1,0:T(8,128)(2,1)S(1)} %apply_first.1._), channel_id=1, source_target_pairs={{0,2},{2,4},{4,6},{6,8},{8,10},{10,12},{12,14},{14,16},{16,18},{18... | collective-permute-start | bytes 1572872 | tf_op jit(solution)/shard_map/ppermute | solution.py:20
  9.1 5.6 %copy-start.2 = (s32[4,4]{1,0:T(4,128)S(1)}, s32[4,4]{1,0:T(4,128)}, u32[]{:S(2)}) copy-start(s32[4,4]{1,0:T(4,128)} %param.9) | copy-start | bytes 196
  9.1 5.6 %copy-start.3 = (f32[64]{0:T(128)S(1)}, f32[64]{0:T(128)}, u32[]{:S(2)}) copy-start(f32[64]{0:T(128)} %param.8) | copy-start | bytes 772
  12.9 22.9 %collective-permute-start.5 = (bf16[3,2048,128]{2,1,0:T(8,128)(2,1)S(1)}, bf16[3,2048,128]{2,1,0:T(8,128)(2,1)S(1)}, u32[]{:S(2)}, u32[]{:S(2)}) collective-permute-start(bf16[3,2048,128]{2,1,0:T(8,128)(2,1)S(1)} %apply_rest.1), channel_id=1, source_target_pairs={{0,2},{2,4},{4,6},{6,8},{8,10},{10,12},{12,14},{14,16},{16,18},{18... | collective-permute-start | bytes 4718600 | tf_op jit(solution)/shard_map/ppermute | solution.py:20
  19.0 1.3 %collective-permute-start.3 = (f32[4,4]{1,0:T(4,128)S(1)}, f32[4,4]{1,0:T(4,128)S(1)}, u32[]{:S(2)}, u32[]{:S(2)}) collective-permute-start(f32[4,4]{1,0:T(4,128)S(1)} %select_reduce_fusion.kin_ref), channel_id=1, source_target_pairs={{0,30},{2,0},{4,2},{6,4},{8,6},{10,8},{12,10},{14,12},{16,14},{18,... | collective-permute-start | bytes 200 | tf_op jit(solution)/shard_map/ppermute | solution.py:20
  28.9 18.1 %collective-permute-start.4 = (bf16[4096,128]{1,0:T(8,128)(2,1)S(1)}, bf16[4096,128]{1,0:T(8,128)(2,1)S(1)}, u32[]{:S(2)}, u32[]{:S(2)}) collective-permute-start(bf16[4096,128]{1,0:T(8,128)(2,1)S(1)} %get-tuple-element.26), channel_id=1, source_target_pairs={{0,2},{2,4},{4,6},{6,8},{8,10},{10,12},{12,14},{14,16},{16,18},{18... | collective-permute-start | bytes 3145736 | tf_op jit(solution)/shard_map/ppermute | solution.py:20
  29.0 29.3 %collective-permute-start.7 = (bf16[4096,128]{1,0:T(8,128)(2,1)S(1)}, bf16[4096,128]{1,0:T(8,128)(2,1)S(1)}, u32[]{:S(2)}, u32[]{:S(2)}) collective-permute-start(bf16[4096,128]{1,0:T(8,128)(2,1)S(1)} %get-tuple-element.30), channel_id=1, source_target_pairs={{0,2},{2,4},{4,6},{6,8},{8,10},{10,12},{12,14},{14,16},{16,18},{18... | collective-permute-start | bytes 3145736 | tf_op jit(solution)/shard_map/ppermute | solution.py:20
  29.0 40.6 %collective-permute-start.9 = (bf16[4096,128]{1,0:T(8,128)(2,1)}, bf16[4096,128]{1,0:T(8,128)(2,1)S(1)}, u32[]{:S(2)}, u32[]{:S(2)}) collective-permute-start(bf16[4096,128]{1,0:T(8,128)(2,1)} %get-tuple-element.34), channel_id=1, source_target_pairs={{0,2},{2,4},{4,6},{6,8},{8,10},{10,12},{12,14},{14,16},{16,18},{18... | collective-permute-start | bytes 3145736 | tf_op jit(solution)/shard_map/ppermute | solution.py:20
  31.0 47.0 %collective-permute-start.12 = (bf16[3072,128]{1,0:T(8,128)(2,1)S(1)}, bf16[3072,128]{1,0:T(8,128)(2,1)S(1)}, u32[]{:S(2)}, u32[]{:S(2)}) collective-permute-start(bf16[3072,128]{1,0:T(8,128)(2,1)S(1)} %get-tuple-element.39), channel_id=1, source_target_pairs={{0,2},{2,4},{4,6},{6,8},{8,10},{10,12},{12,14},{14,16},{16,18},{18... | collective-permute-start | bytes 2359304 | tf_op jit(solution)/shard_map/ppermute | solution.py:20
  49.8 30.6 %collective-permute-start.6 = (bf16[192,128]{1,0:T(8,128)(2,1)S(1)}, bf16[192,128]{1,0:T(8,128)(2,1)S(1)}, u32[]{:S(2)}, u32[]{:S(2)}) collective-permute-start(bf16[192,128]{1,0:T(8,128)(2,1)S(1)} %bitcast.13), channel_id=1, source_target_pairs={{0,1},{1,0},{2,3},{3,2},{4,5},{5,4},{6,7},{7,6},{8,9},{9,8},{10,11... | collective-permute-start | bytes 147464 | tf_op jit(solution)/shard_map/ppermute | solution.py:20
  53.3 27.5 %collective-permute-start.11 = (bf16[1024,128]{1,0:T(8,128)(2,1)S(1)}, bf16[1024,128]{1,0:T(8,128)(2,1)S(1)}, u32[]{:S(2)}, u32[]{:S(2)}) collective-permute-start(bf16[1024,128]{1,0:T(8,128)(2,1)S(1)} %get-tuple-element.40), channel_id=1, source_target_pairs={{0,2},{2,4},{4,6},{6,8},{8,10},{10,12},{12,14},{14,16},{16,18},{18... | collective-permute-start | bytes 786440 | tf_op jit(solution)/shard_map/ppermute | solution.py:20
  61.1 19.4 %collective-permute-start.8 = (bf16[192,128]{1,0:T(8,128)(2,1)S(1)}, bf16[192,128]{1,0:T(8,128)(2,1)S(1)}, u32[]{:S(2)}, u32[]{:S(2)}) collective-permute-start(bf16[192,128]{1,0:T(8,128)(2,1)S(1)} %bitcast.14), channel_id=1, source_target_pairs={{0,1},{1,0},{2,3},{3,2},{4,5},{5,4},{6,7},{7,6},{8,9},{9,8},{10,11... | collective-permute-start | bytes 147464 | tf_op jit(solution)/shard_map/ppermute | solution.py:20
  72.3 8.2 %collective-permute-start.10 = (bf16[192,128]{1,0:T(8,128)(2,1)S(1)}, bf16[192,128]{1,0:T(8,128)(2,1)S(1)}, u32[]{:S(2)}, u32[]{:S(2)}) collective-permute-start(bf16[192,128]{1,0:T(8,128)(2,1)S(1)} %bitcast.15), channel_id=1, source_target_pairs={{0,1},{1,0},{2,3},{3,2},{4,5},{5,4},{6,7},{7,6},{8,9},{9,8},{10,11... | collective-permute-start | bytes 147464 | tf_op jit(solution)/shard_map/ppermute | solution.py:20
  80.6 5.4 %copy-start = (bf16[4,192,128]{2,1,0:T(8,128)(2,1)}, bf16[4,192,128]{2,1,0:T(8,128)(2,1)S(1)}, u32[]{:S(2)}) copy-start(bf16[4,192,128]{2,1,0:T(8,128)(2,1)S(1)} %pad_maximum_fusion._) | copy-start | bytes 589828
  81.7 4.3 %collective-permute-start.13 = (bf16[192,128]{1,0:T(8,128)(2,1)S(1)}, bf16[192,128]{1,0:T(8,128)(2,1)S(1)}, u32[]{:S(2)}, u32[]{:S(2)}) collective-permute-start(bf16[192,128]{1,0:T(8,128)(2,1)S(1)} %bitcast.16), channel_id=1, source_target_pairs={{0,1},{1,0},{2,3},{3,2},{4,5},{5,4},{6,7},{7,6},{8,9},{9,8},{10,11... | collective-permute-start | bytes 147464 | tf_op jit(solution)/shard_map/ppermute | solution.py:20

commit v5 on v4

--- a/solution.py
+++ b/solution.py
@@ -44,6 +44,25 @@
         vectors[pl.ds(start, share), :] = kept.astype(vectors.dtype)
 
 
+def chosen(rows, values, shape):
+    result = values[0]
+    for index in range(1, len(values)):
+        result = jnp.where(jnp.broadcast_to(rows, shape) == index, values[index], result)
+    return result
+
+
+def fill_by(vectors, pieces, flags_ref, point):
+    shape = pieces[0].shape
+    share, blocks = shape[0], len(pieces)
+    held = [piece.astype(jnp.float32) for piece in pieces]
+    for p in range(blocks):
+        value = chosen(flags_ref[0:1, :], [held[(m - p) % blocks] for m in range(blocks)], shape)
+        row = p * share + lax.broadcasted_iota(jnp.int32, shape, 0)
+        count = jnp.broadcast_to(flags_ref[1 + point : 2 + point, :], shape)
+        kept = jnp.where(row < count, value, 0.0)
+        vectors[p * share : (p + 1) * share, :] = kept.astype(vectors.dtype)
+
+
 def parcels(points):
     return 1, points - 1
 
@@ -97,37 +116,37 @@
     )(sets, earlier)
 
 
-def apply_first(sets, pieces, facts):
+def apply_first(sets, pieces, flags):
     rows, kept = sets.shape
     width = pieces[0].shape[2]
 
-    def kernel(facts_ref, sets_ref, *rest):
+    def kernel(flags_ref, sets_ref, *rest):
         *piece_refs, out_ref, vectors = rest
-        fill(vectors, [r[0] for r in piece_refs], facts_ref[1], facts_ref[0])
+        fill_by(vectors, [r[0] for r in piece_refs], flags_ref, 0)
         out_ref[0] = jnp.dot(
             sets_ref[...], vectors[...], preferred_element_type=jnp.float32
         ).astype(out_ref.dtype)
 
     return pl.pallas_call(
         kernel,
-        in_specs=[SMEM] + [VMEM] * (1 + len(pieces)),
+        in_specs=[VMEM] * (2 + len(pieces)),
         out_specs=VMEM,
         out_shape=jax.ShapeDtypeStruct((1, rows, width), jnp.bfloat16),
         scratch_shapes=[pltpu.VMEM((kept, width), jnp.bfloat16)],
         compiler_params=params(),
         cost_estimate=pl.CostEstimate(flops=10**9, bytes_accessed=10**6, transcendentals=0),
         name="apply_first",
-    )(facts, sets, *pieces)
-
-
-def apply_rest(sets, second, pieces, facts, start):
+    )(flags, sets, *pieces)
+
+
+def apply_rest(sets, second, pieces, flags, start):
     points, _, kept = sets.shape
     rows = second.shape[0]
     width = pieces[0][0].shape[2]
     blocks = len(pieces[0])
     sizes = parcels(points)
 
-    def kernel(facts_ref, sets_ref, second_ref, *rest):
+    def kernel(flags_ref, sets_ref, second_ref, *rest):
         *piece_refs, out_ref, vectors, held, sems = rest
         copies = [
             pltpu.make_async_copy(
@@ -140,7 +159,7 @@
         for j in range(1, points):
             index, row = place(j, sizes)
             mine = piece_refs[index * blocks :][:blocks]
-            fill(vectors, [r[row] for r in mine], facts_ref[1 + j], facts_ref[0])
+            fill_by(vectors, [r[row] for r in mine], flags_ref, j)
             if j > 1:
                 copies[j - 2].wait()
             block = second_ref[...] if j == 1 else held[j - 2]
@@ -150,7 +169,7 @@
 
     return pl.pallas_call(
         kernel,
-        in_specs=[SMEM, ORDER, VMEM] + [VMEM] * (len(sizes) * blocks),
+        in_specs=[VMEM, ORDER, VMEM] + [VMEM] * (len(sizes) * blocks),
         out_specs=VMEM,
         out_shape=jax.ShapeDtypeStruct((points - 1, rows, width), jnp.bfloat16),
         scratch_shapes=[
@@ -161,7 +180,7 @@
         compiler_params=params(),
         cost_estimate=CHEAP,
         name="apply_rest",
-    )(facts, sets, second, *sum(pieces, []))
+    )(flags, sets, second, *sum(pieces, []))
 
 
 def combine(sets, pieces, facts, kin, length, block, tail):
@@ -343,28 +362,39 @@
     )(earlier, facts, sets, arrived, before)
 
 
-def finish_last(sets, arrived, before, earlier, facts, point, points, share):
+def finish_last(sets, arrived, before, earlier, flags, point, points, share):
     kept = sets.shape[1]
     width = arrived.shape[1]
-    blocks = facts.shape[0] - 1 - points
-
-    def kernel(_, facts_ref, sets_ref, arrived_ref, before_ref, own_ref, send_ref, held):
+    blocks = kept // share
+
+    def kernel(_, flags_ref, sets_ref, arrived_ref, before_ref, own_ref, send_ref):
         total = before_ref[...] + contract_rows(sets_ref[...], arrived_ref[...])
-        split_blocks(total, point, points, facts_ref, held, own_ref, send_ref)
-
-    return pl.pallas_call(
-        kernel,
-        in_specs=[ORDER, SMEM] + [VMEM] * 3,
+        row = lax.broadcasted_iota(jnp.int32, total.shape, 0)
+        count = jnp.broadcast_to(flags_ref[1 + point : 2 + point, :], total.shape)
+        total = jnp.where(row < count, total, 0.0)
+        parts = [total[b * share : (b + 1) * share] for b in range(blocks)]
+        owners = [flags_ref[1 + points + i : 2 + points + i, :] for i in range(blocks)]
+        me = flags_ref[0:1, :]
+        for d in range(blocks):
+            owner = chosen(me, [owners[(m + d) % blocks] for m in range(blocks)], me.shape)
+            part = chosen(owner, parts, parts[0].shape)
+            if d == 0:
+                own_ref[...] = part
+            else:
+                send_ref[d - 1] = part.astype(send_ref.dtype)
+
+    return pl.pallas_call(
+        kernel,
+        in_specs=[ORDER] + [VMEM] * 4,
         out_specs=[VMEM, VMEM],
         out_shape=[
             jax.ShapeDtypeStruct((share, width), jnp.float32),
             jax.ShapeDtypeStruct((blocks - 1, share, width), jnp.bfloat16),
         ],
-        scratch_shapes=[pltpu.VMEM((kept, width), jnp.float32)],
         compiler_params=params(),
         cost_estimate=CHEAP,
         name="finish_last",
-    )(earlier, facts, sets, arrived, before)
+    )(earlier, flags, sets, arrived, before)
 
 
 def place_last(ready, own, others):
@@ -402,6 +432,7 @@
     blocks = owner_map.shape[0]
     me = lax.axis_index("rows").astype(jnp.int32).reshape(1)
     facts = jnp.concatenate([me, counts, owner_map])
+    flags = jnp.broadcast_to(facts[:, None], (facts.shape[0], width))
     unit = radial // 12
     plain, tail = 4 * unit, 2 * unit
     mixed_rows = radial - plain
@@ -411,14 +442,14 @@
     late = part_of(trial_vecs, 1, points - 1, early)
     first_sets = fetch(coeffs, late, 0, mixed_rows, plain)
     pieces = [[v] + [shifted(v, "rows", d) for d in peers] for v in (early, late)]
-    first = apply_first(first_sets, pieces[0], facts)
+    first = apply_first(first_sets, pieces[0], flags)
     first_sent = shifted(first, "blk", 1)
 
     table_index = jnp.arange(kinetic.shape[0], dtype=jnp.int32)
     one_hot = pair_table[:, :, None] == table_index[None, None, :]
     kin_own = jnp.sum(jnp.where(one_hot, kinetic[None, None, :], 0.0), axis=2)
     second = fetch(coeffs, first, 1, mixed_rows, plain)
-    rest = apply_rest(coeffs, second, pieces, facts, mixed_rows)
+    rest = apply_rest(coeffs, second, pieces, flags, mixed_rows)
     rest_sent = shifted(rest, "blk", 1)
     kin_next = shifted(after(kin_own, rest, first_sent), "blk", -1)
     mixed = combine(coeffs, pieces, facts, kin_next, mixed_rows, tail, tail)
@@ -442,7 +473,7 @@
     total = gather_rows(coeffs, mixed_sent[last], base, earlier, last, mixed_rows - tail)
     ready = jnp.stack(done + done[:1]).astype(jnp.bfloat16)
     own, send = finish_last(
-        coeffs[last, mixed_rows - tail : mixed_rows], mixed_sent[points], total, ready, facts, last, points, share
+        coeffs[last, mixed_rows - tail : mixed_rows], mixed_sent[points], total, ready, flags, last, points, share
     )
     return place_last(ready, own, [shifted(send[d - 1], "rows", d) for d in peers])
 

time: 87 us -> 86.1 us (0.990)
  Pallas kernels: 34.6 us -> 33 us
  waiting for transfers between devices: 32.8 us -> 33.7 us
    pallas_call x3, Pallas kernels: 5.49 us -> 4 us  [the longest x1 3 us: apply_rest(): pl.pallas_call(kernel, in_specs=[VMEM, ORDER, VMEM] + [VMEM] * (len(sizes...]
    ppermute x14, waiting for transfers between devices: 32.8 us -> 33.7 us  [shifted(): return lax.ppermute(block, axis, route)]
  transfers between devices with their start and end apart: 14 -> 14, of which waited for: 10 -> 10; matrix products, arithmetic and copies ran while one was open for 3% -> 3% of each run, Pallas kernels for 38% -> 37%
where the time goes in v5:
time: 86.1 us; the launch traced here: 85.6 us
  waiting for transfers between devices  33.7 us (39%)
  Pallas kernels  33 us (38%)
  starting transfers between devices  15.5 us (18%)
  local copies, waits for them, and re-layouts  2.23 us (3%)
  other arithmetic  0.97 us (1%)
    ppermute x14, waiting for transfers between devices, shifted(): return lax.ppermute(block, axis, route)  33.7 us
    ppermute x14, starting transfers between devices, shifted(): return lax.ppermute(block, axis, route)  15.5 us
    pallas_call x1, Pallas kernels, combine(): pl.pallas_call(kernel, grid=(steps,), in_specs=[SMEM, SMEM, pl.BlockSpec(...  8.67 us
    pallas_call x3, Pallas kernels, finish_rows(): pl.pallas_call(kernel, grid=(steps,), in_specs=[ORDER, SMEM, pl.BlockSpec...  8.23 us
    pallas_call x1, Pallas kernels, collect(): pl.pallas_call(kernel, grid=(points,), in_specs=[SMEM, pl.BlockSpec((1, r...  5.99 us
    pallas_call x1, Pallas kernels, apply_rest(): pl.pallas_call(kernel, in_specs=[VMEM, ORDER, VMEM] + [VMEM] * (len(sizes...  3 us
    pallas_call x2, Pallas kernels, fetch(): pl.pallas_call(kernel, in_specs=[ORDER, ORDER], out_specs=VMEM, out_shape...  2.84 us
    pallas_call x1, Pallas kernels, gather_rows(): pl.pallas_call(kernel, grid=(length // block,), in_specs=[ORDER, pl.Block...  2.48 us
  transfers between devices with their start and end apart: 14, of which 10 were waited for; matrix products, arithmetic and copies ran while one was open for 3% of the time, Pallas kernels for 37%

profile of v5, /device:TPU:0, one launch (start us, length us, event | category | flops | bytes accessed | tf_op | source)
XLA Modules:
  0.0 85.6 jit_solution(1313928404161682701)
XLA Ops:
  0.0 0.9 %copy-done.1 = bf16[4,192,128]{2,1,0:T(8,128)(2,1)S(1)} copy-done((bf16[4,192,128]{2,1,0:T(8,128)(2,1)S(1)}, bf16[4,192,128]{2,1,0:T(8,128)(2,1)}, u32[]{:S(2)}) %copy-start.1) | copy-done | bytes 196632
  1.0 3.0 %collective-permute-start = (bf16[1,192,128]{2,1,0:T(8,128)(2,1)S(1)}, bf16[1,192,128]{2,1,0:T(8,128)(2,1)S(1)}, u32[]{:S(2)}, u32[]{:S(2)}) collective-permute-start(bf16[1,192,128]{2,1,0:T(8,128)(2,1)S(1)} %part_of.2.rest_0_.refs_0_), channel_id=1, source_target_pairs={{0,1},{1,0},{2,3},{3,2},{4,5},{5,4},{6,7},{7,6},{8,9},{9,8},{10,11... | collective-permute-start | bytes 147464 | tf_op jit(solution)/shard_map/ppermute | solution.py:20
  4.0 0.2 part_of.3._.rest_2_.refs_2_
  4.2 0.1 collective-permute-start.2
  4.3 0.7 pad_add_fusion.facts_ref
  5.0 1.4 %fetch.2.sets_ref = bf16[2048,384]{1,0:T(8,128)(2,1)S(1)} custom-call(bf16[4,6144,384]{2,1,0:T(8,128)(2,1)} %sets_ref.17, bf16[3,192,128]{2,1,0:T(8,128)(2,1)S(1)} %part_of.3._.rest_2_.refs_2_), custom_call_target="tpu_custom_call" | custom-call | flops 1 | bytes 1 | tf_op jit(solution)/shard_map/fetch/pallas_call | solution.py:107
  6.4 0.0 collective-permute-done.rest_1_.refs_1_
  6.5 0.1 broadcast_in_dim.10.flags_ref
  6.5 0.6 apply_first.1._
  7.1 0.1 collective-permute-start.1
  7.2 1.4 %fetch.3.second_ref = bf16[2048,384]{1,0:T(8,128)(2,1)S(1)} custom-call(bf16[4,6144,384]{2,1,0:T(8,128)(2,1)} %sets_ref.17, bf16[1,2048,128]{2,1,0:T(8,128)(2,1)S(1)} %apply_first.1._), custom_call_target="tpu_custom_call" | custom-call | flops 1 | bytes 1 | tf_op jit(solution)/shard_map/fetch/pallas_call | solution.py:107
  8.6 0.0 copy-start.2
  8.6 0.0 copy-start.3
  8.6 0.9 %collective-permute-done.2.rest_3_.refs_3_ = bf16[3,192,128]{2,1,0:T(8,128)(2,1)S(1)} collective-permute-done((bf16[3,192,128]{2,1,0:T(8,128)(2,1)S(1)}, bf16[3,192,128]{2,1,0:T(8,128)(2,1)S(1)}, u32[]{:S(2)}, u32[]{:S(2)}) %collective-permute-start.2) | collective-permute-done | bytes 147488 | tf_op jit(solution)/shard_map/ppermute | solution.py:20
  9.5 3.0 %apply_rest.1 = bf16[3,2048,128]{2,1,0:T(8,128)(2,1)S(1)} custom-call(s32[7,128]{1,0:T(8,128)S(1)} %broadcast_in_dim.10.flags_ref, bf16[4,6144,384]{2,1,0:T(8,128)(2,1)} %sets_ref.17, bf16[2048,384]{1,0:T(8,128)(2,1)S(1)} %fetch.3.second_ref, bf16[1,192,128]{2,1,0:T(8,128)(2,1)S(1)} %part_of.2.rest_0_.refs_0_, ...), custom_call_target="tpu_custom_call" | custom-call | flops 1 | bytes 1 | tf_op jit(solution)/shard_map/apply_rest/pallas_call | solution.py:170
  12.5 1.3 %collective-permute-start.5 = (bf16[3,2048,128]{2,1,0:T(8,128)(2,1)S(1)}, bf16[3,2048,128]{2,1,0:T(8,128)(2,1)S(1)}, u32[]{:S(2)}, u32[]{:S(2)}) collective-permute-start(bf16[3,2048,128]{2,1,0:T(8,128)(2,1)S(1)} %apply_rest.1), channel_id=1, source_target_pairs={{0,2},{2,4},{4,6},{6,8},{8,10},{10,12},{12,14},{14,16},{16,18},{18... | collective-permute-start | bytes 4718600 | tf_op jit(solution)/shard_map/ppermute | solution.py:20
  13.8 0.2 select_reduce_fusion.kin_ref
  14.0 4.5 %collective-permute-done.1.first_ref._ = bf16[1,2048,128]{2,1,0:T(8,128)(2,1)S(1)} collective-permute-done((bf16[1,2048,128]{2,1,0:T(8,128)(2,1)S(1)}, bf16[1,2048,128]{2,1,0:T(8,128)(2,1)S(1)}, u32[]{:S(2)}, u32[]{:S(2)}) %collective-permute-start.1) | collective-permute-done | bytes 524320 | tf_op jit(solution)/shard_map/ppermute | solution.py:20
  18.5 0.0 collective-permute-start.3
  18.5 1.3 %collective-permute-done.3.kin_ref = f32[4,4]{1,0:T(4,128)S(1)} collective-permute-done((f32[4,4]{1,0:T(4,128)S(1)}, f32[4,4]{1,0:T(4,128)S(1)}, u32[]{:S(2)}, u32[]{:S(2)}) %collective-permute-start.3) | collective-permute-done | bytes 96 | tf_op jit(solution)/shard_map/ppermute | solution.py:20
  19.8 8.7 %combine.1 = (bf16[4096,128]{1,0:T(8,128)(2,1)S(1)}, bf16[4096,128]{1,0:T(8,128)(2,1)S(1)}, bf16[4096,128]{1,0:T(8,128)(2,1)}, bf16[3072,128]{1,0:T(8,128)(2,1)S(1)}, bf16[1024,128]{1,0:T(8,128)(2,1)S(1)}) custom-call(s32[7]{0:T(128)S(1)} %pad_add_fusion.facts_ref, f32[4,4]{1,0:T(4,128)S(1)} %collective-permute-done.3.kin_ref, ...), custom_call_target="tpu_custom_call" | custom-call | flops 1 | bytes 1 | tf_op jit(solution)/shard_map/combine/pallas_call | solution.py:231
  28.5 0.0 collective-permute-start.4
  28.5 0.0 collective-permute-start.7
  28.5 2.0 %collective-permute-start.9 = (bf16[4096,128]{1,0:T(8,128)(2,1)}, bf16[4096,128]{1,0:T(8,128)(2,1)S(1)}, u32[]{:S(2)}, u32[]{:S(2)}) collective-permute-start(bf16[4096,128]{1,0:T(8,128)(2,1)} %get-tuple-element.34), channel_id=1, source_target_pairs={{0,2},{2,4},{4,6},{6,8},{8,10},{10,12},{12,14},{14,16},{16,18},{18... | collective-permute-start | bytes 3145736 | tf_op jit(solution)/shard_map/ppermute | solution.py:20
  30.5 0.0 collective-permute-start.12
  30.5 4.8 %collective-permute-done.5.rest_ref = bf16[3,2048,128]{2,1,0:T(8,128)(2,1)S(1)} collective-permute-done((bf16[3,2048,128]{2,1,0:T(8,128)(2,1)S(1)}, bf16[3,2048,128]{2,1,0:T(8,128)(2,1)S(1)}, u32[]{:S(2)}, u32[]{:S(2)}) %collective-permute-start.5) | collective-permute-done | bytes 1572896 | tf_op jit(solution)/shard_map/ppermute | solution.py:20
  35.4 6.0 %collect.1.before_ref = f32[4,384,128]{2,1,0:T(8,128)S(1)} custom-call(f32[4,4]{1,0:T(4,128)S(1)} %select_reduce_fusion.kin_ref, bf16[4,6144,384]{2,1,0:T(8,128)(2,1)} %sets_ref.17, bf16[1,2048,128]{2,1,0:T(8,128)(2,1)S(1)} %collective-permute-done.1.first_ref._, bf16[3,2048,128]{2,1,0:T(8,128)(2,1)S(1)} %collective-permute-done.5.rest_ref), custom_call_target="tpu_custom_call" | custom-call | flops 1 | bytes 1 | tf_op jit(solution)/shard_map/collect/pallas_call | solution.py:267
  41.4 5.2 %collective-permute-done.4.arrived_ref = bf16[4096,128]{1,0:T(8,128)(2,1)S(1)} collective-permute-done((bf16[4096,128]{1,0:T(8,128)(2,1)S(1)}, bf16[4096,128]{1,0:T(8,128)(2,1)S(1)}, u32[]{:S(2)}, u32[]{:S(2)}) %collective-permute-start.4) | collective-permute-done | bytes 1048608 | tf_op jit(solution)/shard_map/ppermute | solution.py:20
  46.6 2.7 %finish_rows.3 = (f32[192,128]{1,0:T(8,128)S(1)}, bf16[1,192,128]{2,1,0:T(8,128)(2,1)S(1)}) custom-call(bf16[1,2048,128]{2,1,0:T(8,128)(2,1)S(1)} %collective-permute-done.1.first_ref._, s32[7]{0:T(128)S(1)} %pad_add_fusion.facts_ref, bf16[4,6144,384]{2,1,0:T(8,128)(2,1)} %sets_ref.17, bf16[4096,128]{1,0:T(8,128)(2,1)S(1)} %collective-permute-done.4.arrived_ref, ...), custom_call_target="tpu_custom_call" | custom-call | flops 1 | bytes 1 | tf_op jit(solution)/shard_map/finish_rows/pallas_call | solution.py:340
  49.3 2.2 %collective-permute-start.6 = (bf16[192,128]{1,0:T(8,128)(2,1)S(1)}, bf16[192,128]{1,0:T(8,128)(2,1)S(1)}, u32[]{:S(2)}, u32[]{:S(2)}) collective-permute-start(bf16[192,128]{1,0:T(8,128)(2,1)S(1)} %bitcast.13), channel_id=1, source_target_pairs={{0,1},{1,0},{2,3},{3,2},{4,5},{5,4},{6,7},{7,6},{8,9},{9,8},{10,11... | collective-permute-start | bytes 147464 | tf_op jit(solution)/shard_map/ppermute | solution.py:20
  51.6 1.2 %slice_bitcast_fusion.sets_ref = bf16[1024,384]{1,0:T(8,128)(2,1)S(1)} fusion(bf16[4,6144,384]{2,1,0:T(8,128)(2,1)} %sets_ref.17), kind=kLoop, calls=%fused_computation | loop fusion | bytes 1572864 | tf_op jit(solution)/shard_map/squeeze | solution.py:476
  52.8 0.1 collective-permute-start.11
  52.8 5.0 %collective-permute-done.7.arrived_ref = bf16[4096,128]{1,0:T(8,128)(2,1)S(1)} collective-permute-done((bf16[4096,128]{1,0:T(8,128)(2,1)S(1)}, bf16[4096,128]{1,0:T(8,128)(2,1)S(1)}, u32[]{:S(2)}, u32[]{:S(2)}) %collective-permute-start.7) | collective-permute-done | bytes 1048608 | tf_op jit(solution)/shard_map/ppermute | solution.py:20
  57.8 2.7 %finish_rows.4 = (f32[192,128]{1,0:T(8,128)S(1)}, bf16[1,192,128]{2,1,0:T(8,128)(2,1)S(1)}) custom-call(f32[192,128]{1,0:T(8,128)S(1)} %get-tuple-element.27._, s32[7]{0:T(128)S(1)} %pad_add_fusion.facts_ref, bf16[4,6144,384]{2,1,0:T(8,128)(2,1)} %sets_ref.17, bf16[4096,128]{1,0:T(8,128)(2,1)S(1)} %collective-permute-done.7.arrived_ref, ...), custom_call_target="tpu_custom_call" | custom-call | flops 1 | bytes 1 | tf_op jit(solution)/shard_map/finish_rows/pallas_call | solution.py:340
  60.6 2.2 %collective-permute-start.8 = (bf16[192,128]{1,0:T(8,128)(2,1)S(1)}, bf16[192,128]{1,0:T(8,128)(2,1)S(1)}, u32[]{:S(2)}, u32[]{:S(2)}) collective-permute-start(bf16[192,128]{1,0:T(8,128)(2,1)S(1)} %bitcast.14), channel_id=1, source_target_pairs={{0,1},{1,0},{2,3},{3,2},{4,5},{5,4},{6,7},{7,6},{8,9},{9,8},{10,11... | collective-permute-start | bytes 147464 | tf_op jit(solution)/shard_map/ppermute | solution.py:20
  62.8 6.3 %collective-permute-done.9.arrived_ref = bf16[4096,128]{1,0:T(8,128)(2,1)S(1)} collective-permute-done((bf16[4096,128]{1,0:T(8,128)(2,1)}, bf16[4096,128]{1,0:T(8,128)(2,1)S(1)}, u32[]{:S(2)}, u32[]{:S(2)}) %collective-permute-start.9) | collective-permute-done | bytes 1048608 | tf_op jit(solution)/shard_map/ppermute | solution.py:20
  69.1 2.7 %finish_rows.5 = (f32[192,128]{1,0:T(8,128)S(1)}, bf16[1,192,128]{2,1,0:T(8,128)(2,1)S(1)}) custom-call(f32[192,128]{1,0:T(8,128)S(1)} %get-tuple-element.31._, s32[7]{0:T(128)S(1)} %pad_add_fusion.facts_ref, bf16[4,6144,384]{2,1,0:T(8,128)(2,1)} %sets_ref.17, bf16[4096,128]{1,0:T(8,128)(2,1)S(1)} %collective-permute-done.9.arrived_ref, ...), custom_call_target="tpu_custom_call" | custom-call | flops 1 | bytes 1 | tf_op jit(solution)/shard_map/finish_rows/pallas_call | solution.py:340
  71.8 2.2 %collective-permute-start.10 = (bf16[192,128]{1,0:T(8,128)(2,1)S(1)}, bf16[192,128]{1,0:T(8,128)(2,1)S(1)}, u32[]{:S(2)}, u32[]{:S(2)}) collective-permute-start(bf16[192,128]{1,0:T(8,128)(2,1)S(1)} %bitcast.15), channel_id=1, source_target_pairs={{0,1},{1,0},{2,3},{3,2},{4,5},{5,4},{6,7},{7,6},{8,9},{9,8},{10,11... | collective-permute-start | bytes 147464 | tf_op jit(solution)/shard_map/ppermute | solution.py:20
  74.0 3.4 %collective-permute-done.12.arrived_ref = bf16[3072,128]{1,0:T(8,128)(2,1)S(1)} collective-permute-done((bf16[3072,128]{1,0:T(8,128)(2,1)S(1)}, bf16[3072,128]{1,0:T(8,128)(2,1)S(1)}, u32[]{:S(2)}, u32[]{:S(2)}) %collective-permute-start.12) | collective-permute-done | bytes 786464 | tf_op jit(solution)/shard_map/ppermute | solution.py:20
  77.5 2.5 %gather_rows.1.before_ref = f32[384,128]{1,0:T(8,128)S(1)} custom-call(f32[192,128]{1,0:T(8,128)S(1)} %get-tuple-element.35._, bf16[4,6144,384]{2,1,0:T(8,128)(2,1)} %sets_ref.17, bf16[3072,128]{1,0:T(8,128)(2,1)S(1)} %collective-permute-done.12.arrived_ref, f32[4,384,128]{2,1,0:T(8,128)S(1)} %collect.1.before_ref), custom_call_target="tpu_custom_call" | custom-call | flops 1 | bytes 1 | tf_op jit(solution)/shard_map/gather_rows/pallas_call | solution.py:304
  80.0 0.0 collective-permute-done.6
  80.0 0.0 collective-permute-done.8
  80.1 0.0 copy-start
  80.1 0.2 collective-permute-done.11.arrived_ref
  80.3 0.4 finish_last.1
  80.7 2.2 %collective-permute-start.13 = (bf16[192,128]{1,0:T(8,128)(2,1)S(1)}, bf16[192,128]{1,0:T(8,128)(2,1)S(1)}, u32[]{:S(2)}, u32[]{:S(2)}) collective-permute-start(bf16[192,128]{1,0:T(8,128)(2,1)S(1)} %bitcast.16), channel_id=1, source_target_pairs={{0,1},{1,0},{2,3},{3,2},{4,5},{5,4},{6,7},{7,6},{8,9},{9,8},{10,11... | collective-permute-start | bytes 147464 | tf_op jit(solution)/shard_map/ppermute | solution.py:20
  82.9 2.1 %collective-permute-done.13.rest_0_ = bf16[192,128]{1,0:T(8,128)(2,1)S(1)} collective-permute-done((bf16[192,128]{1,0:T(8,128)(2,1)S(1)}, bf16[192,128]{1,0:T(8,128)(2,1)S(1)}, u32[]{:S(2)}, u32[]{:S(2)}) %collective-permute-start.13) | collective-permute-done | bytes 49184 | tf_op jit(solution)/shard_map/ppermute | solution.py:20
  85.0 0.6 place_last.1
  (10 shorter events, 0.1 us)
Async XLA Ops:
  0.0 0.9 %copy-start.1 = (bf16[4,192,128]{2,1,0:T(8,128)(2,1)S(1)}, bf16[4,192,128]{2,1,0:T(8,128)(2,1)}, u32[]{:S(2)}) copy-start(bf16[4,192,128]{2,1,0:T(8,128)(2,1)} %vectors_ref.3) | copy-start | bytes 589828
  1.0 5.5 %collective-permute-start = (bf16[1,192,128]{2,1,0:T(8,128)(2,1)S(1)}, bf16[1,192,128]{2,1,0:T(8,128)(2,1)S(1)}, u32[]{:S(2)}, u32[]{:S(2)}) collective-permute-start(bf16[1,192,128]{2,1,0:T(8,128)(2,1)S(1)} %part_of.2.rest_0_.refs_0_), channel_id=1, source_target_pairs={{0,1},{1,0},{2,3},{3,2},{4,5},{5,4},{6,7},{7,6},{8,9},{9,8},{10,11... | collective-permute-start | bytes 147464 | tf_op jit(solution)/shard_map/ppermute | solution.py:20
  4.2 5.4 %collective-permute-start.2 = (bf16[3,192,128]{2,1,0:T(8,128)(2,1)S(1)}, bf16[3,192,128]{2,1,0:T(8,128)(2,1)S(1)}, u32[]{:S(2)}, u32[]{:S(2)}) collective-permute-start(bf16[3,192,128]{2,1,0:T(8,128)(2,1)S(1)} %part_of.3._.rest_2_.refs_2_), channel_id=1, source_target_pairs={{0,1},{1,0},{2,3},{3,2},{4,5},{5,4},{6,7},{7,6},{8,9},{9,8},{10,11... | collective-permute-start | bytes 442376 | tf_op jit(solution)/shard_map/ppermute | solution.py:20
  7.1 11.4 %collective-permute-start.1 = (bf16[1,2048,128]{2,1,0:T(8,128)(2,1)S(1)}, bf16[1,2048,128]{2,1,0:T(8,128)(2,1)S(1)}, u32[]{:S(2)}, u32[]{:S(2)}) collective-permute-start(bf16[1,2048,128]{2,1,0:T(8,128)(2,1)S(1)} %apply_first.1._), channel_id=1, source_target_pairs={{0,2},{2,4},{4,6},{6,8},{8,10},{10,12},{12,14},{14,16},{16,18},{18... | collective-permute-start | bytes 1572872 | tf_op jit(solution)/shard_map/ppermute | solution.py:20
  8.6 5.2 %copy-start.2 = (s32[4,4]{1,0:T(4,128)S(1)}, s32[4,4]{1,0:T(4,128)}, u32[]{:S(2)}) copy-start(s32[4,4]{1,0:T(4,128)} %param.9) | copy-start | bytes 196
  8.6 5.2 %copy-start.3 = (f32[64]{0:T(128)S(1)}, f32[64]{0:T(128)}, u32[]{:S(2)}) copy-start(f32[64]{0:T(128)} %param.8) | copy-start | bytes 772
  12.5 22.8 %collective-permute-start.5 = (bf16[3,2048,128]{2,1,0:T(8,128)(2,1)S(1)}, bf16[3,2048,128]{2,1,0:T(8,128)(2,1)S(1)}, u32[]{:S(2)}, u32[]{:S(2)}) collective-permute-start(bf16[3,2048,128]{2,1,0:T(8,128)(2,1)S(1)} %apply_rest.1), channel_id=1, source_target_pairs={{0,2},{2,4},{4,6},{6,8},{8,10},{10,12},{12,14},{14,16},{16,18},{18... | collective-permute-start | bytes 4718600 | tf_op jit(solution)/shard_map/ppermute | solution.py:20
  18.5 1.3 %collective-permute-start.3 = (f32[4,4]{1,0:T(4,128)S(1)}, f32[4,4]{1,0:T(4,128)S(1)}, u32[]{:S(2)}, u32[]{:S(2)}) collective-permute-start(f32[4,4]{1,0:T(4,128)S(1)} %select_reduce_fusion.kin_ref), channel_id=1, source_target_pairs={{0,30},{2,0},{4,2},{6,4},{8,6},{10,8},{12,10},{14,12},{16,14},{18,... | collective-permute-start | bytes 200 | tf_op jit(solution)/shard_map/ppermute | solution.py:20
  28.5 18.1 %collective-permute-start.4 = (bf16[4096,128]{1,0:T(8,128)(2,1)S(1)}, bf16[4096,128]{1,0:T(8,128)(2,1)S(1)}, u32[]{:S(2)}, u32[]{:S(2)}) collective-permute-start(bf16[4096,128]{1,0:T(8,128)(2,1)S(1)} %get-tuple-element.26), channel_id=1, source_target_pairs={{0,2},{2,4},{4,6},{6,8},{8,10},{10,12},{12,14},{14,16},{16,18},{18... | collective-permute-start | bytes 3145736 | tf_op jit(solution)/shard_map/ppermute | solution.py:20
  28.5 29.3 %collective-permute-start.7 = (bf16[4096,128]{1,0:T(8,128)(2,1)S(1)}, bf16[4096,128]{1,0:T(8,128)(2,1)S(1)}, u32[]{:S(2)}, u32[]{:S(2)}) collective-permute-start(bf16[4096,128]{1,0:T(8,128)(2,1)S(1)} %get-tuple-element.30), channel_id=1, source_target_pairs={{0,2},{2,4},{4,6},{6,8},{8,10},{10,12},{12,14},{14,16},{16,18},{18... | collective-permute-start | bytes 3145736 | tf_op jit(solution)/shard_map/ppermute | solution.py:20
  28.5 40.6 %collective-permute-start.9 = (bf16[4096,128]{1,0:T(8,128)(2,1)}, bf16[4096,128]{1,0:T(8,128)(2,1)S(1)}, u32[]{:S(2)}, u32[]{:S(2)}) collective-permute-start(bf16[4096,128]{1,0:T(8,128)(2,1)} %get-tuple-element.34), channel_id=1, source_target_pairs={{0,2},{2,4},{4,6},{6,8},{8,10},{10,12},{12,14},{14,16},{16,18},{18... | collective-permute-start | bytes 3145736 | tf_op jit(solution)/shard_map/ppermute | solution.py:20
  30.5 47.0 %collective-permute-start.12 = (bf16[3072,128]{1,0:T(8,128)(2,1)S(1)}, bf16[3072,128]{1,0:T(8,128)(2,1)S(1)}, u32[]{:S(2)}, u32[]{:S(2)}) collective-permute-start(bf16[3072,128]{1,0:T(8,128)(2,1)S(1)} %get-tuple-element.39), channel_id=1, source_target_pairs={{0,2},{2,4},{4,6},{6,8},{8,10},{10,12},{12,14},{14,16},{16,18},{18... | collective-permute-start | bytes 2359304 | tf_op jit(solution)/shard_map/ppermute | solution.py:20
  49.3 30.6 %collective-permute-start.6 = (bf16[192,128]{1,0:T(8,128)(2,1)S(1)}, bf16[192,128]{1,0:T(8,128)(2,1)S(1)}, u32[]{:S(2)}, u32[]{:S(2)}) collective-permute-start(bf16[192,128]{1,0:T(8,128)(2,1)S(1)} %bitcast.13), channel_id=1, source_target_pairs={{0,1},{1,0},{2,3},{3,2},{4,5},{5,4},{6,7},{7,6},{8,9},{9,8},{10,11... | collective-permute-start | bytes 147464 | tf_op jit(solution)/shard_map/ppermute | solution.py:20
  52.8 27.5 %collective-permute-start.11 = (bf16[1024,128]{1,0:T(8,128)(2,1)S(1)}, bf16[1024,128]{1,0:T(8,128)(2,1)S(1)}, u32[]{:S(2)}, u32[]{:S(2)}) collective-permute-start(bf16[1024,128]{1,0:T(8,128)(2,1)S(1)} %get-tuple-element.40), channel_id=1, source_target_pairs={{0,2},{2,4},{4,6},{6,8},{8,10},{10,12},{12,14},{14,16},{16,18},{18... | collective-permute-start | bytes 786440 | tf_op jit(solution)/shard_map/ppermute | solution.py:20
  60.6 19.4 %collective-permute-start.8 = (bf16[192,128]{1,0:T(8,128)(2,1)S(1)}, bf16[192,128]{1,0:T(8,128)(2,1)S(1)}, u32[]{:S(2)}, u32[]{:S(2)}) collective-permute-start(bf16[192,128]{1,0:T(8,128)(2,1)S(1)} %bitcast.14), channel_id=1, source_target_pairs={{0,1},{1,0},{2,3},{3,2},{4,5},{5,4},{6,7},{7,6},{8,9},{9,8},{10,11... | collective-permute-start | bytes 147464 | tf_op jit(solution)/shard_map/ppermute | solution.py:20
  71.8 8.2 %collective-permute-start.10 = (bf16[192,128]{1,0:T(8,128)(2,1)S(1)}, bf16[192,128]{1,0:T(8,128)(2,1)S(1)}, u32[]{:S(2)}, u32[]{:S(2)}) collective-permute-start(bf16[192,128]{1,0:T(8,128)(2,1)S(1)} %bitcast.15), channel_id=1, source_target_pairs={{0,1},{1,0},{2,3},{3,2},{4,5},{5,4},{6,7},{7,6},{8,9},{9,8},{10,11... | collective-permute-start | bytes 147464 | tf_op jit(solution)/shard_map/ppermute | solution.py:20
  80.1 4.9 %copy-start = (bf16[4,192,128]{2,1,0:T(8,128)(2,1)}, bf16[4,192,128]{2,1,0:T(8,128)(2,1)S(1)}, u32[]{:S(2)}) copy-start(bf16[4,192,128]{2,1,0:T(8,128)(2,1)S(1)} %pad_maximum_fusion._) | copy-start | bytes 589828
  80.7 4.3 %collective-permute-start.13 = (bf16[192,128]{1,0:T(8,128)(2,1)S(1)}, bf16[192,128]{1,0:T(8,128)(2,1)S(1)}, u32[]{:S(2)}, u32[]{:S(2)}) collective-permute-start(bf16[192,128]{1,0:T(8,128)(2,1)S(1)} %bitcast.16), channel_id=1, source_target_pairs={{0,1},{1,0},{2,3},{3,2},{4,5},{5,4},{6,7},{7,6},{8,9},{9,8},{10,11... | collective-permute-start | bytes 147464 | tf_op jit(solution)/shard_map/ppermute | solution.py:20
